TPU v7x, 128 devices: a whole 4x4x4 slice. The times are simulated.
128 devices in a mesh: row: 8 (over x, core), col: 16 (over y, z).
Axes of the slice: x: 4, y: 4, z: 4, core: 2. Of those that a mesh axis runs over, the one named last changes fastest.
Arguments:
- points: bfloat16 [131072, 256], P(('row', 'col')), may hold values from -6 to 6
- feature_scale: float32 [256], replicated, may hold values from 0.02 to 0.25
- tile_tasks: int32 [8, 16, 8], P('row', 'col'), may hold values from 0 to 127, as said below
- task_count: int32 [8, 16], P('row', 'col'), may hold values from 1 to 8, as said below
- seed_ids: int32 [64], replicated, may hold values from 0 to 131071, as said below
Outputs:
- embedding: float32 [131072, 64], P(('row', 'col'))
Inputs may be any that keep to these rules, and one draw needn't show every extreme that they name: `tile_tasks`: entries at slots below task_count of a device name devices other than itself (row-major over row, col); entries from task_count on are ignored. Over all devices, each device is named by at most 8 listed entries, and some device by exactly 8. Entries may repeat. `task_count`: some device lists exactly 8 tasks. `seed_ids`: the 64 seeds are distinct.
All inputs are finite; a program needn't handle non-finite values.
Results may differ from a plain program's by a relative error of at most 0.035.
Values may be sent and summed in bfloat16 or wider, within the bound.
No kernel may reach another device: no remote copies, remote signals or barrier semaphores. Data moves between devices by JAX's collectives and lax.ppermute only.
A program may use at most 128 MiB of HBM per device.

v0:
```python
import jax
import jax.numpy as jnp
from jax import lax
from jax.sharding import PartitionSpec as P

ITERS = 2


def squares(rows):
    widened = rows.astype(jnp.float32)
    return jnp.sum(widened * widened, axis=1)


def kernel_block(left_rows, right_rows, left_sq, right_sq):
    dot_terms = lax.dot_general(
        left_rows, right_rows, (((1,), (1,)), ((), ())), preferred_element_type=jnp.float32
    )
    return jnp.exp(-0.5 * (left_sq[:, None] + right_sq[None, :] - 2.0 * dot_terms))


def orthonormal(subspace):
    local_gram = lax.dot_general(
        subspace, subspace, (((0,), (0,)), ((), ())), precision=lax.Precision.HIGHEST
    )
    gram_total = lax.psum(local_gram, ("row", "col"))
    factor = jnp.linalg.cholesky(gram_total)
    return lax.linalg.triangular_solve(
        factor, subspace, left_side=False, lower=True, transpose_a=True
    )


def add_rows(accum, start_row, values):
    current = lax.dynamic_slice_in_dim(accum, start_row, values.shape[0], 0)
    return lax.dynamic_update_slice_in_dim(accum, current + values, start_row, 0)


def shards(points, feature_scale, tile_tasks, task_count, seed_ids):
    tile_rows = points.shape[0]
    row_devices = lax.axis_size("row")
    col_devices = lax.axis_size("col")
    all_devices = row_devices * col_devices
    self_index = lax.axis_index("row") * col_devices + lax.axis_index("col")
    weighted = (points.astype(jnp.float32) * feature_scale[None, :]).astype(jnp.bfloat16)
    own_sq = squares(weighted)
    row_band = lax.all_gather(weighted, "col", axis=0, tiled=True)
    col_band = lax.all_gather(weighted, "row", axis=0, tiled=True)
    row_band_sq = squares(row_band)
    col_band_sq = squares(col_band)
    listed = tile_tasks.reshape(-1)
    own_count = task_count.reshape(())
    list_slots = listed.shape[0]

    def tile_of(position):
        partner = listed[position]
        first_slot = partner % col_devices
        second_slot = partner // col_devices
        left_rows = lax.dynamic_slice_in_dim(row_band, first_slot * tile_rows, tile_rows, 0)
        left_sq = lax.dynamic_slice_in_dim(row_band_sq, first_slot * tile_rows, tile_rows, 0)
        right_rows = lax.dynamic_slice_in_dim(col_band, second_slot * tile_rows, tile_rows, 0)
        right_sq = lax.dynamic_slice_in_dim(col_band_sq, second_slot * tile_rows, tile_rows, 0)
        return (first_slot, second_slot, kernel_block(left_rows, right_rows, left_sq, right_sq))

    diagonal = kernel_block(weighted, weighted, own_sq, own_sq)
    tile_store = jnp.zeros((list_slots, tile_rows, tile_rows), jnp.bfloat16)

    def form(position, state):
        store_now, row_deg, col_deg = state
        first_slot, second_slot, tile_value = tile_of(position)
        row_deg = add_rows(row_deg, first_slot * tile_rows, jnp.sum(tile_value, axis=1))
        col_deg = add_rows(col_deg, second_slot * tile_rows, jnp.sum(tile_value, axis=0))
        store_now = lax.dynamic_update_index_in_dim(
            store_now, tile_value.astype(jnp.bfloat16), position, 0
        )
        return (store_now, row_deg, col_deg)

    tile_store, row_deg, col_deg = lax.fori_loop(
        0,
        own_count,
        form,
        (
            tile_store,
            jnp.zeros((col_devices * tile_rows,), jnp.float32),
            jnp.zeros((row_devices * tile_rows,), jnp.float32),
        ),
    )
    degree = (
        jnp.sum(diagonal, axis=1)
        + lax.psum_scatter(
            row_deg.astype(jnp.bfloat16), "col", scatter_dimension=0, tiled=True
        ).astype(jnp.float32)
        + lax.psum_scatter(
            col_deg.astype(jnp.bfloat16), "row", scatter_dimension=0, tiled=True
        ).astype(jnp.float32)
    )
    inv_root = lax.rsqrt(degree)
    diagonal16 = diagonal.astype(jnp.bfloat16)
    local_seed = seed_ids - self_index * tile_rows
    inside = (local_seed >= 0) & (local_seed < tile_rows)
    picked = jnp.take(weighted, jnp.clip(local_seed, 0, tile_rows - 1), axis=0).astype(
        jnp.float32
    ) * inside[:, None].astype(jnp.float32)
    seed_rows = lax.psum(picked, ("row", "col")).astype(jnp.bfloat16)
    subspace = orthonormal(kernel_block(weighted, seed_rows, own_sq, squares(seed_rows)))
    for iteration in range(ITERS):
        spread = (subspace * inv_root[:, None]).astype(jnp.bfloat16)
        row_vec = lax.all_gather(spread, "col", axis=0, tiled=True)
        col_vec = lax.all_gather(spread, "row", axis=0, tiled=True)
        vec_count = spread.shape[1]

        def apply_tile(position, state):
            row_acc, col_acc = state
            partner = listed[position]
            first_slot = partner % col_devices
            second_slot = partner // col_devices
            tile_value = tile_store[position]
            from_second = lax.dynamic_slice_in_dim(col_vec, second_slot * tile_rows, tile_rows, 0)
            from_first = lax.dynamic_slice_in_dim(row_vec, first_slot * tile_rows, tile_rows, 0)
            row_part = jnp.dot(tile_value, from_second, preferred_element_type=jnp.float32)
            col_part = lax.dot_general(
                tile_value, from_first, (((0,), (0,)), ((), ())), preferred_element_type=jnp.float32
            )
            return (
                add_rows(row_acc, first_slot * tile_rows, row_part),
                add_rows(col_acc, second_slot * tile_rows, col_part),
            )

        row_acc, col_acc = lax.fori_loop(
            0,
            own_count,
            apply_tile,
            (
                jnp.zeros((col_devices * tile_rows, vec_count), jnp.float32),
                jnp.zeros((row_devices * tile_rows, vec_count), jnp.float32),
            ),
        )
        applied = jnp.dot(diagonal16, spread, preferred_element_type=jnp.float32)
        applied = (
            applied
            + lax.psum_scatter(
                row_acc.astype(jnp.bfloat16), "col", scatter_dimension=0, tiled=True
            ).astype(jnp.float32)
            + lax.psum_scatter(
                col_acc.astype(jnp.bfloat16), "row", scatter_dimension=0, tiled=True
            ).astype(jnp.float32)
        )
        subspace = orthonormal(applied * inv_root[:, None])
    scaled = subspace * jnp.sqrt(jnp.float32(all_devices * tile_rows))
    return scaled * lax.rsqrt(jnp.mean(scaled * scaled, axis=1, keepdims=True) + 1e-06)


def solution(mesh):
    return jax.shard_map(
        shards,
        mesh=mesh,
        in_specs=(P(("row", "col"), None), P(), P("row", "col", None), P("row", "col"), P()),
        out_specs=P(("row", "col"), None),
        check_vma=False,
    )
```

profile of v0, /device:TPU:0, one launch (start us, length us, event | category | flops | bytes accessed | tf_op | source)
XLA Modules:
  0.0 1003.3 jit_solution(15847328262933258841)
XLA Ops:
  11.9 69.6 %psum.28 = bf16[64,256]{1,0:T(8,128)(2,1)S(1)} all-reduce(f32[64,256]{1,0:T(8,128)S(1)} %convert_multiply_fusion), channel_id=1, replica_groups=mesh['row'=8,'col'=16] {'row','col'}, use_global_device_ids=true, to_apply=%region_1.0 | all-reduce | flops 16384 | bytes 98304 | tf_op jit(solution)/shard_map/psum | solution.py:102
  83.3 63.4 %psum.29 = f32[64,64]{0,1:T(8,128)S(1)} all-reduce(f32[64,64]{0,1:T(8,128)S(1)} %fusion.75), channel_id=1, replica_groups=mesh['row'=8,'col'=16] {'row','col'}, use_global_device_ids=true, to_apply=%region_3.4 | all-reduce | flops 4096 | bytes 32768 | tf_op jit(solution)/shard_map/psum | solution.py:25
  146.8 5.8 cholesky.59
  154.0 4.9 custom-call.7
  168.6 5.2 multiply_reduce_fusion
  173.8 6.0 broadcast_in_dim.45
  179.9 8.9 while.44
  188.8 128.1 %all-reduce = bf16[16384]{0:T(1024)(128)(2,1)S(1)} all-reduce(bf16[16384]{0:T(1024)(128)(2,1)S(1)} %convert_element_type.89), channel_id=2, replica_groups=mesh['row'=8,'col'=16] {'col'}, use_global_device_ids=true, to_apply=%region_13.16.clone | all-reduce | flops 16384 | bytes 65536
  316.9 23.6 %all-reduce.1 = bf16[8192]{0:T(1024)(128)(2,1)S(1)} all-reduce(bf16[8192]{0:T(1024)(128)(2,1)S(1)} %convert_element_type.91), channel_id=3, replica_groups=mesh['row'=8,'col'=16] {'row'}, use_global_device_ids=true, to_apply=%region_14.17.clone | all-reduce | flops 8192 | bytes 32768
  342.2 16.2 %all-gather.11.cloned.1.call-done = bf16[8192,64]{0,1:T(8,128)(2,1)} async-done(((bf16[1024,64]{0,1:T(8,128)(2,1)}), bf16[8192,64]{0,1:T(8,128)(2,1)}) %all-gather.11.cloned.1.call-update) | async-done | bytes 1048592 | tf_op jit(solution)/shard_map/all_gather | solution.py:107
  358.4 47.3 %all-gather.13.cloned.1.call-done = bf16[16384,64]{0,1:T(8,128)(2,1)} async-done(((bf16[1024,64]{0,1:T(8,128)(2,1)}), bf16[16384,64]{0,1:T(8,128)(2,1)}) %all-gather.13.cloned.1.call-update) | async-done | bytes 2097168 | tf_op jit(solution)/shard_map/all_gather | solution.py:106
  408.1 9.7 while.45
  422.9 88.1 %reduce-scatter.7.cloned.1.call-done = bf16[1024,64]{0,1:T(8,128)(2,1)} async-done(((bf16[8192,64]{0,1:T(8,128)(2,1)}), bf16[1024,64]{0,1:T(8,128)(2,1)}) %reduce-scatter.7.cloned.1.call-update) | async-done | bytes 131088 | tf_op jit(solution)/shard_map/reduce_scatter | solution.py:142
  511.1 76.6 %reduce-scatter.5.cloned.1.call-done = bf16[1024,64]{0,1:T(8,128)(2,1)} async-done(((bf16[16384,64]{0,1:T(8,128)(2,1)}), bf16[1024,64]{0,1:T(8,128)(2,1)}) %reduce-scatter.5.cloned.1.call-update) | async-done | bytes 131088 | tf_op jit(solution)/shard_map/reduce_scatter | solution.py:139
  589.5 64.6 %psum.30 = f32[64,64]{0,1:T(8,128)S(1)} all-reduce(f32[64,64]{0,1:T(8,128)S(1)} %fusion.76), channel_id=1, replica_groups=mesh['row'=8,'col'=16] {'row','col'}, use_global_device_ids=true, to_apply=%region_19.22 | all-reduce | flops 4096 | bytes 32768 | tf_op jit(solution)/shard_map/psum | solution.py:25
  654.2 5.8 cholesky.70
  668.2 18.7 %all-gather.15.cloned.1.call-done = bf16[8192,64]{0,1:T(8,128)(2,1)} async-done(((bf16[1024,64]{0,1:T(8,128)(2,1)}), bf16[8192,64]{0,1:T(8,128)(2,1)}) %all-gather.15.cloned.1.call-update) | async-done | bytes 1048592 | tf_op jit(solution)/shard_map/all_gather | solution.py:107
  686.9 47.6 %all-gather.17.cloned.1.call-done = bf16[16384,64]{0,1:T(8,128)(2,1)} async-done(((bf16[1024,64]{0,1:T(8,128)(2,1)}), bf16[16384,64]{0,1:T(8,128)(2,1)}) %all-gather.17.cloned.1.call-update) | async-done | bytes 2097168 | tf_op jit(solution)/shard_map/all_gather | solution.py:106
  737.0 9.5 while.46
  751.6 88.2 %reduce-scatter.11.cloned.1.call-done = bf16[1024,64]{0,1:T(8,128)(2,1)} async-done(((bf16[8192,64]{0,1:T(8,128)(2,1)}), bf16[1024,64]{0,1:T(8,128)(2,1)}) %reduce-scatter.11.cloned.1.call-update) | async-done | bytes 131088 | tf_op jit(solution)/shard_map/reduce_scatter | solution.py:142
  839.8 76.9 %reduce-scatter.9.cloned.1.call-done = bf16[1024,64]{0,1:T(8,128)(2,1)} async-done(((bf16[16384,64]{0,1:T(8,128)(2,1)}), bf16[1024,64]{0,1:T(8,128)(2,1)}) %reduce-scatter.9.cloned.1.call-update) | async-done | bytes 131088 | tf_op jit(solution)/shard_map/reduce_scatter | solution.py:139
  918.5 64.6 %psum.31 = f32[64,64]{0,1:T(8,128)S(1)} all-reduce(f32[64,64]{0,1:T(8,128)S(1)} %fusion.77), channel_id=1, replica_groups=mesh['row'=8,'col'=16] {'row','col'}, use_global_device_ids=true, to_apply=%region_24.27 | all-reduce | flops 4096 | bytes 32768 | tf_op jit(solution)/shard_map/psum | solution.py:25
  983.2 5.8 cholesky.81
  990.4 4.9 custom-call.9
  (98 shorter events, 64.6 us)
Async XLA Ops:
  6.5 152.4 %copy-start.6 = (u32[128]{0:T(128)S(1)}, u32[128]{0:T(128)}, u32[]{:S(2)}) copy-start(u32[128]{0:T(128)} %constant.298) | copy-start | bytes 1540
  6.5 153.0 %copy-start.5 = (u32[128]{0:T(128)S(1)}, u32[128]{0:T(128)}, u32[]{:S(2)}) copy-start(u32[128]{0:T(128)} %constant.302) | copy-start | bytes 1540
  6.5 158.7 %all-gather.9.cloned.1.call-start = ((), (), s32[]{:S(2)}) async-start(), calls=%async_computation.5 | async-start | bytes 4718592 | tf_op jit(solution)/shard_map/all_gather | solution.py:46
  8.6 160.0 %all-gather.7.cloned.1.call-start = ((), (), s32[]{:S(2)}) async-start(), calls=%async_computation.4 | async-start | bytes 8912896 | tf_op jit(solution)/shard_map/all_gather | solution.py:45
  9.3 349.1 %all-gather.11.cloned.1.call-start = ((), (), s32[]{:S(2)}) async-start(), calls=%async_computation.6 | async-start | bytes 1179648 | tf_op jit(solution)/shard_map/all_gather | solution.py:107
  173.8 6.0 copy-start.4
  341.6 64.1 %all-gather.13.cloned.1.call-start = ((), (), s32[]{:S(2)}) async-start(), calls=%async_computation.7 | async-start | bytes 2228224 | tf_op jit(solution)/shard_map/all_gather | solution.py:106
  342.1 168.9 %reduce-scatter.7.cloned.1.call-start = ((), (), s32[]{:S(2)}) async-start(), calls=%async_computation.9 | async-start | bytes 1179648 | tf_op jit(solution)/shard_map/reduce_scatter | solution.py:142
  418.9 168.7 %reduce-scatter.5.cloned.1.call-start = ((), (), s32[]{:S(2)}) async-start(), calls=%async_computation.8 | async-start | bytes 2228224 | tf_op jit(solution)/shard_map/reduce_scatter | solution.py:139
  419.0 168.7 %copy-start = (bf16[1024,1024]{0,1:T(8,128)(2,1)S(1)}, bf16[1024,1024]{0,1:T(8,128)(2,1)}, u32[]{:S(2)}) copy-start(bf16[1024,1024]{0,1:T(8,128)(2,1)} %get-tuple-element.457) | copy-start | bytes 6291460
  419.0 168.6 %copy-start.3 = (bf16[1024,64]{0,1:T(8,128)(2,1)S(1)}, bf16[1024,64]{0,1:T(8,128)(2,1)}, u32[]{:S(2)}) copy-start(bf16[1024,64]{0,1:T(8,128)(2,1)} %fusion.58) | copy-start | bytes 393220
  422.9 264.0 %all-gather.15.cloned.1.call-start = ((), (), s32[]{:S(2)}) async-start(), calls=%async_computation.10 | async-start | bytes 1179648 | tf_op jit(solution)/shard_map/all_gather | solution.py:107
  667.4 67.2 %all-gather.17.cloned.1.call-start = ((), (), s32[]{:S(2)}) async-start(), calls=%async_computation.11 | async-start | bytes 2228224 | tf_op jit(solution)/shard_map/all_gather | solution.py:106
  668.2 171.6 %reduce-scatter.11.cloned.1.call-start = ((), (), s32[]{:S(2)}) async-start(), calls=%async_computation.13 | async-start | bytes 1179648 | tf_op jit(solution)/shard_map/reduce_scatter | solution.py:142
  747.6 169.0 %reduce-scatter.9.cloned.1.call-start = ((), (), s32[]{:S(2)}) async-start(), calls=%async_computation.12 | async-start | bytes 2228224 | tf_op jit(solution)/shard_map/reduce_scatter | solution.py:139
  747.7 169.0 %copy-start.1 = (bf16[1024,1024]{0,1:T(8,128)(2,1)S(1)}, bf16[1024,1024]{0,1:T(8,128)(2,1)}, u32[]{:S(2)}) copy-start(bf16[1024,1024]{0,1:T(8,128)(2,1)} %get-tuple-element.457) | copy-start | bytes 6291460
  747.7 169.0 %copy-start.2 = (bf16[1024,64]{0,1:T(8,128)(2,1)S(1)}, bf16[1024,64]{0,1:T(8,128)(2,1)}, u32[]{:S(2)}) copy-start(bf16[1024,64]{0,1:T(8,128)(2,1)} %fusion.59) | copy-start | bytes 393220
Sparse Core Ops, SparseCore 0:
  9.1 35.2 all-gather.8
  46.5 71.5 all-gather.6
  341.7 16.6 all-gather.10
  360.5 45.1 all-gather.12
  419.0 91.9 reduce-scatter.6
  514.2 73.4 reduce-scatter.4
  667.5 19.3 all-gather.14
  689.4 45.1 all-gather.16
  747.8 91.9 reduce-scatter.10
  843.2 73.3 reduce-scatter.8
where the time goes:
time: 1010 us; the launch traced here: 1000 us
  waiting for transfers between devices  462 us (46%)
  blocking collectives  414 us (41%)
  other arithmetic  58.8 us (6%)
  matrix products  26 us (3%)
  local copies, waits for them, and re-layouts  15.9 us (2%)
  between operations  15.1 us (1%)
  loops' own time  11.6 us (1%)
    psum x3, blocking collectives, orthonormal(): gram_total = lax.psum(local_gram, ('row', 'col'))  193 us
    reduce_scatter x2, waiting for transfers between devices, shards(): lax.psum_scatter(col_acc.astype(jnp.bfloat16), 'row', scatter_dimension=0...  176 us
    reduce_scatter x2, waiting for transfers between devices, shards(): lax.psum_scatter(row_acc.astype(jnp.bfloat16), 'col', scatter_dimension=0...  153 us
    unnamed x2, blocking collectives  152 us
    all_gather x2, waiting for transfers between devices, shards(): row_vec = lax.all_gather(spread, 'col', axis=0, tiled=True)  94.9 us
    psum x1, blocking collectives, shards(): seed_rows = lax.psum(picked, ('row', 'col')).astype(jnp.bfloat16)  69.6 us
    all_gather x2, waiting for transfers between devices, shards(): col_vec = lax.all_gather(spread, 'row', axis=0, tiled=True)  34.9 us
  transfers between devices with their start and end apart: 10, of which 8 were waited for; matrix products, arithmetic and copies ran while one was open for 3% of the time, Pallas kernels for 0%

commit v1 on v0

v1 whole, which is shorter than its diff:
```python
import functools
import math

import jax
import jax.numpy as jnp
from jax import lax
from jax.experimental import pallas as pl
from jax.experimental.pallas import tpu as pltpu
from jax.sharding import PartitionSpec as P

ITERS = 2
LOG2E = math.log2(math.e)
VMEM = 48 * 1024 * 1024
HIGH = lax.Precision.HIGHEST


def lane_sums(values):
    part = values[:, :128]
    for start in range(128, values.shape[1], 128):
        part = part + values[:, start : start + 128]
    return jnp.sum(part.T, axis=0, keepdims=True)


def half_squares(rows):
    wide = rows.astype(jnp.float32)
    return wide * wide * (0.5 * LOG2E)


def tile_chunk(left, right, right_half):
    dots = lax.dot_general(
        left, right, (((1,), (1,)), ((), ())), preferred_element_type=jnp.float32
    )
    left_half = jnp.sum(half_squares(left), axis=1, keepdims=True)
    return jnp.exp2(dots * LOG2E - left_half - right_half)


def form_kernel(chunk, first, second, live, left, right, tile, row_deg, col_deg):
    step = pl.program_id(0)

    @pl.when(step == 0)
    def clear():
        row_deg[...] = jnp.zeros_like(row_deg)
        col_deg[...] = jnp.zeros_like(col_deg)

    @pl.when(step < live[0])
    def work():
        rows = left.shape[1]
        right_rows = right[0]
        right_half = lane_sums(half_squares(right_rows))
        col_total = jnp.zeros((1, rows), jnp.float32)
        row_totals = []
        for start in range(0, rows, chunk):
            value = tile_chunk(left[0, start : start + chunk, :], right_rows, right_half)
            tile[0, start : start + chunk, :] = value.astype(jnp.bfloat16)
            col_total = col_total + jnp.sum(value, axis=0, keepdims=True)
            row_totals.append(lane_sums(value))
        row_slot = first[step]
        col_slot = second[step]
        row_deg[row_slot] = row_deg[row_slot] + jnp.concatenate(row_totals, axis=1)
        col_deg[col_slot] = col_deg[col_slot] + col_total


def form_tiles(first, second, live, row_band, col_band):
    col_devices, rows, depth = row_band.shape
    row_devices = col_band.shape[0]
    slots = first.shape[0]

    def last(step, live_ref):
        return jnp.minimum(step, live_ref[0] - 1)

    return pl.pallas_call(
        functools.partial(form_kernel, min(256, rows)),
        grid_spec=pltpu.PrefetchScalarGridSpec(
            num_scalar_prefetch=3,
            grid=(slots,),
            in_specs=[
                pl.BlockSpec((1, rows, depth), lambda s, f, g, n: (f[last(s, n)], 0, 0)),
                pl.BlockSpec((1, rows, depth), lambda s, f, g, n: (g[last(s, n)], 0, 0)),
            ],
            out_specs=[
                pl.BlockSpec((1, rows, rows), lambda s, f, g, n: (last(s, n), 0, 0)),
                pl.BlockSpec((col_devices, 1, rows), lambda s, f, g, n: (0, 0, 0)),
                pl.BlockSpec((row_devices, 1, rows), lambda s, f, g, n: (0, 0, 0)),
            ],
        ),
        out_shape=[
            jax.ShapeDtypeStruct((slots, rows, rows), jnp.bfloat16),
            jax.ShapeDtypeStruct((col_devices, 1, rows), jnp.float32),
            jax.ShapeDtypeStruct((row_devices, 1, rows), jnp.float32),
        ],
        compiler_params=pltpu.CompilerParams(vmem_limit_bytes=VMEM),
        name="form_tiles",
    )(first, second, live, row_band, col_band)


def diagonal_kernel(chunk, own, tile, degree):
    rows = own.shape[0]
    right_rows = own[...]
    right_half = lane_sums(half_squares(right_rows))
    total = jnp.zeros((1, rows), jnp.float32)
    for start in range(0, rows, chunk):
        value = tile_chunk(own[start : start + chunk, :], right_rows, right_half)
        tile[start : start + chunk, :] = value.astype(jnp.bfloat16)
        total = total + jnp.sum(value, axis=0, keepdims=True)
    degree[...] = total


def form_diagonal(own):
    rows = own.shape[0]
    return pl.pallas_call(
        functools.partial(diagonal_kernel, min(256, rows)),
        out_shape=[
            jax.ShapeDtypeStruct((rows, rows), jnp.bfloat16),
            jax.ShapeDtypeStruct((1, rows), jnp.float32),
        ],
        compiler_params=pltpu.CompilerParams(vmem_limit_bytes=VMEM),
        name="form_diagonal",
    )(own)


def apply_kernel(contract, source, target, live, tile, vectors, out, total):
    step = pl.program_id(0)

    @pl.when(step == 0)
    def clear():
        total[...] = jnp.zeros_like(total)

    @pl.when(step < live[0])
    def work():
        slot = target[step]
        total[slot] = total[slot] + lax.dot_general(
            vectors[0],
            tile[0],
            (((1,), (contract,)), ((), ())),
            preferred_element_type=jnp.float32,
        )

    @pl.when(step == pl.num_programs(0) - 1)
    def store():
        out[...] = total[...].astype(jnp.bfloat16)


def apply_tiles(contract, source, target, live, tiles, vectors, targets):
    slots, rows, unused = tiles.shape
    vecs = vectors.shape[1]

    def last(step, live_ref):
        return jnp.minimum(step, live_ref[0] - 1)

    return pl.pallas_call(
        functools.partial(apply_kernel, contract),
        grid_spec=pltpu.PrefetchScalarGridSpec(
            num_scalar_prefetch=3,
            grid=(slots,),
            in_specs=[
                pl.BlockSpec((1, rows, rows), lambda s, f, g, n: (last(s, n), 0, 0)),
                pl.BlockSpec((1, vecs, rows), lambda s, f, g, n: (f[last(s, n)], 0, 0)),
            ],
            out_specs=pl.BlockSpec((targets, vecs, rows), lambda s, f, g, n: (0, 0, 0)),
            scratch_shapes=[pltpu.VMEM((targets, vecs, rows), jnp.float32)],
        ),
        out_shape=jax.ShapeDtypeStruct((targets, vecs, rows), jnp.bfloat16),
        compiler_params=pltpu.CompilerParams(vmem_limit_bytes=VMEM),
        name="apply_tiles",
    )(source, target, live, tiles, vectors)


def spread_to(array, axis):
    devices = lax.axis_size(axis)
    copies = jnp.broadcast_to(array[None], (devices,) + array.shape)
    return lax.all_to_all(copies, axis, 0, 0, tiled=True)


def sum_over_mesh(array):
    return jnp.sum(spread_to(jnp.sum(spread_to(array, "row"), axis=0), "col"), axis=0)


def orthonormal(subspace):
    local_gram = lax.dot_general(subspace, subspace, (((1,), (1,)), ((), ())), precision=HIGH)
    factor = jnp.linalg.cholesky(sum_over_mesh(local_gram))
    return lax.linalg.triangular_solve(factor, subspace, left_side=True, lower=True)


def gather_row(own):
    devices = lax.axis_size("row")
    half = own.shape[0] // 2

    def shift(array, by):
        return lax.ppermute(array, "row", [(i, (i + by) % devices) for i in range(devices)])

    before = shift(own, 2)
    after = shift(own, -2)
    across = jnp.concatenate([shift(before[:half], 2), shift(after[half:], -2)], axis=0)
    mine = jnp.stack([own, before, after, across])
    other = lax.ppermute(mine, "row", [(i, i ^ 1) for i in range(devices)])
    return jnp.concatenate([mine, other], axis=0)


def place_in_row(index):
    here = lax.axis_index("row")
    apart = (index // 2 - here // 2) % 4
    order = jnp.where(apart == 0, 0, jnp.where(apart == 3, 1, jnp.where(apart == 1, 2, 3)))
    return order + 4 * ((index - here) % 2)


def shards(points, feature_scale, tile_tasks, task_count, seed_ids):
    rows = points.shape[0]
    row_devices = lax.axis_size("row")
    col_devices = lax.axis_size("col")
    all_devices = row_devices * col_devices
    self_index = lax.axis_index("row") * col_devices + lax.axis_index("col")
    weighted = (points.astype(jnp.float32) * feature_scale[None, :]).astype(jnp.bfloat16)
    row_band = lax.all_gather(weighted, "col", axis=0)
    col_band = gather_row(weighted)
    listed = tile_tasks.reshape(-1)
    live = task_count.reshape(1)
    used = jnp.where(jnp.arange(listed.shape[0]) < live, listed, 0)
    first = used % col_devices
    second = used // col_devices

    local_seed = seed_ids - self_index * rows
    inside = (local_seed >= 0) & (local_seed < rows)
    picked = jnp.where(
        inside[:, None], jnp.take(weighted, jnp.clip(local_seed, 0, rows - 1), axis=0), 0
    ).astype(jnp.bfloat16)
    seed_rows = sum_over_mesh(picked)

    diagonal, own_degree = form_diagonal(weighted)
    own_half = jnp.sum(half_squares(weighted), axis=1)
    seed_half = jnp.sum(half_squares(seed_rows), axis=1)
    seed_dots = lax.dot_general(
        seed_rows, weighted, (((1,), (1,)), ((), ())), preferred_element_type=jnp.float32
    )
    start = jnp.exp2(seed_dots * LOG2E - seed_half[:, None] - own_half[None, :])
    subspace = orthonormal(start)

    tiles, row_deg, col_deg = form_tiles(
        first, place_in_row(second), live, row_band, col_band
    )
    row_places = place_in_row(jnp.arange(row_devices))
    col_deg = jnp.take(col_deg, row_places, axis=0)
    degree = (
        own_degree
        + jnp.sum(lax.all_to_all(row_deg, "col", 0, 0, tiled=True), axis=0)
        + jnp.sum(lax.all_to_all(col_deg, "row", 0, 0, tiled=True), axis=0)
    )
    inv_root = lax.rsqrt(degree)
    for iteration in range(ITERS):
        spread = (subspace * inv_root).astype(jnp.bfloat16)
        col_vec = lax.all_gather(spread, "row", axis=0)
        row_vec = spread_to(spread, "col")
        own_part = lax.dot_general(
            spread, diagonal, (((1,), (0,)), ((), ())), preferred_element_type=jnp.float32
        )
        to_second = apply_tiles(0, first, second, live, tiles, row_vec, row_devices)
        second_part = lax.psum_scatter(to_second, "row", scatter_dimension=0, tiled=False)
        to_first = apply_tiles(1, second, first, live, tiles, col_vec, col_devices)
        first_parts = lax.all_to_all(to_first, "col", 0, 0, tiled=True)
        applied = (
            own_part
            + jnp.sum(first_parts.astype(jnp.float32), axis=0)
            + second_part.astype(jnp.float32)
        )
        subspace = orthonormal(applied * inv_root)
    scaled = subspace * jnp.sqrt(jnp.float32(all_devices * rows))
    result = scaled * lax.rsqrt(jnp.mean(scaled * scaled, axis=0, keepdims=True) + 1e-06)
    return result.T


def solution(mesh):
    return jax.shard_map(
        shards,
        mesh=mesh,
        in_specs=(P(("row", "col"), None), P(), P("row", "col", None), P("row", "col"), P()),
        out_specs=P(("row", "col"), None),
        check_vma=False,
    )
```

time: 1010 us -> 427 us (0.42)
  blocking collectives: 414 us -> 47.3 us
  waiting for transfers between devices: 462 us -> 169 us
  starting transfers between devices: 0.37 us -> 82.6 us
  Pallas kernels: 0 us -> 25.6 us
  matrix products: 26 us -> 5.51 us
  loops' own time: 11.6 us -> 0 us
  local copies, waits for them, and re-layouts: 15.9 us -> 26.9 us
    reduce_scatter x4 -> x2, waiting for transfers between devices: 330 us -> 26.7 us  [shards(): lax.psum_scatter(to_second, 'row', scatter_dimension=0, tiled=False)]
    psum x4 -> x0, blocking collectives: 262 us -> none  [the longest x3 193 us: orthonormal(): gram_total = lax.psum(local_gram, ('row', 'col'))]
    unnamed x2 -> x0, blocking collectives: 152 us -> none
    all_to_all x0 -> x10, waiting for transfers between devices: none -> 82.9 us  [the longest x2 46.2 us: shards(): first_parts = lax.all_to_all(to_first, 'col', 0, 0, tiled=True)]
    all_gather x6 -> x3, waiting for transfers between devices: 130 us -> 49.5 us  [the longest x2 49.5 us: shards(): col_vec = lax.all_gather(spread, 'row', axis=0)]
    all_to_all x0 -> x10, starting transfers between devices: none -> 75.5 us  [the longest x6 30.4 us: spread_to(): return lax.all_to_all(copies, axis, 0, 0, tiled=True)]
    all_to_all x0 -> x4, blocking collectives: none -> 47.3 us  [spread_to(): return lax.all_to_all(copies, axis, 0, 0, tiled=True)]
    pallas_call x0 -> x6, Pallas kernels: none -> 25.6 us  [the longest x4 18.2 us: apply_tiles(): pl.pallas_call(functools.partial(apply_kernel, contract), grid_spec=pltpu...]
  transfers between devices with their start and end apart: 10 -> 20, of which waited for: 8 -> 13; matrix products, arithmetic and copies ran while one was open for 3% -> 8% of each run, Pallas kernels for 0% -> 5%
where the time goes in v1:
time: 427 us; the launch traced here: 425 us
  waiting for transfers between devices  169 us (40%)
  starting transfers between devices  82.6 us (19%)
  other arithmetic  53.9 us (13%)
  blocking collectives  47.3 us (11%)
  local copies, waits for them, and re-layouts  26.9 us (6%)
  Pallas kernels  25.6 us (6%)
  between operations  14.4 us (3%)
  matrix products  5.51 us (1%)
    all_gather x2, waiting for transfers between devices, shards(): col_vec = lax.all_gather(spread, 'row', axis=0)  49.5 us
    all_to_all x4, blocking collectives, spread_to(): return lax.all_to_all(copies, axis, 0, 0, tiled=True)  47.3 us
    all_to_all x2, waiting for transfers between devices, shards(): first_parts = lax.all_to_all(to_first, 'col', 0, 0, tiled=True)  46.2 us
    all_to_all x6, starting transfers between devices, spread_to(): return lax.all_to_all(copies, axis, 0, 0, tiled=True)  30.4 us
    all_to_all x6, waiting for transfers between devices, spread_to(): return lax.all_to_all(copies, axis, 0, 0, tiled=True)  29.8 us
    all_to_all x2, starting transfers between devices, shards(): first_parts = lax.all_to_all(to_first, 'col', 0, 0, tiled=True)  28.7 us
    reduce_scatter x2, waiting for transfers between devices, shards(): lax.psum_scatter(to_second, 'row', scatter_dimension=0, tiled=False)  26.7 us
    another operation x9, other arithmetic, orthonormal(): factor = jnp.linalg.cholesky(sum_over_mesh(local_gram))  19.6 us
  transfers between devices with their start and end apart: 20, of which 13 were waited for; matrix products, arithmetic and copies ran while one was open for 8% of the time, Pallas kernels for 5%

profile of v1, /device:TPU:0, one launch (start us, length us, event | category | flops | bytes accessed | tf_op | source)
XLA Modules:
  0.0 425.5 jit_solution(4742589848638009350)
XLA Ops:
  14.0 9.0 %collective-permute-done.1 = bf16[1024,256]{1,0:T(8,128)(2,1)S(1)} collective-permute-done((bf16[1024,256]{1,0:T(8,128)(2,1)}, bf16[1024,256]{1,0:T(8,128)(2,1)S(1)}, u32[]{:S(2)}, u32[]{:S(2)}) %collective-permute-start.1) | collective-permute-done | bytes 524320 | tf_op jit(solution)/shard_map/ppermute | solution.py:189
  32.9 6.8 %all-to-all-done = bf16[8,64,256]{2,1,0:T(8,128)(2,1)S(1)} async-done(((bf16[8,64,256]{2,1,0:T(8,128)(2,1)}), bf16[8,64,256]{2,1,0:T(8,128)(2,1)S(1)}, u32[]{:S(2)}, u32[]{:S(2)}) %all-to-all-start) | async-done | bytes 262176 | tf_op jit(solution)/shard_map/all_to_all | solution.py:171
  40.7 8.0 %all-to-all-start.1 = ((bf16[16,64,256]{2,1,0:T(8,128)(2,1)}), bf16[16,64,256]{2,1,0:T(8,128)(2,1)S(1)}, u32[]{:S(2)}, u32[]{:S(2)}) async-start(bf16[16,64,256]{2,1,0:T(8,128)(2,1)} %broadcast_in_dim.123), calls=%async_computation.1 | async-start | bytes 1048576 | tf_op jit(solution)/shard_map/all_to_all | solution.py:171
  53.9 10.5 %all-to-all-done.1 = bf16[16,64,256]{2,1,0:T(8,128)(2,1)S(1)} async-done(((bf16[16,64,256]{2,1,0:T(8,128)(2,1)}), bf16[16,64,256]{2,1,0:T(8,128)(2,1)S(1)}, u32[]{:S(2)}, u32[]{:S(2)}) %all-to-all-start.1) | async-done | bytes 524320 | tf_op jit(solution)/shard_map/all_to_all | solution.py:171
  70.4 5.2 %all-to-all-done.2 = f32[8,1,4096]{2,1,0:T(1,128)S(1)} async-done(((f32[8,1,4096]{2,1,0:T(1,128)}), f32[8,1,4096]{2,1,0:T(1,128)S(1)}, u32[]{:S(2)}, u32[]{:S(2)}) %all-to-all-start.2) | async-done | bytes 131104 | tf_op jit(solution)/shard_map/all_to_all | solution.py:171
  78.4 5.7 %all-to-all-start.3 = ((f32[16,1,4096]{2,1,0:T(1,128)}), f32[16,1,4096]{2,1,0:T(1,128)S(1)}, u32[]{:S(2)}, u32[]{:S(2)}) async-start(f32[16,1,4096]{2,1,0:T(1,128)} %reshape.283), calls=%async_computation.3 | async-start | bytes 524288 | tf_op jit(solution)/shard_map/all_to_all | solution.py:171
  85.7 7.3 %all-to-all-done.3 = f32[16,1,4096]{2,1,0:T(1,128)S(1)} async-done(((f32[16,1,4096]{2,1,0:T(1,128)}), f32[16,1,4096]{2,1,0:T(1,128)S(1)}, u32[]{:S(2)}, u32[]{:S(2)}) %all-to-all-start.3) | async-done | bytes 262176 | tf_op jit(solution)/shard_map/all_to_all | solution.py:171
  94.7 5.8 %cholesky.59 = f32[64,64]{1,0:T(8,128)S(1)} custom-call(f32[64,64]{1,0:T(8,128)S(1)} %fusion.19), custom_call_target="Cholesky" | custom-call | tf_op jit(solution)/shard_map/jit(cholesky)/cholesky | solution.py:180
  105.8 6.2 %form_tiles.1 = (bf16[8,1024,1024]{2,1,0:T(8,128)(2,1)}, f32[16,1,1024]{2,1,0:T(1,128)}, f32[8,1,1024]{2,1,0:T(1,128)S(1)}) custom-call(s32[8]{0:T(128)S(1)} %and_select_fusion.10.first.target.source, s32[8]{0:T(128)S(1)} %get-tuple-element.21.second, s32[1]{0:T(128)} %bitcast.86.live, bf16[16,1024,256]{2,1,0:T(8,128)(2,1)} %bitcast.94, ...), custom_call_target="tpu_custom_call" | custom-call | tf_op jit(solution)/shard_map/form_tiles/pallas_call | solution.py:71
  122.8 12.3 %all-to-all-start.4 = ((f32[16,1,1024]{2,1,0:T(1,128)}), f32[16,1,1024]{2,1,0:T(1,128)S(1)}, u32[]{:S(2)}, u32[]{:S(2)}) async-start(f32[16,1,1024]{2,1,0:T(1,128)} %get-tuple-element.13), calls=%async_computation.4 | async-start | bytes 131072 | tf_op jit(solution)/shard_map/all_to_all | solution.py:244
  150.8 24.8 %all-gather.9.cloned.1.call-done = bf16[512,1024]{1,0:T(8,128)(2,1)} async-done(((bf16[64,1024]{1,0:T(8,128)(2,1)}), bf16[512,1024]{1,0:T(8,128)(2,1)}) %all-gather.9.cloned.1.call-update) | async-done | bytes 1048592 | tf_op jit(solution)/shard_map/all_gather | solution.py:250
  182.6 14.3 %all-to-all-start.6 = ((bf16[16,64,1024]{2,1,0:T(8,128)(2,1)}), bf16[16,64,1024]{2,1,0:T(8,128)(2,1)}, u32[]{:S(2)}, u32[]{:S(2)}) async-start(bf16[16,64,1024]{2,1,0:T(8,128)(2,1)} %copy-done.2), calls=%async_computation.6 | async-start | bytes 4194304 | tf_op jit(solution)/shard_map/all_to_all | solution.py:258
  201.7 23.2 %all-to-all-done.6 = bf16[16,64,1024]{2,1,0:T(8,128)(2,1)} async-done(((bf16[16,64,1024]{2,1,0:T(8,128)(2,1)}), bf16[16,64,1024]{2,1,0:T(8,128)(2,1)}, u32[]{:S(2)}, u32[]{:S(2)}) %all-to-all-start.6) | async-done | bytes 2097184 | tf_op jit(solution)/shard_map/all_to_all | solution.py:258
  227.0 13.3 %reduce-scatter.3.cloned.1.call-done = bf16[1,64,1024]{2,1,0:T(8,128)(2,1)} async-done(((bf16[8,64,1024]{2,1,0:T(8,128)(2,1)}), bf16[1,64,1024]{2,1,0:T(8,128)(2,1)}) %reduce-scatter.3.cloned.1.call-update) | async-done | bytes 131088 | tf_op jit(solution)/shard_map/reduce_scatter | solution.py:256
  242.2 8.5 %all_to_all.70 = f32[8,1,4096]{2,1,0:T(1,128)S(1)} all-to-all(f32[8,1,4096]{2,1,0:T(1,128)S(1)} %reshape.285), channel_id=1, replica_groups=mesh['row'=8,'col'=16] {'row'}, dimensions={0} | all-to-all | bytes 262144 | tf_op jit(solution)/shard_map/all_to_all | solution.py:171
  252.2 15.1 %all_to_all.71 = f32[16,1,4096]{2,1,0:T(1,128)S(1)} all-to-all(f32[16,1,4096]{2,1,0:T(1,128)S(1)} %reshape.287), channel_id=1, replica_groups=mesh['row'=8,'col'=16] {'col'}, dimensions={0} | all-to-all | bytes 524288 | tf_op jit(solution)/shard_map/all_to_all | solution.py:171
  269.0 5.8 %cholesky.70 = f32[64,64]{1,0:T(8,128)S(1)} custom-call(f32[64,64]{1,0:T(8,128)S(1)} %fusion.17), custom_call_target="Cholesky" | custom-call | tf_op jit(solution)/shard_map/jit(cholesky)/cholesky | solution.py:180
  287.4 24.6 %all-gather.11.cloned.1.call-done = bf16[512,1024]{1,0:T(8,128)(2,1)} async-done(((bf16[64,1024]{1,0:T(8,128)(2,1)}), bf16[512,1024]{1,0:T(8,128)(2,1)}) %all-gather.11.cloned.1.call-update) | async-done | bytes 1048592 | tf_op jit(solution)/shard_map/all_gather | solution.py:250
  319.1 14.3 %all-to-all-start.10 = ((bf16[16,64,1024]{2,1,0:T(8,128)(2,1)}), bf16[16,64,1024]{2,1,0:T(8,128)(2,1)}, u32[]{:S(2)}, u32[]{:S(2)}) async-start(bf16[16,64,1024]{2,1,0:T(8,128)(2,1)} %copy-done.1), calls=%async_computation.11 | async-start | bytes 4194304 | tf_op jit(solution)/shard_map/all_to_all | solution.py:258
  338.4 23.0 %all-to-all-done.10 = bf16[16,64,1024]{2,1,0:T(8,128)(2,1)} async-done(((bf16[16,64,1024]{2,1,0:T(8,128)(2,1)}), bf16[16,64,1024]{2,1,0:T(8,128)(2,1)}, u32[]{:S(2)}, u32[]{:S(2)}) %all-to-all-start.10) | async-done | bytes 2097184 | tf_op jit(solution)/shard_map/all_to_all | solution.py:258
  363.4 13.5 %reduce-scatter.5.cloned.1.call-done = bf16[1,64,1024]{2,1,0:T(8,128)(2,1)} async-done(((bf16[8,64,1024]{2,1,0:T(8,128)(2,1)}), bf16[1,64,1024]{2,1,0:T(8,128)(2,1)}) %reduce-scatter.5.cloned.1.call-update) | async-done | bytes 131088 | tf_op jit(solution)/shard_map/reduce_scatter | solution.py:256
  378.9 8.5 %all_to_all.72 = f32[8,1,4096]{2,1,0:T(1,128)S(1)} all-to-all(f32[8,1,4096]{2,1,0:T(1,128)S(1)} %reshape.289), channel_id=1, replica_groups=mesh['row'=8,'col'=16] {'row'}, dimensions={0} | all-to-all | bytes 262144 | tf_op jit(solution)/shard_map/all_to_all | solution.py:171
  388.9 15.1 %all_to_all.73 = f32[16,1,4096]{2,1,0:T(1,128)S(1)} all-to-all(f32[16,1,4096]{2,1,0:T(1,128)S(1)} %reshape.291), channel_id=1, replica_groups=mesh['row'=8,'col'=16] {'col'}, dimensions={0} | all-to-all | bytes 524288 | tf_op jit(solution)/shard_map/all_to_all | solution.py:171
  405.7 5.8 %cholesky.81 = f32[64,64]{1,0:T(8,128)S(1)} custom-call(f32[64,64]{1,0:T(8,128)S(1)} %fusion.15), custom_call_target="Cholesky" | custom-call | tf_op jit(solution)/shard_map/jit(cholesky)/cholesky | solution.py:180
  (156 shorter events, 124.2 us)
Async XLA Ops:
  6.5 97.0 %all-gather.7.cloned.1.call-start = ((), (), s32[]{:S(2)}) async-start(), calls=%async_computation.18 | async-start | bytes 8912896 | tf_op jit(solution)/shard_map/all_gather | solution.py:213
  8.7 14.4 %collective-permute-start.1 = (bf16[1024,256]{1,0:T(8,128)(2,1)}, bf16[1024,256]{1,0:T(8,128)(2,1)S(1)}, u32[]{:S(2)}, u32[]{:S(2)}) collective-permute-start(bf16[1024,256]{1,0:T(8,128)(2,1)} %get-tuple-element.18.own), channel_id=1, source_target_pairs={{0,96},{16,112},{32,0},{48,16},{64,32},{80,48},{96,64},{112,80},{1... | collective-permute-start | bytes 1572872 | tf_op jit(solution)/shard_map/ppermute | solution.py:189
  11.6 15.2 %collective-permute-start = (bf16[1024,256]{1,0:T(8,128)(2,1)}, bf16[1024,256]{1,0:T(8,128)(2,1)S(1)}, u32[]{:S(2)}, u32[]{:S(2)}) collective-permute-start(bf16[1024,256]{1,0:T(8,128)(2,1)} %get-tuple-element.18.own), channel_id=1, source_target_pairs={{0,32},{16,48},{32,64},{48,80},{64,96},{80,112},{96,0},{112,16},{1... | collective-permute-start | bytes 1572872 | tf_op jit(solution)/shard_map/ppermute | solution.py:189
  23.1 25.6 %collective-permute-start.3 = (bf16[512,256]{1,0:T(8,128)(2,1)S(1)}, bf16[512,256]{1,0:T(8,128)(2,1)S(1)}, u32[]{:S(2)}, u32[]{:S(2)}) collective-permute-start(bf16[512,256]{1,0:T(8,128)(2,1)S(1)} %slice.19), channel_id=1, source_target_pairs={{0,96},{16,112},{32,0},{48,16},{64,32},{80,48},{96,64},{112,80},{1... | collective-permute-start | bytes 786440 | tf_op jit(solution)/shard_map/ppermute | solution.py:189
  26.8 22.0 %collective-permute-start.2 = (bf16[512,256]{1,0:T(8,128)(2,1)S(1)}, bf16[512,256]{1,0:T(8,128)(2,1)S(1)}, u32[]{:S(2)}, u32[]{:S(2)}) collective-permute-start(bf16[512,256]{1,0:T(8,128)(2,1)S(1)} %slice.18), channel_id=1, source_target_pairs={{0,32},{16,48},{32,64},{48,80},{64,96},{80,112},{96,0},{112,16},{1... | collective-permute-start | bytes 786440 | tf_op jit(solution)/shard_map/ppermute | solution.py:189
  27.7 12.0 %all-to-all-start = ((bf16[8,64,256]{2,1,0:T(8,128)(2,1)}), bf16[8,64,256]{2,1,0:T(8,128)(2,1)S(1)}, u32[]{:S(2)}, u32[]{:S(2)}) async-start(bf16[8,64,256]{2,1,0:T(8,128)(2,1)} %broadcast_in_dim.122), calls=%async_computation | async-start | bytes 524288 | tf_op jit(solution)/shard_map/all_to_all | solution.py:171
  40.7 23.7 %all-to-all-start.1 = ((bf16[16,64,256]{2,1,0:T(8,128)(2,1)}), bf16[16,64,256]{2,1,0:T(8,128)(2,1)S(1)}, u32[]{:S(2)}, u32[]{:S(2)}) async-start(bf16[16,64,256]{2,1,0:T(8,128)(2,1)} %broadcast_in_dim.123), calls=%async_computation.1 | async-start | bytes 1048576 | tf_op jit(solution)/shard_map/all_to_all | solution.py:171
  50.4 50.1 %collective-permute-start.4 = (bf16[4,1024,256]{2,1,0:T(8,128)(2,1)}, bf16[4,1024,256]{2,1,0:T(8,128)(2,1)}, u32[]{:S(2)}, u32[]{:S(2)}) collective-permute-start(bf16[4,1024,256]{2,1,0:T(8,128)(2,1)} %pad_maximum_fusion), channel_id=1, source_target_pairs={{0,16},{16,0},{32,48},{48,32},{64,80},{80,64},{96,112},{112,96},{1... | collective-permute-start | bytes 6291464 | tf_op jit(solution)/shard_map/ppermute | solution.py:195
  66.1 9.4 %all-to-all-start.2 = ((f32[8,1,4096]{2,1,0:T(1,128)}), f32[8,1,4096]{2,1,0:T(1,128)S(1)}, u32[]{:S(2)}, u32[]{:S(2)}) async-start(f32[8,1,4096]{2,1,0:T(1,128)} %reshape.281), calls=%async_computation.2 | async-start | bytes 262144 | tf_op jit(solution)/shard_map/all_to_all | solution.py:171
  78.4 14.6 %all-to-all-start.3 = ((f32[16,1,4096]{2,1,0:T(1,128)}), f32[16,1,4096]{2,1,0:T(1,128)S(1)}, u32[]{:S(2)}, u32[]{:S(2)}) async-start(f32[16,1,4096]{2,1,0:T(1,128)} %reshape.283), calls=%async_computation.3 | async-start | bytes 524288 | tf_op jit(solution)/shard_map/all_to_all | solution.py:171
  113.2 9.6 %all-to-all-start.5 = ((f32[8,1,1024]{2,1,0:T(1,128)}), f32[8,1,1024]{2,1,0:T(1,128)S(1)}, u32[]{:S(2)}, u32[]{:S(2)}) async-start(f32[8,1,1024]{2,1,0:T(1,128)} %copy.14), calls=%async_computation.5 | async-start | bytes 65536 | tf_op jit(solution)/shard_map/all_to_all | solution.py:245
  122.8 19.9 %all-to-all-start.4 = ((f32[16,1,1024]{2,1,0:T(1,128)}), f32[16,1,1024]{2,1,0:T(1,128)S(1)}, u32[]{:S(2)}, u32[]{:S(2)}) async-start(f32[16,1,1024]{2,1,0:T(1,128)} %get-tuple-element.13), calls=%async_computation.4 | async-start | bytes 131072 | tf_op jit(solution)/shard_map/all_to_all | solution.py:244
  144.9 37.8 %all-to-all-start.7 = ((bf16[16,64,1024]{2,1,0:T(8,128)(2,1)}), bf16[16,64,1024]{2,1,0:T(8,128)(2,1)S(1)}, u32[]{:S(2)}, u32[]{:S(2)}) async-start(bf16[16,64,1024]{2,1,0:T(8,128)(2,1)} %broadcast_in_dim.130), calls=%async_computation.7 | async-start | bytes 4194304 | tf_op jit(solution)/shard_map/all_to_all | solution.py:171
  150.0 25.6 %all-gather.9.cloned.1.call-start = ((), (), s32[]{:S(2)}) async-start(), calls=%async_computation.19 | async-start | bytes 1179648 | tf_op jit(solution)/shard_map/all_gather | solution.py:250
  182.6 42.3 %all-to-all-start.6 = ((bf16[16,64,1024]{2,1,0:T(8,128)(2,1)}), bf16[16,64,1024]{2,1,0:T(8,128)(2,1)}, u32[]{:S(2)}, u32[]{:S(2)}) async-start(bf16[16,64,1024]{2,1,0:T(8,128)(2,1)} %copy-done.2), calls=%async_computation.6 | async-start | bytes 4194304 | tf_op jit(solution)/shard_map/all_to_all | solution.py:258
  197.0 43.2 %reduce-scatter.3.cloned.1.call-start = ((), (), s32[]{:S(2)}) async-start(), calls=%async_computation.16 | async-start | bytes 1179648 | tf_op jit(solution)/shard_map/reduce_scatter | solution.py:256
  201.7 38.5 %copy-start.4 = (bf16[1024,1024]{1,0:T(8,128)(2,1)S(1)}, bf16[1024,1024]{1,0:T(8,128)(2,1)}, u32[]{:S(2)}) copy-start(bf16[1024,1024]{1,0:T(8,128)(2,1)} %copy-done.3) | copy-start | bytes 6291460
  201.7 38.5 %copy-start.12 = (bf16[64,1024]{1,0:T(8,128)(2,1)S(1)}, bf16[64,1024]{1,0:T(8,128)(2,1)}, u32[]{:S(2)}) copy-start(bf16[64,1024]{1,0:T(8,128)(2,1)} %copy-done.11) | copy-start | bytes 393220
  283.1 36.0 %all-to-all-start.11 = ((bf16[16,64,1024]{2,1,0:T(8,128)(2,1)}), bf16[16,64,1024]{2,1,0:T(8,128)(2,1)S(1)}, u32[]{:S(2)}, u32[]{:S(2)}) async-start(bf16[16,64,1024]{2,1,0:T(8,128)(2,1)} %broadcast_in_dim.133), calls=%async_computation.12 | async-start | bytes 4194304 | tf_op jit(solution)/shard_map/all_to_all | solution.py:171
  286.9 25.2 %all-gather.11.cloned.1.call-start = ((), (), s32[]{:S(2)}) async-start(), calls=%async_computation.20 | async-start | bytes 1179648 | tf_op jit(solution)/shard_map/all_gather | solution.py:250
  319.1 42.3 %all-to-all-start.10 = ((bf16[16,64,1024]{2,1,0:T(8,128)(2,1)}), bf16[16,64,1024]{2,1,0:T(8,128)(2,1)}, u32[]{:S(2)}, u32[]{:S(2)}) async-start(bf16[16,64,1024]{2,1,0:T(8,128)(2,1)} %copy-done.1), calls=%async_computation.11 | async-start | bytes 4194304 | tf_op jit(solution)/shard_map/all_to_all | solution.py:258
  333.4 43.4 %reduce-scatter.5.cloned.1.call-start = ((), (), s32[]{:S(2)}) async-start(), calls=%async_computation.17 | async-start | bytes 1179648 | tf_op jit(solution)/shard_map/reduce_scatter | solution.py:256
  338.4 38.5 %copy-start.5 = (bf16[1024,1024]{1,0:T(8,128)(2,1)S(1)}, bf16[1024,1024]{1,0:T(8,128)(2,1)}, u32[]{:S(2)}) copy-start(bf16[1024,1024]{1,0:T(8,128)(2,1)} %copy-done.3) | copy-start | bytes 6291460
  338.4 38.5 %copy-start.10 = (bf16[64,1024]{1,0:T(8,128)(2,1)S(1)}, bf16[64,1024]{1,0:T(8,128)(2,1)}, u32[]{:S(2)}) copy-start(bf16[64,1024]{1,0:T(8,128)(2,1)} %copy-done.9) | copy-start | bytes 393220
  (10 other events, 63.9 us)
Sparse Core Ops, SparseCore 0:
  9.5 79.2 all-gather.6
  152.6 22.9 all-gather.8
  201.8 38.3 reduce-scatter.2
  289.1 22.9 all-gather.10
  338.5 38.3 reduce-scatter.4

commit v2 on v1

v2 whole, which is shorter than its diff:
```python
import functools
import math

import jax
import jax.numpy as jnp
from jax import lax
from jax.experimental import pallas as pl
from jax.experimental.pallas import tpu as pltpu
from jax.sharding import PartitionSpec as P

ITERS = 2
LOG2E = math.log2(math.e)
VMEM = 48 * 1024 * 1024
HIGH = lax.Precision.HIGHEST
RIDGE = 1e-6


def lane_sums(values):
    part = values[:, :128]
    for start in range(128, values.shape[1], 128):
        part = part + values[:, start : start + 128]
    return jnp.sum(part.T, axis=0, keepdims=True)


def half_squares(rows):
    wide = rows.astype(jnp.float32)
    return wide * wide * (0.5 * LOG2E)


def tile_chunk(left, right, right_half):
    dots = lax.dot_general(
        left, right, (((1,), (1,)), ((), ())), preferred_element_type=jnp.float32
    )
    left_half = jnp.sum(half_squares(left), axis=1, keepdims=True)
    return jnp.exp2(dots * LOG2E - left_half - right_half)


def pack_row(row):
    return jnp.concatenate([row[:, i : i + 128] for i in range(0, row.shape[1], 128)], axis=0)


def unpack_row(block):
    return jnp.concatenate([block[i : i + 1, :] for i in range(block.shape[0])], axis=1)


def packed_gram(vectors):
    gram = lax.dot_general(
        vectors,
        vectors,
        (((1,), (1,)), ((), ())),
        precision=HIGH,
        preferred_element_type=jnp.float32,
    )
    half = gram.shape[0] // 2
    return jnp.concatenate([gram[:half], gram[half:]], axis=1)


def inverse_factor(packed, ridge):
    half, width = packed.shape
    size = 2 * half
    state = jnp.concatenate([packed, pltpu.roll(packed, size, 1)], axis=0)
    row_id = lax.broadcasted_iota(jnp.int32, state.shape, 0)
    lane_id = lax.broadcasted_iota(jnp.int32, state.shape, 1)
    state = jnp.where(lane_id < size, state, jnp.where(lane_id - size == row_id, 1.0, 0.0))
    if ridge:
        on_diagonal = lane_id == row_id
        trace = jnp.sum(jnp.where(on_diagonal, state, 0.0))
        state = jnp.where(on_diagonal, state + trace * (RIDGE / size), state)
    done = []
    for start in range(0, size, 8):
        columns = [
            jnp.broadcast_to(state[:, start + j : start + j + 1], state.shape) for j in range(8)
        ]
        row_id = lax.broadcasted_iota(jnp.int32, state.shape, 0)
        scale = jnp.zeros((8, width), jnp.float32)
        for j in range(8):
            column = columns[j]
            pivot = column[j : j + 1, :]
            scale = jnp.where(row_id[:8] == j, lax.rsqrt(pivot), scale)
            factor = jnp.where(row_id > j, column * (1.0 / pivot), 0.0)
            state = state - factor * state[j : j + 1, :]
            for m in range(j + 1, 8):
                columns[m] = columns[m] - factor * column[m : m + 1, :]
        done.append(state[:8] * scale)
        state = state[8:]
    full = jnp.concatenate(done, axis=0)
    return pltpu.roll(full, size, 1)[:, :size]


def transform(matrix, vectors):
    return jnp.dot(matrix, vectors, precision=HIGH, preferred_element_type=jnp.float32)


def call(kernel, name, out_shape):
    return pl.pallas_call(
        kernel,
        out_shape=out_shape,
        compiler_params=pltpu.CompilerParams(vmem_limit_bytes=VMEM),
        name=name,
    )


def f32(*shape):
    return jax.ShapeDtypeStruct(shape, jnp.float32)


def bf16(*shape):
    return jax.ShapeDtypeStruct(shape, jnp.bfloat16)


def seed_kernel_rows(seeds, block):
    dots = lax.dot_general(
        seeds, block, (((1,), (1,)), ((), ())), preferred_element_type=jnp.float32
    )
    seed_half = jnp.sum(half_squares(seeds), axis=1, keepdims=True)
    return jnp.exp2(dots * LOG2E - seed_half - lane_sums(half_squares(block)))


def start_kernel(seeds, own, start, grams):
    value = seed_kernel_rows(seeds[...], own[...])
    start[...] = value
    grams[...] = jnp.broadcast_to(packed_gram(value)[None], grams.shape)


def first_factor_kernel(grams, start, diagonal, own_degree, factor, subspace, later_gram):
    inverse = inverse_factor(jnp.sum(grams[...], axis=0), False)
    factor[...] = inverse
    value = transform(inverse, start[...])
    subspace[...] = value
    root = lax.rsqrt(own_degree[...])
    product = jnp.dot(
        (value * root).astype(jnp.bfloat16), diagonal[...], preferred_element_type=jnp.float32
    )
    later_gram[...] = packed_gram(product * root)


def later_factor_kernel(grams, factor):
    factor[...] = inverse_factor(jnp.sum(grams[...], axis=0), True)


def degree_kernel(own_degree, row_parts, col_parts, roots, root):
    total = jnp.sum(row_parts[...], axis=0) + jnp.sum(col_parts[...], axis=0)
    value = lax.rsqrt(total + pack_row(own_degree[...]))
    roots[...] = jnp.broadcast_to(value[None], roots.shape)
    root[...] = unpack_row(value)


def gathered(own_part, first_parts, second_part, root):
    total = own_part[...] + second_part[...].astype(jnp.float32)
    for index in range(first_parts.shape[0]):
        total = total + first_parts[index].astype(jnp.float32)
    return total * root[...]


def between_kernel(own_part, first_parts, second_part, root, factor, copies, spread):
    value = transform(factor[...], gathered(own_part, first_parts, second_part, root))
    value = (value * root[...]).astype(jnp.bfloat16)
    spread[...] = value
    copies[...] = jnp.broadcast_to(value[None], copies.shape)


def last_kernel(own_part, first_parts, second_part, root, subspace, grams):
    value = gathered(own_part, first_parts, second_part, root)
    subspace[...] = value
    grams[...] = jnp.broadcast_to(packed_gram(value)[None], grams.shape)


def final_kernel(points_all, grams, subspace, embedding):
    inverse = inverse_factor(jnp.sum(grams[...], axis=0), False)
    scaled = transform(inverse, subspace[...]) * math.sqrt(points_all)
    mean = jnp.mean(scaled * scaled, axis=0, keepdims=True)
    embedding[...] = (scaled * lax.rsqrt(mean + 1e-06)).T


def relay_kernel(grams, copies):
    copies[...] = jnp.broadcast_to(jnp.sum(grams[...], axis=0)[None], copies.shape)


def vectors_kernel(first, second, live, left, right, seeds, factor, from_first, from_second):
    @pl.when(pl.program_id(0) < live[0])
    def work():
        for block, out in ((left, from_first), (right, from_second)):
            out[0] = transform(factor[...], seed_kernel_rows(seeds[...], block[0]))


def start_vectors(first, second, live, row_band, col_band, seeds, factor):
    unused, rows, depth = row_band.shape
    slots = first.shape[0]
    vecs = seeds.shape[0]

    def last(step, live_ref):
        return jnp.minimum(step, live_ref[0] - 1)

    return pl.pallas_call(
        vectors_kernel,
        grid_spec=pltpu.PrefetchScalarGridSpec(
            num_scalar_prefetch=3,
            grid=(slots,),
            in_specs=[
                pl.BlockSpec((1, rows, depth), lambda s, f, g, n: (f[last(s, n)], 0, 0)),
                pl.BlockSpec((1, rows, depth), lambda s, f, g, n: (g[last(s, n)], 0, 0)),
                pl.BlockSpec((vecs, depth), lambda s, f, g, n: (0, 0)),
                pl.BlockSpec((vecs, vecs), lambda s, f, g, n: (0, 0)),
            ],
            out_specs=[
                pl.BlockSpec((1, vecs, rows), lambda s, f, g, n: (last(s, n), 0, 0))
            ] * 2,
        ),
        out_shape=[f32(slots, vecs, rows)] * 2,
        compiler_params=pltpu.CompilerParams(vmem_limit_bytes=VMEM),
        name="start_vectors",
    )(first, second, live, row_band, col_band, seeds, factor)


def form_kernel(chunk, first, second, live, left, right, tile, row_deg, col_deg):
    step = pl.program_id(0)

    @pl.when(step == 0)
    def clear():
        row_deg[...] = jnp.zeros_like(row_deg)
        col_deg[...] = jnp.zeros_like(col_deg)

    @pl.when(step < live[0])
    def work():
        rows = left.shape[1]
        right_rows = right[0]
        right_half = lane_sums(half_squares(right_rows))
        col_total = jnp.zeros((1, rows), jnp.float32)
        row_totals = []
        for start in range(0, rows, chunk):
            value = tile_chunk(left[0, start : start + chunk, :], right_rows, right_half)
            tile[0, start : start + chunk, :] = value.astype(jnp.bfloat16)
            col_total = col_total + jnp.sum(value, axis=0, keepdims=True)
            row_totals.append(lane_sums(value))
        row_slot = first[step]
        col_slot = second[step]
        row_total = jnp.concatenate(row_totals, axis=1)
        row_deg[row_slot] = row_deg[row_slot] + pack_row(row_total)
        col_deg[col_slot] = col_deg[col_slot] + pack_row(col_total)


def form_tiles(first, second, live, row_band, col_band):
    col_devices, rows, depth = row_band.shape
    row_devices = col_band.shape[0]
    slots = first.shape[0]

    def last(step, live_ref):
        return jnp.minimum(step, live_ref[0] - 1)

    return pl.pallas_call(
        functools.partial(form_kernel, min(256, rows)),
        grid_spec=pltpu.PrefetchScalarGridSpec(
            num_scalar_prefetch=3,
            grid=(slots,),
            in_specs=[
                pl.BlockSpec((1, rows, depth), lambda s, f, g, n: (f[last(s, n)], 0, 0)),
                pl.BlockSpec((1, rows, depth), lambda s, f, g, n: (g[last(s, n)], 0, 0)),
            ],
            out_specs=[
                pl.BlockSpec((1, rows, rows), lambda s, f, g, n: (last(s, n), 0, 0)),
                pl.BlockSpec((col_devices, rows // 128, 128), lambda s, f, g, n: (0, 0, 0)),
                pl.BlockSpec((row_devices, rows // 128, 128), lambda s, f, g, n: (0, 0, 0)),
            ],
        ),
        out_shape=[
            bf16(slots, rows, rows),
            f32(col_devices, rows // 128, 128),
            f32(row_devices, rows // 128, 128),
        ],
        compiler_params=pltpu.CompilerParams(vmem_limit_bytes=VMEM),
        name="form_tiles",
    )(first, second, live, row_band, col_band)


def diagonal_kernel(chunk, own, tile, degree):
    rows = own.shape[0]
    right_rows = own[...]
    right_half = lane_sums(half_squares(right_rows))
    total = jnp.zeros((1, rows), jnp.float32)
    for start in range(0, rows, chunk):
        value = tile_chunk(own[start : start + chunk, :], right_rows, right_half)
        tile[start : start + chunk, :] = value.astype(jnp.bfloat16)
        total = total + jnp.sum(value, axis=0, keepdims=True)
    degree[...] = total


def form_diagonal(own):
    rows = own.shape[0]
    return pl.pallas_call(
        functools.partial(diagonal_kernel, min(256, rows)),
        out_shape=[
            jax.ShapeDtypeStruct((rows, rows), jnp.bfloat16),
            jax.ShapeDtypeStruct((1, rows), jnp.float32),
        ],
        compiler_params=pltpu.CompilerParams(vmem_limit_bytes=VMEM),
        name="form_diagonal",
    )(own)


def apply_kernel(contract, source, target, live, tile, vectors, *rest):
    step = pl.program_id(0)
    roots, out, total = rest if len(rest) == 3 else (None,) + rest

    @pl.when(step == 0)
    def clear():
        total[...] = jnp.zeros_like(total)

    @pl.when(step < live[0])
    def work():
        slot = target[step]
        block = vectors[0]
        if roots is not None:
            block = (block * unpack_row(roots[0])).astype(jnp.bfloat16)
        total[slot] = total[slot] + lax.dot_general(
            block, tile[0], (((1,), (contract,)), ((), ())), preferred_element_type=jnp.float32
        )

    @pl.when(step == pl.num_programs(0) - 1)
    def store():
        out[...] = total[...].astype(jnp.bfloat16)


def apply_tiles(contract, source, target, live, tiles, vectors, roots, targets):
    slots, rows, unused = tiles.shape
    vecs = vectors.shape[1]

    def last(step, live_ref):
        return jnp.minimum(step, live_ref[0] - 1)

    def by_task(s, f, g, n):
        return (last(s, n), 0, 0)

    def by_block(s, f, g, n):
        return (f[last(s, n)], 0, 0)

    in_specs = [
        pl.BlockSpec((1, rows, rows), by_task),
        pl.BlockSpec((1, vecs, rows), by_block if roots is None else by_task),
    ]
    operands = [tiles, vectors]
    if roots is not None:
        in_specs.append(pl.BlockSpec((1, rows // 128, 128), by_block))
        operands.append(roots)
    return pl.pallas_call(
        functools.partial(apply_kernel, contract),
        grid_spec=pltpu.PrefetchScalarGridSpec(
            num_scalar_prefetch=3,
            grid=(slots,),
            in_specs=in_specs,
            out_specs=pl.BlockSpec((targets, vecs, rows), lambda s, f, g, n: (0, 0, 0)),
            scratch_shapes=[pltpu.VMEM((targets, vecs, rows), jnp.float32)],
        ),
        out_shape=bf16(targets, vecs, rows),
        compiler_params=pltpu.CompilerParams(vmem_limit_bytes=VMEM),
        name="apply_tiles",
    )(source, target, live, *operands)


def spread_to(array, axis):
    devices = lax.axis_size(axis)
    copies = jnp.broadcast_to(array[None], (devices,) + array.shape)
    return lax.all_to_all(copies, axis, 0, 0, tiled=True)


def exchange(copies, axis):
    return lax.all_to_all(copies, axis, 0, 0, tiled=True)


def together(*arrays):
    return lax.optimization_barrier(arrays)


def place_in_row(index):
    here = lax.axis_index("row")
    apart = (index // 2 - here // 2) % 4
    order = jnp.where(apart == 0, 0, jnp.where(apart == 3, 1, jnp.where(apart == 1, 2, 3)))
    return order + 4 * ((index - here) % 2)


def shards(points, feature_scale, tile_tasks, task_count, seed_ids):
    rows = points.shape[0]
    vecs = seed_ids.shape[0]
    row_devices = lax.axis_size("row")
    col_devices = lax.axis_size("col")
    all_devices = row_devices * col_devices
    self_index = lax.axis_index("row") * col_devices + lax.axis_index("col")
    weighted = (points.astype(jnp.float32) * feature_scale[None, :]).astype(jnp.bfloat16)
    row_band = lax.all_gather(weighted, "col", axis=0)
    listed = tile_tasks.reshape(-1)
    live = task_count.reshape(1)
    used = jnp.where(jnp.arange(listed.shape[0]) < live, listed, 0)
    first = used % col_devices
    second_device = used // col_devices
    second = place_in_row(second_device)

    def shift(array, by):
        return lax.ppermute(
            array, "row", [(i, (i + by) % row_devices) for i in range(row_devices)]
        )

    local_seed = seed_ids - self_index * rows
    inside = (local_seed >= 0) & (local_seed < rows)
    picked = jnp.where(
        inside[:, None], jnp.take(weighted, jnp.clip(local_seed, 0, rows - 1), axis=0), 0
    ).astype(jnp.bfloat16)
    seed_parts = spread_to(picked, "row")
    before = shift(weighted, 2)
    after = shift(weighted, -2)
    before, after, seed_parts = together(before, after, seed_parts)
    half = rows // 2
    across_low = shift(before[:half], 2)
    across_high = shift(after[half:], -2)
    seed_parts = spread_to(jnp.sum(seed_parts, axis=0), "col")
    across_low, across_high, seed_parts = together(across_low, across_high, seed_parts)
    seeds = jnp.sum(seed_parts, axis=0)
    across = jnp.concatenate([across_low, across_high], axis=0)
    mine = jnp.stack([weighted, before, after, across])
    other = lax.ppermute(mine, "row", [(i, i ^ 1) for i in range(row_devices)])

    start, grams = call(
        start_kernel, "start", [f32(vecs, rows), f32(row_devices, vecs // 2, 2 * vecs)]
    )(seeds, weighted)
    grams = exchange(grams, "row")
    col_band, grams = together(jnp.concatenate([mine, other], axis=0), grams)
    grams = call(relay_kernel, "relay", f32(col_devices, vecs // 2, 2 * vecs))(grams)
    grams = exchange(grams, "col")
    diagonal, own_degree = form_diagonal(weighted)
    factor, subspace, later_gram = call(
        first_factor_kernel,
        "first_factor",
        [f32(vecs, vecs), f32(vecs, rows), f32(vecs // 2, 2 * vecs)],
    )(grams, start, diagonal, own_degree)
    later_grams = lax.all_gather(later_gram, ("row", "col"), axis=0)

    tiles, row_deg, col_deg = form_tiles(first, second, live, row_band, col_band)
    row_places = place_in_row(jnp.arange(row_devices))
    col_deg = jnp.take(col_deg, row_places, axis=0)
    row_parts = exchange(row_deg, "col")
    col_parts = exchange(col_deg, "row")
    roots, inv_root = call(
        degree_kernel, "degree", [f32(col_devices, rows // 128, 128), f32(1, rows)]
    )(own_degree, row_parts, col_parts)
    from_first, from_second = start_vectors(
        first, second, live, row_band, col_band, seeds, factor
    )
    col_roots = exchange(roots[:row_devices], "row")
    row_roots = exchange(roots, "col")
    spread = (subspace * inv_root).astype(jnp.bfloat16)
    for iteration in range(ITERS):
        own_part = lax.dot_general(
            spread, diagonal, (((1,), (0,)), ((), ())), preferred_element_type=jnp.float32
        )
        to_second = apply_tiles(
            0, first, second_device, live, tiles, from_first, row_roots, row_devices
        )
        to_second, from_second = together(to_second, from_second)
        second_part = lax.psum_scatter(to_second, "row", scatter_dimension=0, tiled=False)
        to_first = apply_tiles(
            1, second_device, first, live, tiles, from_second, col_roots, col_devices
        )
        first_parts = exchange(to_first, "col")
        if iteration + 1 < ITERS:
            later_factor = call(later_factor_kernel, "later_factor", f32(vecs, vecs))(later_grams)
            copies, spread = call(
                between_kernel, "between", [bf16(col_devices, vecs, rows), bf16(vecs, rows)]
            )(own_part, first_parts, second_part, inv_root, later_factor)
            from_second = lax.all_gather(spread, "row", axis=0)
            from_first = exchange(copies, "col")
            row_roots = col_roots = None
    subspace, grams = call(
        last_kernel, "last", [f32(vecs, rows), f32(row_devices, vecs // 2, 2 * vecs)]
    )(own_part, first_parts, second_part, inv_root)
    grams = exchange(grams, "row")
    grams = call(relay_kernel, "relay", f32(col_devices, vecs // 2, 2 * vecs))(grams)
    grams = exchange(grams, "col")
    return call(
        functools.partial(final_kernel, all_devices * rows), "final", f32(rows, vecs)
    )(grams, subspace)


def solution(mesh):
    return jax.shard_map(
        shards,
        mesh=mesh,
        in_specs=(P(("row", "col"), None), P(), P("row", "col", None), P("row", "col"), P()),
        out_specs=P(("row", "col"), None),
        check_vma=False,
    )
```

time: 427 us -> 346 us (0.81); the launches traced: 425 us -> 340 us
  waiting for transfers between devices: 169 us -> 93.4 us
  other arithmetic: 53.9 us -> 5.07 us
  blocking collectives: 47.3 us -> 80.4 us
  Pallas kernels: 25.6 us -> 46 us
  starting transfers between devices: 82.6 us -> 74.5 us
    all_to_all x0 -> x5, blocking collectives: none -> 66.6 us  [exchange(): return lax.all_to_all(copies, axis, 0, 0, tiled=True)]
    all_gather x2, waiting for transfers between devices: 49.5 us -> 0.02 us  [the longest x1 0.02 us: shards(): later_grams = lax.all_gather(later_gram, ('row', 'col'), axis=0)]
    another operation x17 -> x2, other arithmetic: 37.8 us -> 1.63 us  [shards(): mine = jnp.stack([weighted, before, after, across])]
    all_to_all x4 -> x1, blocking collectives: 47.3 us -> 13.8 us  [spread_to(): return lax.all_to_all(copies, axis, 0, 0, tiled=True)]
    all_to_all x4 -> x6, waiting for transfers between devices: 53.1 us -> 83.6 us  [exchange(): return lax.all_to_all(copies, axis, 0, 0, tiled=True)]
    all_to_all x6 -> x1, waiting for transfers between devices: 29.8 us -> 2.41 us  [spread_to(): return lax.all_to_all(copies, axis, 0, 0, tiled=True)]
    reduce_scatter x2, waiting for transfers between devices: 26.7 us -> 0.01 us  [shards(): lax.psum_scatter(to_second, 'row', scatter_dimension=0, tiled=False)]
    all_to_all x6 -> x1, starting transfers between devices: 30.4 us -> 8.05 us  [spread_to(): return lax.all_to_all(copies, axis, 0, 0, tiled=True)]
  transfers between devices with their start and end apart: 20 -> 17, of which waited for: 13 -> 9; matrix products, arithmetic and copies ran while one was open for 8% -> 4% of each run, Pallas kernels for 5% -> 11%
where the time goes in v2:
time: 346 us; the launch traced here: 340 us
  waiting for transfers between devices  93.4 us (27%)
  blocking collectives  80.4 us (23%)
  starting transfers between devices  74.5 us (22%)
  Pallas kernels  46 us (13%)
  local copies, waits for them, and re-layouts  24.2 us (7%)
  between operations  14.1 us (4%)
  other arithmetic  5.07 us (1%)
    all_to_all x6, waiting for transfers between devices, exchange(): return lax.all_to_all(copies, axis, 0, 0, tiled=True)  83.6 us
    all_to_all x5, blocking collectives, exchange(): return lax.all_to_all(copies, axis, 0, 0, tiled=True)  66.6 us
    all_to_all x6, starting transfers between devices, exchange(): return lax.all_to_all(copies, axis, 0, 0, tiled=True)  59.6 us
    pallas_call x4, Pallas kernels, apply_tiles(): pl.pallas_call(functools.partial(apply_kernel, contract), grid_spec=pltpu...  18.2 us
    unnamed x30, local copies, waits for them, and re-layouts  16.2 us
    all_to_all x1, blocking collectives, spread_to(): return lax.all_to_all(copies, axis, 0, 0, tiled=True)  13.8 us
    all_to_all x1, starting transfers between devices, spread_to(): return lax.all_to_all(copies, axis, 0, 0, tiled=True)  8.05 us
  transfers between devices with their start and end apart: 17, of which 9 were waited for; matrix products, arithmetic and copies ran while one was open for 4% of the time, Pallas kernels for 11%

profile of v2, /device:TPU:0, one launch (start us, length us, event | category | flops | bytes accessed | tf_op | source)
XLA Modules:
  0.0 339.5 jit_solution(10669629635033733836)
XLA Ops:
  14.0 13.8 %all_to_all.65 = bf16[8,64,256]{2,1,0:T(8,128)(2,1)S(1)} all-to-all(bf16[8,64,256]{2,1,0:T(8,128)(2,1)S(1)} %broadcast_in_dim.70), channel_id=1, replica_groups=mesh['row'=8,'col'=16] {'row'}, dimensions={0} | all-to-all | bytes 524288 | tf_op jit(solution)/shard_map/all_to_all | solution.py:362
  28.7 8.0 %all-to-all-start.1 = ((bf16[16,64,256]{2,1,0:T(8,128)(2,1)}), bf16[16,64,256]{2,1,0:T(8,128)(2,1)S(1)}, u32[]{:S(2)}, u32[]{:S(2)}) async-start(bf16[16,64,256]{2,1,0:T(8,128)(2,1)} %broadcast_in_dim.71), calls=%async_computation.1 | async-start | bytes 1048576 | tf_op jit(solution)/shard_map/all_to_all | solution.py:362
  40.2 5.3 %collective-permute-done.2 = bf16[512,256]{1,0:T(8,128)(2,1)S(1)} collective-permute-done((bf16[512,256]{1,0:T(8,128)(2,1)S(1)}, bf16[512,256]{1,0:T(8,128)(2,1)S(1)}, u32[]{:S(2)}, u32[]{:S(2)}) %collective-permute-start.2) | collective-permute-done | bytes 262176 | tf_op jit(solution)/shard_map/ppermute | solution.py:397
  63.0 5.7 %all-to-all-start.3 = ((f32[16,32,128]{2,1,0:T(8,128)}), f32[16,32,128]{2,1,0:T(8,128)S(1)}, u32[]{:S(2)}, u32[]{:S(2)}) async-start(f32[16,32,128]{2,1,0:T(8,128)} %relay.2), calls=%async_computation.3 | async-start | bytes 524288 | tf_op jit(solution)/shard_map/all_to_all | solution.py:366
  69.9 10.0 %all-to-all-done.3.grams = f32[16,32,128]{2,1,0:T(8,128)S(1)} async-done(((f32[16,32,128]{2,1,0:T(8,128)}), f32[16,32,128]{2,1,0:T(8,128)S(1)}, u32[]{:S(2)}, u32[]{:S(2)}) %all-to-all-start.3) | async-done | bytes 262176 | tf_op jit(solution)/shard_map/all_to_all | solution.py:366
  79.9 3.5 %first_factor.1 = (f32[64,64]{1,0:T(8,128)S(1)}, f32[64,1024]{1,0:T(8,128)S(1)}, f32[32,128]{1,0:T(8,128)}) custom-call(f32[16,32,128]{2,1,0:T(8,128)S(1)} %all-to-all-done.3.grams, f32[64,1024]{1,0:T(8,128)S(1)} %get-tuple-element.43.start, bf16[1024,1024]{1,0:T(8,128)(2,1)S(1)} %get-tuple-element.44.diagonal, f32[1,1024]{1,0:T(1,128)S(1)} %get-tuple-element.45.own_degree), custom_call_target="tpu_custom_call" | custom-call | tf_op jit(solution)/shard_map/first_factor/pallas_call | solution.py:428
  85.7 6.3 %form_tiles.1 = (bf16[8,1024,1024]{2,1,0:T(8,128)(2,1)}, f32[16,8,128]{2,1,0:T(8,128)S(1)}, f32[8,8,128]{2,1,0:T(8,128)S(1)}) custom-call(s32[8]{0:T(128)S(1)} %and_select_fusion.10.first.source.target, s32[8]{0:T(128)S(1)} %get-tuple-element.65.second, s32[1]{0:T(128)} %bitcast.32.live, bf16[16,1024,256]{2,1,0:T(8,128)(2,1)} %bitcast.44, ...), custom_call_target="tpu_custom_call" | custom-call | tf_op jit(solution)/shard_map/form_tiles/pallas_call | solution.py:250
  92.6 9.2 %all_to_all.66.col_parts = f32[8,8,128]{2,1,0:T(8,128)S(1)} all-to-all(f32[8,8,128]{2,1,0:T(8,128)S(1)} %broadcast_select_fusion), channel_id=1, replica_groups=mesh['row'=8,'col'=16] {'row'}, dimensions={0} | all-to-all | bytes 65536 | tf_op jit(solution)/shard_map/all_to_all | solution.py:366
  101.8 22.6 %all_to_all.67.row_parts = f32[16,8,128]{2,1,0:T(8,128)S(1)} all-to-all(f32[16,8,128]{2,1,0:T(8,128)S(1)} %get-tuple-element.48), channel_id=1, replica_groups=mesh['row'=8,'col'=16] {'col'}, dimensions={0} | all-to-all | bytes 131072 | tf_op jit(solution)/shard_map/all_to_all | solution.py:366
  125.1 3.5 %all-to-all-start.6 = ((f32[16,8,128]{2,1,0:T(8,128)}), f32[16,8,128]{2,1,0:T(8,128)S(1)}, u32[]{:S(2)}, u32[]{:S(2)}) async-start(f32[16,8,128]{2,1,0:T(8,128)} %get-tuple-element.54), calls=%async_computation.6 | async-start | bytes 131072 | tf_op jit(solution)/shard_map/all_to_all | solution.py:366
  128.7 4.2 %start_vectors.1 = (f32[8,64,1024]{2,1,0:T(8,128)S(1)}, f32[8,64,1024]{2,1,0:T(8,128)S(1)}) custom-call(s32[8]{0:T(128)S(1)} %and_select_fusion.10.first.source.target, s32[8]{0:T(128)S(1)} %get-tuple-element.65.second, s32[1]{0:T(128)} %bitcast.33.live, bf16[16,1024,256]{2,1,0:T(8,128)(2,1)} %bitcast.45, ...), custom_call_target="tpu_custom_call" | custom-call | tf_op jit(solution)/shard_map/start_vectors/pallas_call | solution.py:194
  137.9 4.7 %apply_tiles.4 = bf16[8,64,1024]{2,1,0:T(8,128)(2,1)} custom-call(s32[8]{0:T(128)S(1)} %and_select_fusion.10.first.source.target, s32[8]{0:T(128)S(1)} %get-tuple-element.66.target.source, s32[1]{0:T(128)} %bitcast.34.live, bf16[8,1024,1024]{2,1,0:T(8,128)(2,1)} %get-tuple-element.51.tile, f32[8,64,1024]{2,1,0:T(8,128)S(1)} %copy-done.6, ...), custom_call_target="tpu_custom_call" | custom-call | tf_op jit(solution)/shard_map/apply_tiles/pallas_call | solution.py:344
  143.4 7.8 %all_to_all.68.rest_0_ = f32[8,8,128]{2,1,0:T(8,128)S(1)} all-to-all(f32[8,8,128]{2,1,0:T(8,128)S(1)} %slice.11), channel_id=1, replica_groups=mesh['row'=8,'col'=16] {'row'}, dimensions={0} | all-to-all | bytes 65536 | tf_op jit(solution)/shard_map/all_to_all | solution.py:366
  152.8 4.4 %apply_tiles.5 = bf16[16,64,1024]{2,1,0:T(8,128)(2,1)S(1)} custom-call(s32[8]{0:T(128)S(1)} %get-tuple-element.66.target.source, s32[8]{0:T(128)S(1)} %and_select_fusion.10.first.source.target, s32[1]{0:T(128)} %bitcast.35.live, bf16[8,1024,1024]{2,1,0:T(8,128)(2,1)} %get-tuple-element.51.tile, f32[8,64,1024]{2,1,0:T(8,128)S(1)} %copy-done.4, ...), custom_call_target="tpu_custom_call" | custom-call | tf_op jit(solution)/shard_map/apply_tiles/pallas_call | solution.py:344
  158.6 26.4 %all-to-all-start.8 = ((bf16[16,64,1024]{2,1,0:T(8,128)(2,1)}), bf16[16,64,1024]{2,1,0:T(8,128)(2,1)}, u32[]{:S(2)}, u32[]{:S(2)}) async-start(bf16[16,64,1024]{2,1,0:T(8,128)(2,1)} %copy-done.1), calls=%async_computation.8 | async-start | bytes 4194304 | tf_op jit(solution)/shard_map/all_to_all | solution.py:366
  189.2 23.5 %all-to-all-done.8.first_parts = bf16[16,64,1024]{2,1,0:T(8,128)(2,1)} async-done(((bf16[16,64,1024]{2,1,0:T(8,128)(2,1)}), bf16[16,64,1024]{2,1,0:T(8,128)(2,1)}, u32[]{:S(2)}, u32[]{:S(2)}) %all-to-all-start.8) | async-done | bytes 2097184 | tf_op jit(solution)/shard_map/all_to_all | solution.py:366
  218.0 4.5 %all-to-all-start.9 = ((bf16[16,64,1024]{2,1,0:T(8,128)(2,1)}), bf16[16,64,1024]{2,1,0:T(8,128)(2,1)}, u32[]{:S(2)}, u32[]{:S(2)}) async-start(bf16[16,64,1024]{2,1,0:T(8,128)(2,1)} %copy-done.8), calls=%async_computation.10 | async-start | bytes 4194304 | tf_op jit(solution)/shard_map/all_to_all | solution.py:366
  223.1 25.8 %all-to-all-done.9.vectors = bf16[16,64,1024]{2,1,0:T(8,128)(2,1)} async-done(((bf16[16,64,1024]{2,1,0:T(8,128)(2,1)}), bf16[16,64,1024]{2,1,0:T(8,128)(2,1)}, u32[]{:S(2)}, u32[]{:S(2)}) %all-to-all-start.9) | async-done | bytes 2097184 | tf_op jit(solution)/shard_map/all_to_all | solution.py:366
  248.9 4.7 %apply_tiles.6 = bf16[8,64,1024]{2,1,0:T(8,128)(2,1)} custom-call(s32[8]{0:T(128)S(1)} %and_select_fusion.10.first.source.target, s32[8]{0:T(128)S(1)} %get-tuple-element.66.target.source, s32[1]{0:T(128)} %bitcast.36.live, bf16[8,1024,1024]{2,1,0:T(8,128)(2,1)} %get-tuple-element.51.tile, bf16[16,64,1024]{2,1,0:T(8,128)(2,1)} %all-to-all-done.9.vectors), custom_call_target="tpu_custom_call" | custom-call | tf_op jit(solution)/shard_map/apply_tiles/pallas_call | solution.py:344
  254.8 4.4 %apply_tiles.7 = bf16[16,64,1024]{2,1,0:T(8,128)(2,1)S(1)} custom-call(s32[8]{0:T(128)S(1)} %get-tuple-element.66.target.source, s32[8]{0:T(128)S(1)} %and_select_fusion.10.first.source.target, s32[1]{0:T(128)} %bitcast.37.live, bf16[8,1024,1024]{2,1,0:T(8,128)(2,1)} %get-tuple-element.51.tile, bf16[8,64,1024]{2,1,0:T(8,128)(2,1)S(1)} %bitcast.40), custom_call_target="tpu_custom_call" | custom-call | tf_op jit(solution)/shard_map/apply_tiles/pallas_call | solution.py:344
  260.6 16.2 %all-to-all-start.10 = ((bf16[16,64,1024]{2,1,0:T(8,128)(2,1)}), bf16[16,64,1024]{2,1,0:T(8,128)(2,1)}, u32[]{:S(2)}, u32[]{:S(2)}) async-start(bf16[16,64,1024]{2,1,0:T(8,128)(2,1)} %copy-done.2), calls=%async_computation.11 | async-start | bytes 4194304 | tf_op jit(solution)/shard_map/all_to_all | solution.py:366
  278.2 21.4 %all-to-all-done.10.first_parts = bf16[16,64,1024]{2,1,0:T(8,128)(2,1)} async-done(((bf16[16,64,1024]{2,1,0:T(8,128)(2,1)}), bf16[16,64,1024]{2,1,0:T(8,128)(2,1)}, u32[]{:S(2)}, u32[]{:S(2)}) %all-to-all-start.10) | async-done | bytes 2097184 | tf_op jit(solution)/shard_map/all_to_all | solution.py:366
  302.8 14.6 %all_to_all.69.grams = f32[8,32,128]{2,1,0:T(8,128)S(1)} all-to-all(f32[8,32,128]{2,1,0:T(8,128)S(1)} %get-tuple-element.63), channel_id=1, replica_groups=mesh['row'=8,'col'=16] {'row'}, dimensions={0} | all-to-all | bytes 262144 | tf_op jit(solution)/shard_map/all_to_all | solution.py:366
  317.5 12.4 %all_to_all.70.grams = f32[16,32,128]{2,1,0:T(8,128)S(1)} all-to-all(f32[16,32,128]{2,1,0:T(8,128)S(1)} %relay.3), channel_id=1, replica_groups=mesh['row'=8,'col'=16] {'col'}, dimensions={0} | all-to-all | bytes 524288 | tf_op jit(solution)/shard_map/all_to_all | solution.py:366
  (92 shorter events, 62.6 us)
Async XLA Ops:
  6.5 5.6 %copy-start.12 = (s32[64]{0:T(128)S(1)}, s32[64]{0:T(128)}, u32[]{:S(2)}) copy-start(s32[64]{0:T(128)} %param.9) | copy-start | bytes 772
  6.5 79.1 %all-gather.7.cloned.1.call-start = ((), (), s32[]{:S(2)}) async-start(), calls=%async_computation.17 | async-start | bytes 8912896 | tf_op jit(solution)/shard_map/all_gather | solution.py:388
  8.8 19.0 %collective-permute-start = (bf16[1024,256]{1,0:T(8,128)(2,1)}, bf16[1024,256]{1,0:T(8,128)(2,1)S(1)}, u32[]{:S(2)}, u32[]{:S(2)}) collective-permute-start(bf16[1024,256]{1,0:T(8,128)(2,1)} %get-tuple-element.71.own), channel_id=1, source_target_pairs={{0,32},{16,48},{32,64},{48,80},{64,96},{80,112},{96,0},{112,16},{1... | collective-permute-start | bytes 1572872 | tf_op jit(solution)/shard_map/ppermute | solution.py:397
  10.4 17.4 %collective-permute-start.1 = (bf16[1024,256]{1,0:T(8,128)(2,1)}, bf16[1024,256]{1,0:T(8,128)(2,1)S(1)}, u32[]{:S(2)}, u32[]{:S(2)}) collective-permute-start(bf16[1024,256]{1,0:T(8,128)(2,1)} %get-tuple-element.71.own), channel_id=1, source_target_pairs={{0,96},{16,112},{32,0},{48,16},{64,32},{80,48},{96,64},{112,80},{1... | collective-permute-start | bytes 1572872 | tf_op jit(solution)/shard_map/ppermute | solution.py:397
  27.8 20.1 %copy-start = (bf16[1024,256]{1,0:T(8,128)(2,1)S(1)}, bf16[1024,256]{1,0:T(8,128)(2,1)}, u32[]{:S(2)}) copy-start(bf16[1024,256]{1,0:T(8,128)(2,1)} %get-tuple-element.71.own) | copy-start | bytes 1572868
  28.7 19.2 %all-to-all-start.1 = ((bf16[16,64,256]{2,1,0:T(8,128)(2,1)}), bf16[16,64,256]{2,1,0:T(8,128)(2,1)S(1)}, u32[]{:S(2)}, u32[]{:S(2)}) async-start(bf16[16,64,256]{2,1,0:T(8,128)(2,1)} %broadcast_in_dim.71), calls=%async_computation.1 | async-start | bytes 1048576 | tf_op jit(solution)/shard_map/all_to_all | solution.py:362
  36.8 8.7 %collective-permute-start.2 = (bf16[512,256]{1,0:T(8,128)(2,1)S(1)}, bf16[512,256]{1,0:T(8,128)(2,1)S(1)}, u32[]{:S(2)}, u32[]{:S(2)}) collective-permute-start(bf16[512,256]{1,0:T(8,128)(2,1)S(1)} %slice.9), channel_id=1, source_target_pairs={{0,32},{16,48},{32,64},{48,80},{64,96},{80,112},{96,0},{112,16},{1... | collective-permute-start | bytes 786440 | tf_op jit(solution)/shard_map/ppermute | solution.py:397
  38.0 7.5 %collective-permute-start.3 = (bf16[512,256]{1,0:T(8,128)(2,1)S(1)}, bf16[512,256]{1,0:T(8,128)(2,1)S(1)}, u32[]{:S(2)}, u32[]{:S(2)}) collective-permute-start(bf16[512,256]{1,0:T(8,128)(2,1)S(1)} %slice.10), channel_id=1, source_target_pairs={{0,96},{16,112},{32,0},{48,16},{64,32},{80,48},{96,64},{112,80},{1... | collective-permute-start | bytes 786440 | tf_op jit(solution)/shard_map/ppermute | solution.py:397
  49.6 7.5 %collective-permute-start.4 = (bf16[4,1024,256]{2,1,0:T(8,128)(2,1)}, bf16[4,1024,256]{2,1,0:T(8,128)(2,1)}, u32[]{:S(2)}, u32[]{:S(2)}) collective-permute-start(bf16[4,1024,256]{2,1,0:T(8,128)(2,1)} %pad_maximum_fusion), channel_id=1, source_target_pairs={{0,16},{16,0},{32,48},{48,32},{64,80},{80,64},{96,112},{112,96},{1... | collective-permute-start | bytes 6291464 | tf_op jit(solution)/shard_map/ppermute | solution.py:418
  52.8 9.4 %all-to-all-start.2 = ((f32[8,32,128]{2,1,0:T(8,128)}), f32[8,32,128]{2,1,0:T(8,128)S(1)}, u32[]{:S(2)}, u32[]{:S(2)}) async-start(f32[8,32,128]{2,1,0:T(8,128)} %get-tuple-element.41), calls=%async_computation.2 | async-start | bytes 262144 | tf_op jit(solution)/shard_map/all_to_all | solution.py:366
  60.2 24.0 %copy-start.13 = (s32[1,1,8]{2,1,0:T(1,128)S(1)}, s32[1,1,8]{2,1,0:T(1,128)}, u32[]{:S(2)}) copy-start(s32[1,1,8]{2,1,0:T(1,128)} %param.7) | copy-start | bytes 100
  63.0 16.9 %all-to-all-start.3 = ((f32[16,32,128]{2,1,0:T(8,128)}), f32[16,32,128]{2,1,0:T(8,128)S(1)}, u32[]{:S(2)}, u32[]{:S(2)}) async-start(f32[16,32,128]{2,1,0:T(8,128)} %relay.2), calls=%async_computation.3 | async-start | bytes 524288 | tf_op jit(solution)/shard_map/all_to_all | solution.py:366
  68.6 116.4 %all-gather.9.cloned.1.call-start = ((), (), s32[]{:S(2)}) async-start(), calls=%async_computation.18 | async-start | bytes 2113536 | tf_op jit(solution)/shard_map/all_gather | solution.py:433
  125.1 11.2 %all-to-all-start.6 = ((f32[16,8,128]{2,1,0:T(8,128)}), f32[16,8,128]{2,1,0:T(8,128)S(1)}, u32[]{:S(2)}, u32[]{:S(2)}) async-start(f32[16,8,128]{2,1,0:T(8,128)} %get-tuple-element.54), calls=%async_computation.6 | async-start | bytes 131072 | tf_op jit(solution)/shard_map/all_to_all | solution.py:366
  128.7 84.0 %reduce-scatter.3.cloned.1.call-start = ((), (), s32[]{:S(2)}) async-start(), calls=%async_computation.15 | async-start | bytes 1179648 | tf_op jit(solution)/shard_map/reduce_scatter | solution.py:457
  136.3 1.6 copy-start.6
  151.2 1.6 copy-start.4
  158.6 54.1 %all-to-all-start.8 = ((bf16[16,64,1024]{2,1,0:T(8,128)(2,1)}), bf16[16,64,1024]{2,1,0:T(8,128)(2,1)}, u32[]{:S(2)}, u32[]{:S(2)}) async-start(bf16[16,64,1024]{2,1,0:T(8,128)(2,1)} %copy-done.1), calls=%async_computation.8 | async-start | bytes 4194304 | tf_op jit(solution)/shard_map/all_to_all | solution.py:366
  185.0 1.6 copy-start.7
  218.0 30.9 %all-to-all-start.9 = ((bf16[16,64,1024]{2,1,0:T(8,128)(2,1)}), bf16[16,64,1024]{2,1,0:T(8,128)(2,1)}, u32[]{:S(2)}, u32[]{:S(2)}) async-start(bf16[16,64,1024]{2,1,0:T(8,128)(2,1)} %copy-done.8), calls=%async_computation.10 | async-start | bytes 4194304 | tf_op jit(solution)/shard_map/all_to_all | solution.py:366
  222.5 31.1 %all-gather.11.cloned.1.call-start = ((), (), s32[]{:S(2)}) async-start(), calls=%async_computation.19 | async-start | bytes 1179648 | tf_op jit(solution)/shard_map/all_gather | solution.py:467
  223.0 76.6 %reduce-scatter.5.cloned.1.call-start = ((), (), s32[]{:S(2)}) async-start(), calls=%async_computation.16 | async-start | bytes 1179648 | tf_op jit(solution)/shard_map/reduce_scatter | solution.py:457
  259.3 1.3 copy-start.2
  260.6 39.0 %all-to-all-start.10 = ((bf16[16,64,1024]{2,1,0:T(8,128)(2,1)}), bf16[16,64,1024]{2,1,0:T(8,128)(2,1)}, u32[]{:S(2)}, u32[]{:S(2)}) async-start(bf16[16,64,1024]{2,1,0:T(8,128)(2,1)} %copy-done.2), calls=%async_computation.11 | async-start | bytes 4194304 | tf_op jit(solution)/shard_map/all_to_all | solution.py:366
  (7 other events, 8.4 us)
Sparse Core Ops, SparseCore 0:
  9.5 76.1 all-gather.6
  88.6 64.7 all-gather.8
  155.8 30.7 reduce-scatter.2
  224.7 23.5 all-gather.10
  253.7 37.3 reduce-scatter.4

commit v3 on v2

--- a/solution.py
+++ b/solution.py
@@ -10,7 +10,7 @@
 
 ITERS = 2
 LOG2E = math.log2(math.e)
-VMEM = 48 * 1024 * 1024
+VMEM = 60 * 1024 * 1024
 HIGH = lax.Precision.HIGHEST
 RIDGE = 1e-6
 
@@ -189,7 +189,7 @@
     vecs = seeds.shape[0]
 
     def last(step, live_ref):
-        return jnp.minimum(step, live_ref[0] - 1)
+        return jnp.maximum(jnp.minimum(step, live_ref[0] - 1), 0)
 
     return pl.pallas_call(
         vectors_kernel,
@@ -245,7 +245,7 @@
     slots = first.shape[0]
 
     def last(step, live_ref):
-        return jnp.minimum(step, live_ref[0] - 1)
+        return jnp.maximum(jnp.minimum(step, live_ref[0] - 1), 0)
 
     return pl.pallas_call(
         functools.partial(form_kernel, min(256, rows)),
@@ -325,7 +325,7 @@
     vecs = vectors.shape[1]
 
     def last(step, live_ref):
-        return jnp.minimum(step, live_ref[0] - 1)
+        return jnp.maximum(jnp.minimum(step, live_ref[0] - 1), 0)
 
     def by_task(s, f, g, n):
         return (last(s, n), 0, 0)
@@ -370,11 +370,77 @@
     return lax.optimization_barrier(arrays)
 
 
-def place_in_row(index):
-    here = lax.axis_index("row")
-    apart = (index // 2 - here // 2) % 4
+def place_in_row(index, here):
+    apart = (index // 2 - here // 2 + 4) % 4
     order = jnp.where(apart == 0, 0, jnp.where(apart == 3, 1, jnp.where(apart == 1, 2, 3)))
-    return order + 4 * ((index - here) % 2)
+    return order + 4 * ((index + here) % 2)
+
+
+def assign_kernel(shape, here, table, first, second, place, live, load, ends, chosen):
+    devices, width, slots, cols = shape
+    me = here[0]
+
+    def each_task(body, init):
+        def of_device(device, state):
+            def of_slot(slot, inner):
+                return body(device, slot, table[device * width + slot], inner)
+
+            return lax.fori_loop(0, table[device * width + slots], of_slot, state)
+
+        return lax.fori_loop(0, devices, of_device, init)
+
+    def clear(device, state):
+        load[device] = 0
+        return state
+
+    lax.fori_loop(0, devices, clear, 0)
+
+    def place_first(device, slot, partner, state):
+        end = jnp.where(load[partner] <= load[device], partner, device)
+        load[end] = load[end] + 1
+        ends[device * slots + slot] = end
+        return state
+
+    each_task(place_first, 0)
+
+    def place_last(device, slot, partner, count):
+        end = ends[device * slots + slot]
+        other = device + partner - end
+        move = load[end] > load[other] + 1
+        load[end] = load[end] - jnp.where(move, 1, 0)
+        load[other] = load[other] + jnp.where(move, 1, 0)
+        final = jnp.where(move, other, end)
+        chosen[count] = device + partner - final
+        return count + jnp.where(final == me, 1, 0)
+
+    count = each_task(place_last, 0)
+    most = lax.fori_loop(0, devices, lambda i, top: jnp.maximum(top, load[i]), 0)
+    shared = most <= slots
+    live[0] = jnp.where(shared, count, table[me * width + slots])
+    for slot in range(slots):
+        listed = jnp.where(shared, chosen[slot], table[me * width + slot])
+        partner = jnp.where(slot < live[0], listed, 0)
+        first[slot] = lax.rem(partner, cols)
+        second[slot] = lax.div(partner, cols)
+        place[slot] = place_in_row(second[slot], lax.div(me, cols))
+
+
+def assign_tasks(self_index, table, devices, slots, cols):
+    width = table.shape[0] // devices
+    smem = pl.BlockSpec(memory_space=pltpu.SMEM)
+    lists = jax.ShapeDtypeStruct((slots,), jnp.int32)
+    return pl.pallas_call(
+        functools.partial(assign_kernel, (devices, width, slots, cols)),
+        in_specs=[smem, smem],
+        out_specs=[smem] * 4,
+        out_shape=[lists, lists, lists, jax.ShapeDtypeStruct((1,), jnp.int32)],
+        scratch_shapes=[
+            pltpu.SMEM((devices,), jnp.int32),
+            pltpu.SMEM((devices * slots,), jnp.int32),
+            pltpu.SMEM((4 * slots,), jnp.int32),
+        ],
+        name="assign_tasks",
+    )(self_index.reshape(1), table)
 
 
 def shards(points, feature_scale, tile_tasks, task_count, seed_ids):
@@ -387,11 +453,7 @@
     weighted = (points.astype(jnp.float32) * feature_scale[None, :]).astype(jnp.bfloat16)
     row_band = lax.all_gather(weighted, "col", axis=0)
     listed = tile_tasks.reshape(-1)
-    live = task_count.reshape(1)
-    used = jnp.where(jnp.arange(listed.shape[0]) < live, listed, 0)
-    first = used % col_devices
-    second_device = used // col_devices
-    second = place_in_row(second_device)
+    slots = listed.shape[0]
 
     def shift(array, by):
         return lax.ppermute(
@@ -403,6 +465,15 @@
     picked = jnp.where(
         inside[:, None], jnp.take(weighted, jnp.clip(local_seed, 0, rows - 1), axis=0), 0
     ).astype(jnp.bfloat16)
+    own_line = jnp.concatenate(
+        [listed, task_count.reshape(-1), jnp.zeros((slots - 1,), jnp.int32)]
+    )
+    lines = jnp.where(
+        (jnp.arange(all_devices) == self_index)[:, None], own_line[None, :], 0
+    ).astype(jnp.bfloat16)
+    lines = lines.reshape(-1, weighted.shape[1])
+    padding = jnp.zeros((-lines.shape[0] % 16, weighted.shape[1]), jnp.bfloat16)
+    picked = jnp.concatenate([picked, lines, padding], axis=0)
     seed_parts = spread_to(picked, "row")
     before = shift(weighted, 2)
     after = shift(weighted, -2)
@@ -412,7 +483,12 @@
     across_high = shift(after[half:], -2)
     seed_parts = spread_to(jnp.sum(seed_parts, axis=0), "col")
     across_low, across_high, seed_parts = together(across_low, across_high, seed_parts)
-    seeds = jnp.sum(seed_parts, axis=0)
+    seed_sum = jnp.sum(seed_parts, axis=0)
+    seeds = seed_sum[:vecs]
+    table = seed_sum[vecs : vecs + lines.shape[0]].astype(jnp.int32).reshape(-1)
+    first, second_device, second, live = assign_tasks(
+        self_index, table, all_devices, slots, col_devices
+    )
     across = jnp.concatenate([across_low, across_high], axis=0)
     mine = jnp.stack([weighted, before, after, across])
     other = lax.ppermute(mine, "row", [(i, i ^ 1) for i in range(row_devices)])
@@ -433,7 +509,7 @@
     later_grams = lax.all_gather(later_gram, ("row", "col"), axis=0)
 
     tiles, row_deg, col_deg = form_tiles(first, second, live, row_band, col_band)
-    row_places = place_in_row(jnp.arange(row_devices))
+    row_places = place_in_row(jnp.arange(row_devices), lax.axis_index("row"))
     col_deg = jnp.take(col_deg, row_places, axis=0)
     row_parts = exchange(row_deg, "col")
     col_parts = exchange(col_deg, "row")

time: 346 us -> 341 us (0.986); the launches traced: 340 us -> 339 us
  Pallas kernels: 46 us -> 93.2 us
  starting transfers between devices: 74.5 us -> 42.3 us
  blocking collectives: 80.4 us -> 65.1 us
  local copies, waits for them, and re-layouts: 24.2 us -> 14.4 us
  waiting for transfers between devices: 93.4 us -> 102 us
    all_to_all x6, starting transfers between devices: 59.6 us -> 27.2 us  [exchange(): return lax.all_to_all(copies, axis, 0, 0, tiled=True)]
    pallas_call x0 -> x1, Pallas kernels: none -> 14.8 us  [assign_tasks(): pl.pallas_call(functools.partial(assign_kernel, (devices, width, slots, c...]
    all_to_all x5, blocking collectives: 66.6 us -> 51.9 us  [exchange(): return lax.all_to_all(copies, axis, 0, 0, tiled=True)]
    pallas_call x4, Pallas kernels: 18.2 us -> 30.7 us  [apply_tiles(): pl.pallas_call(functools.partial(apply_kernel, contract), grid_spec=pltpu...]
    unnamed x30 -> x25, local copies, waits for them, and re-layouts: 16.2 us -> 4.28 us
    all_to_all x6, waiting for transfers between devices: 83.6 us -> 92.2 us  [exchange(): return lax.all_to_all(copies, axis, 0, 0, tiled=True)]
  transfers between devices with their start and end apart: 17 -> 17, of which waited for: 9 -> 8; matrix products, arithmetic and copies ran while one was open for 4% -> 5% of each run, Pallas kernels for 11% -> 24%
where the time goes in v3:
time: 341 us; the launch traced here: 339 us
  waiting for transfers between devices  102 us (30%)
  Pallas kernels  93.2 us (27%)
  blocking collectives  65.1 us (19%)
  starting transfers between devices  42.3 us (12%)
  local copies, waits for them, and re-layouts  14.4 us (4%)
  between operations  14.1 us (4%)
  other arithmetic  5.26 us (2%)
    all_to_all x6, waiting for transfers between devices, exchange(): return lax.all_to_all(copies, axis, 0, 0, tiled=True)  92.2 us
    all_to_all x5, blocking collectives, exchange(): return lax.all_to_all(copies, axis, 0, 0, tiled=True)  51.9 us
    pallas_call x4, Pallas kernels, apply_tiles(): pl.pallas_call(functools.partial(apply_kernel, contract), grid_spec=pltpu...  30.7 us
    all_to_all x6, starting transfers between devices, exchange(): return lax.all_to_all(copies, axis, 0, 0, tiled=True)  27.2 us
    pallas_call x1, Pallas kernels, assign_tasks(): pl.pallas_call(functools.partial(assign_kernel, (devices, width, slots, c...  14.8 us
    all_to_all x1, blocking collectives, spread_to(): return lax.all_to_all(copies, axis, 0, 0, tiled=True)  13.2 us
    pallas_call x1, Pallas kernels, form_tiles(): pl.pallas_call(functools.partial(form_kernel, min(256, rows)), grid_spec=...  9.05 us
    all_to_all x1, starting transfers between devices, spread_to(): return lax.all_to_all(copies, axis, 0, 0, tiled=True)  8.05 us
  transfers between devices with their start and end apart: 17, of which 8 were waited for; matrix products, arithmetic and copies ran while one was open for 5% of the time, Pallas kernels for 24%

profile of v3, /device:TPU:0, one launch (start us, length us, event | category | flops | bytes accessed | tf_op | source)
XLA Modules:
  0.0 339.1 jit_solution(17355218354989312435)
XLA Ops:
  15.3 13.2 %all_to_all.65 = bf16[8,80,256]{2,1,0:T(8,128)(2,1)S(1)} all-to-all(bf16[8,80,256]{2,1,0:T(8,128)(2,1)S(1)} %broadcast_in_dim.98), channel_id=1, replica_groups=mesh['row'=8,'col'=16] {'row'}, dimensions={0} | all-to-all | bytes 655360 | tf_op jit(solution)/shard_map/all_to_all | solution.py:362
  29.5 8.0 %all-to-all-start.1 = ((bf16[16,80,256]{2,1,0:T(8,128)(2,1)}), bf16[16,80,256]{2,1,0:T(8,128)(2,1)S(1)}, u32[]{:S(2)}, u32[]{:S(2)}) async-start(bf16[16,80,256]{2,1,0:T(8,128)(2,1)} %broadcast_in_dim.99), calls=%async_computation.1 | async-start | bytes 1310720 | tf_op jit(solution)/shard_map/all_to_all | solution.py:362
  40.9 5.6 %collective-permute-done.2 = bf16[512,256]{1,0:T(8,128)(2,1)S(1)} collective-permute-done((bf16[512,256]{1,0:T(8,128)(2,1)S(1)}, bf16[512,256]{1,0:T(8,128)(2,1)S(1)}, u32[]{:S(2)}, u32[]{:S(2)}) %collective-permute-start.2) | collective-permute-done | bytes 262176 | tf_op jit(solution)/shard_map/ppermute | solution.py:459
  76.5 7.7 %all-to-all-done.3.grams = f32[16,32,128]{2,1,0:T(8,128)S(1)} async-done(((f32[16,32,128]{2,1,0:T(8,128)}), f32[16,32,128]{2,1,0:T(8,128)S(1)}, u32[]{:S(2)}, u32[]{:S(2)}) %all-to-all-start.3) | async-done | bytes 262176 | tf_op jit(solution)/shard_map/all_to_all | solution.py:366
  84.9 5.3 %first_factor.1 = (f32[64,64]{1,0:T(8,128)}, f32[64,1024]{1,0:T(8,128)}, f32[32,128]{1,0:T(8,128)}) custom-call(f32[16,32,128]{2,1,0:T(8,128)} %copy-done.2, f32[64,1024]{1,0:T(8,128)} %get-tuple-element.47.start, bf16[1024,1024]{1,0:T(8,128)(2,1)} %get-tuple-element.48.diagonal, f32[1,1024]{1,0:T(1,128)} %get-tuple-element.49.own_degree), custom_call_target="tpu_custom_call" | custom-call | tf_op jit(solution)/shard_map/first_factor/pallas_call | solution.py:504
  90.9 14.8 %assign_tasks.1 = (s32[8]{0:T(128)}, s32[8]{0:T(128)}, s32[8]{0:T(128)}, s32[1]{0:T(128)}) custom-call(s32[1]{0:T(128)} %bitcast.6.here, s32[2048]{0:T(1024)} %bitcast.38), custom_call_target="tpu_custom_call" | custom-call | tf_op jit(solution)/shard_map/assign_tasks/pallas_call | solution.py:432
  105.7 9.0 %form_tiles.1 = (bf16[8,1024,1024]{2,1,0:T(8,128)(2,1)}, f32[16,8,128]{2,1,0:T(8,128)}, f32[8,8,128]{2,1,0:T(8,128)}) custom-call(s32[8]{0:T(128)} %get-tuple-element.51.first.source.target, s32[8]{0:T(128)} %get-tuple-element.52.second, s32[1]{0:T(128)} %get-tuple-element.53.live, bf16[16,1024,256]{2,1,0:T(8,128)(2,1)} %bitcast.28, ...), custom_call_target="tpu_custom_call" | custom-call | tf_op jit(solution)/shard_map/form_tiles/pallas_call | solution.py:250
  116.2 8.5 %all_to_all.66.col_parts = f32[8,8,128]{2,1,0:T(8,128)} all-to-all(f32[8,8,128]{2,1,0:T(8,128)S(1)} %broadcast_select_fusion), channel_id=1, replica_groups=mesh['row'=8,'col'=16] {'row'}, dimensions={0} | all-to-all | bytes 65536 | tf_op jit(solution)/shard_map/all_to_all | solution.py:366
  124.6 11.8 %all_to_all.67.row_parts = f32[16,8,128]{2,1,0:T(8,128)} all-to-all(f32[16,8,128]{2,1,0:T(8,128)} %get-tuple-element.55), channel_id=1, replica_groups=mesh['row'=8,'col'=16] {'col'}, dimensions={0} | all-to-all | bytes 131072 | tf_op jit(solution)/shard_map/all_to_all | solution.py:366
  141.7 7.2 %start_vectors.1 = (f32[8,64,1024]{2,1,0:T(8,128)}, f32[8,64,1024]{2,1,0:T(8,128)}) custom-call(s32[8]{0:T(128)} %get-tuple-element.51.first.source.target, s32[8]{0:T(128)} %get-tuple-element.52.second, s32[1]{0:T(128)} %get-tuple-element.53.live, bf16[16,1024,256]{2,1,0:T(8,128)(2,1)} %bitcast.29, ...), custom_call_target="tpu_custom_call" | custom-call | tf_op jit(solution)/shard_map/start_vectors/pallas_call | solution.py:194
  149.8 7.3 %apply_tiles.4 = bf16[8,64,1024]{2,1,0:T(8,128)(2,1)} custom-call(s32[8]{0:T(128)} %get-tuple-element.51.first.source.target, s32[8]{0:T(128)} %get-tuple-element.58.target.source, s32[1]{0:T(128)} %get-tuple-element.53.live, bf16[8,1024,1024]{2,1,0:T(8,128)(2,1)} %get-tuple-element.59.tile, f32[8,64,1024]{2,1,0:T(8,128)} %get-tuple-element.61.vectors, ...), custom_call_target="tpu_custom_call" | custom-call | tf_op jit(solution)/shard_map/apply_tiles/pallas_call | solution.py:344
  157.2 8.5 %all_to_all.68.rest_0_ = f32[8,8,128]{2,1,0:T(8,128)} all-to-all(f32[8,8,128]{2,1,0:T(8,128)S(1)} %slice.19), channel_id=1, replica_groups=mesh['row'=8,'col'=16] {'row'}, dimensions={0} | all-to-all | bytes 65536 | tf_op jit(solution)/shard_map/all_to_all | solution.py:366
  165.7 8.3 %apply_tiles.5 = bf16[16,64,1024]{2,1,0:T(8,128)(2,1)} custom-call(s32[8]{0:T(128)} %get-tuple-element.58.target.source, s32[8]{0:T(128)} %get-tuple-element.51.first.source.target, s32[1]{0:T(128)} %get-tuple-element.53.live, bf16[8,1024,1024]{2,1,0:T(8,128)(2,1)} %get-tuple-element.59.tile, f32[8,64,1024]{2,1,0:T(8,128)} %get-tuple-element.64.vectors, ...), custom_call_target="tpu_custom_call" | custom-call | tf_op jit(solution)/shard_map/apply_tiles/pallas_call | solution.py:344
  174.0 4.6 %all-to-all-start.8 = ((bf16[16,64,1024]{2,1,0:T(8,128)(2,1)}), bf16[16,64,1024]{2,1,0:T(8,128)(2,1)}, u32[]{:S(2)}, u32[]{:S(2)}) async-start(bf16[16,64,1024]{2,1,0:T(8,128)(2,1)} %apply_tiles.5), calls=%async_computation.8 | async-start | bytes 4194304 | tf_op jit(solution)/shard_map/all_to_all | solution.py:366
  178.7 4.4 %later_factor.1.factor = f32[64,64]{1,0:T(8,128)} custom-call(f32[128,32,128]{2,1,0:T(8,128)} %bitcast.33), custom_call_target="tpu_custom_call" | custom-call | tf_op jit(solution)/shard_map/later_factor/pallas_call | solution.py:539
  184.3 25.5 %all-to-all-done.8.first_parts = bf16[16,64,1024]{2,1,0:T(8,128)(2,1)} async-done(((bf16[16,64,1024]{2,1,0:T(8,128)(2,1)}), bf16[16,64,1024]{2,1,0:T(8,128)(2,1)}, u32[]{:S(2)}, u32[]{:S(2)}) %all-to-all-start.8) | async-done | bytes 2097184 | tf_op jit(solution)/shard_map/all_to_all | solution.py:366
  213.7 7.1 %all-to-all-start.9 = ((bf16[16,64,1024]{2,1,0:T(8,128)(2,1)}), bf16[16,64,1024]{2,1,0:T(8,128)(2,1)}, u32[]{:S(2)}, u32[]{:S(2)}) async-start(bf16[16,64,1024]{2,1,0:T(8,128)(2,1)} %get-tuple-element.68), calls=%async_computation.10 | async-start | bytes 4194304 | tf_op jit(solution)/shard_map/all_to_all | solution.py:366
  221.4 30.2 %all-to-all-done.9.vectors = bf16[16,64,1024]{2,1,0:T(8,128)(2,1)} async-done(((bf16[16,64,1024]{2,1,0:T(8,128)(2,1)}), bf16[16,64,1024]{2,1,0:T(8,128)(2,1)}, u32[]{:S(2)}, u32[]{:S(2)}) %all-to-all-start.9) | async-done | bytes 2097184 | tf_op jit(solution)/shard_map/all_to_all | solution.py:366
  251.6 7.0 %apply_tiles.6 = bf16[8,64,1024]{2,1,0:T(8,128)(2,1)} custom-call(s32[8]{0:T(128)} %get-tuple-element.51.first.source.target, s32[8]{0:T(128)} %get-tuple-element.58.target.source, s32[1]{0:T(128)} %get-tuple-element.53.live, bf16[8,1024,1024]{2,1,0:T(8,128)(2,1)} %get-tuple-element.59.tile, bf16[16,64,1024]{2,1,0:T(8,128)(2,1)} %all-to-all-done.9.vectors), custom_call_target="tpu_custom_call" | custom-call | tf_op jit(solution)/shard_map/apply_tiles/pallas_call | solution.py:344
  258.5 8.1 %apply_tiles.7 = bf16[16,64,1024]{2,1,0:T(8,128)(2,1)} custom-call(s32[8]{0:T(128)} %get-tuple-element.58.target.source, s32[8]{0:T(128)} %get-tuple-element.51.first.source.target, s32[1]{0:T(128)} %get-tuple-element.53.live, bf16[8,1024,1024]{2,1,0:T(8,128)(2,1)} %get-tuple-element.59.tile, bf16[8,64,1024]{2,1,0:T(8,128)(2,1)} %bitcast.34), custom_call_target="tpu_custom_call" | custom-call | tf_op jit(solution)/shard_map/apply_tiles/pallas_call | solution.py:344
  266.6 4.6 %all-to-all-start.10 = ((bf16[16,64,1024]{2,1,0:T(8,128)(2,1)}), bf16[16,64,1024]{2,1,0:T(8,128)(2,1)}, u32[]{:S(2)}, u32[]{:S(2)}) async-start(bf16[16,64,1024]{2,1,0:T(8,128)(2,1)} %apply_tiles.7), calls=%async_computation.11 | async-start | bytes 4194304 | tf_op jit(solution)/shard_map/all_to_all | solution.py:366
  272.4 26.4 %all-to-all-done.10.first_parts = bf16[16,64,1024]{2,1,0:T(8,128)(2,1)} async-done(((bf16[16,64,1024]{2,1,0:T(8,128)(2,1)}), bf16[16,64,1024]{2,1,0:T(8,128)(2,1)}, u32[]{:S(2)}, u32[]{:S(2)}) %all-to-all-start.10) | async-done | bytes 2097184 | tf_op jit(solution)/shard_map/all_to_all | solution.py:366
  301.8 10.1 %all_to_all.69.grams = f32[8,32,128]{2,1,0:T(8,128)} all-to-all(f32[8,32,128]{2,1,0:T(8,128)} %get-tuple-element.71), channel_id=1, replica_groups=mesh['row'=8,'col'=16] {'row'}, dimensions={0} | all-to-all | bytes 262144 | tf_op jit(solution)/shard_map/all_to_all | solution.py:366
  313.5 13.0 %all_to_all.70.grams = f32[16,32,128]{2,1,0:T(8,128)} all-to-all(f32[16,32,128]{2,1,0:T(8,128)} %relay.3), channel_id=1, replica_groups=mesh['row'=8,'col'=16] {'col'}, dimensions={0} | all-to-all | bytes 524288 | tf_op jit(solution)/shard_map/all_to_all | solution.py:366
  (99 shorter events, 68.7 us)
Async XLA Ops:
  6.5 5.6 %copy-start.9 = (s32[64]{0:T(128)S(1)}, s32[64]{0:T(128)}, u32[]{:S(2)}) copy-start(s32[64]{0:T(128)} %param.9) | copy-start | bytes 772
  6.5 8.3 %copy-start.10 = (s32[1,1,8]{2,1,0:T(1,128)S(1)}, s32[1,1,8]{2,1,0:T(1,128)}, u32[]{:S(2)}) copy-start(s32[1,1,8]{2,1,0:T(1,128)} %param.7) | copy-start | bytes 100
  6.5 99.2 %all-gather.7.cloned.1.call-start = ((), (), s32[]{:S(2)}) async-start(), calls=%async_computation.17 | async-start | bytes 8912896 | tf_op jit(solution)/shard_map/all_gather | solution.py:454
  8.8 19.7 %collective-permute-start = (bf16[1024,256]{1,0:T(8,128)(2,1)}, bf16[1024,256]{1,0:T(8,128)(2,1)S(1)}, u32[]{:S(2)}, u32[]{:S(2)}) collective-permute-start(bf16[1024,256]{1,0:T(8,128)(2,1)} %get-tuple-element.76.own), channel_id=1, source_target_pairs={{0,32},{16,48},{32,64},{48,80},{64,96},{80,112},{96,0},{112,16},{1... | collective-permute-start | bytes 1572872 | tf_op jit(solution)/shard_map/ppermute | solution.py:459
  10.4 18.1 %collective-permute-start.1 = (bf16[1024,256]{1,0:T(8,128)(2,1)}, bf16[1024,256]{1,0:T(8,128)(2,1)S(1)}, u32[]{:S(2)}, u32[]{:S(2)}) collective-permute-start(bf16[1024,256]{1,0:T(8,128)(2,1)} %get-tuple-element.76.own), channel_id=1, source_target_pairs={{0,96},{16,112},{32,0},{48,16},{64,32},{80,48},{96,64},{112,80},{1... | collective-permute-start | bytes 1572872 | tf_op jit(solution)/shard_map/ppermute | solution.py:459
  28.6 21.9 %copy-start.1 = (bf16[1024,256]{1,0:T(8,128)(2,1)S(1)}, bf16[1024,256]{1,0:T(8,128)(2,1)}, u32[]{:S(2)}) copy-start(bf16[1024,256]{1,0:T(8,128)(2,1)} %get-tuple-element.76.own) | copy-start | bytes 1572868
  29.5 21.0 %all-to-all-start.1 = ((bf16[16,80,256]{2,1,0:T(8,128)(2,1)}), bf16[16,80,256]{2,1,0:T(8,128)(2,1)S(1)}, u32[]{:S(2)}, u32[]{:S(2)}) async-start(bf16[16,80,256]{2,1,0:T(8,128)(2,1)} %broadcast_in_dim.99), calls=%async_computation.1 | async-start | bytes 1310720 | tf_op jit(solution)/shard_map/all_to_all | solution.py:362
  37.6 9.0 %collective-permute-start.2 = (bf16[512,256]{1,0:T(8,128)(2,1)S(1)}, bf16[512,256]{1,0:T(8,128)(2,1)S(1)}, u32[]{:S(2)}, u32[]{:S(2)}) collective-permute-start(bf16[512,256]{1,0:T(8,128)(2,1)S(1)} %slice.15), channel_id=1, source_target_pairs={{0,32},{16,48},{32,64},{48,80},{64,96},{80,112},{96,0},{112,16},{1... | collective-permute-start | bytes 786440 | tf_op jit(solution)/shard_map/ppermute | solution.py:459
  38.8 7.7 %collective-permute-start.3 = (bf16[512,256]{1,0:T(8,128)(2,1)S(1)}, bf16[512,256]{1,0:T(8,128)(2,1)S(1)}, u32[]{:S(2)}, u32[]{:S(2)}) collective-permute-start(bf16[512,256]{1,0:T(8,128)(2,1)S(1)} %slice.16), channel_id=1, source_target_pairs={{0,96},{16,112},{32,0},{48,16},{64,32},{80,48},{96,64},{112,80},{1... | collective-permute-start | bytes 786440 | tf_op jit(solution)/shard_map/ppermute | solution.py:459
  52.1 9.3 %collective-permute-start.4 = (bf16[4,1024,256]{2,1,0:T(8,128)(2,1)}, bf16[4,1024,256]{2,1,0:T(8,128)(2,1)}, u32[]{:S(2)}, u32[]{:S(2)}) collective-permute-start(bf16[4,1024,256]{2,1,0:T(8,128)(2,1)} %pad_maximum_fusion), channel_id=1, source_target_pairs={{0,16},{16,0},{32,48},{48,32},{64,80},{80,64},{96,112},{112,96},{1... | collective-permute-start | bytes 6291464 | tf_op jit(solution)/shard_map/ppermute | solution.py:494
  57.0 9.7 %all-to-all-start.2 = ((f32[8,32,128]{2,1,0:T(8,128)}), f32[8,32,128]{2,1,0:T(8,128)S(1)}, u32[]{:S(2)}, u32[]{:S(2)}) async-start(f32[8,32,128]{2,1,0:T(8,128)} %get-tuple-element.45), calls=%async_computation.2 | async-start | bytes 262144 | tf_op jit(solution)/shard_map/all_to_all | solution.py:366
  69.0 15.2 %all-to-all-start.3 = ((f32[16,32,128]{2,1,0:T(8,128)}), f32[16,32,128]{2,1,0:T(8,128)S(1)}, u32[]{:S(2)}, u32[]{:S(2)}) async-start(f32[16,32,128]{2,1,0:T(8,128)} %relay.2), calls=%async_computation.3 | async-start | bytes 524288 | tf_op jit(solution)/shard_map/all_to_all | solution.py:366
  72.9 105.8 %all-gather.9.cloned.1.call-start = ((), (), s32[]{:S(2)}) async-start(), calls=%async_computation.18 | async-start | bytes 2113536 | tf_op jit(solution)/shard_map/all_gather | solution.py:509
  137.9 11.3 %all-to-all-start.6 = ((f32[16,8,128]{2,1,0:T(8,128)}), f32[16,8,128]{2,1,0:T(8,128)S(1)}, u32[]{:S(2)}, u32[]{:S(2)}) async-start(f32[16,8,128]{2,1,0:T(8,128)} %get-tuple-element.62), calls=%async_computation.6 | async-start | bytes 131072 | tf_op jit(solution)/shard_map/all_to_all | solution.py:366
  141.5 68.4 %reduce-scatter.3.cloned.1.call-start = ((), (), s32[]{:S(2)}) async-start(), calls=%async_computation.15 | async-start | bytes 1179648 | tf_op jit(solution)/shard_map/reduce_scatter | solution.py:533
  149.8 7.3 %copy-start.7 = (f32[16,8,128]{2,1,0:T(8,128)S(1)}, f32[16,8,128]{2,1,0:T(8,128)}, u32[]{:S(2)}) copy-start(f32[16,8,128]{2,1,0:T(8,128)} %get-tuple-element.62) | copy-start | bytes 196612
  174.0 9.1 %copy-start.6 = (f32[64,1024]{1,0:T(8,128)S(1)}, f32[64,1024]{1,0:T(8,128)}, u32[]{:S(2)}) copy-start(f32[64,1024]{1,0:T(8,128)} %get-tuple-element.50) | copy-start | bytes 786436
  174.0 35.8 %all-to-all-start.8 = ((bf16[16,64,1024]{2,1,0:T(8,128)(2,1)}), bf16[16,64,1024]{2,1,0:T(8,128)(2,1)}, u32[]{:S(2)}, u32[]{:S(2)}) async-start(bf16[16,64,1024]{2,1,0:T(8,128)(2,1)} %apply_tiles.5), calls=%async_computation.8 | async-start | bytes 4194304 | tf_op jit(solution)/shard_map/all_to_all | solution.py:366
  178.6 4.5 %copy-start = (bf16[1024,1024]{1,0:T(8,128)(2,1)S(1)}, bf16[1024,1024]{1,0:T(8,128)(2,1)}, u32[]{:S(2)}) copy-start(bf16[1024,1024]{1,0:T(8,128)(2,1)} %get-tuple-element.48.diagonal) | copy-start | bytes 6291460
  213.7 37.9 %all-to-all-start.9 = ((bf16[16,64,1024]{2,1,0:T(8,128)(2,1)}), bf16[16,64,1024]{2,1,0:T(8,128)(2,1)}, u32[]{:S(2)}, u32[]{:S(2)}) async-start(bf16[16,64,1024]{2,1,0:T(8,128)(2,1)} %get-tuple-element.68), calls=%async_computation.10 | async-start | bytes 4194304 | tf_op jit(solution)/shard_map/all_to_all | solution.py:366
  220.7 37.8 %all-gather.11.cloned.1.call-start = ((), (), s32[]{:S(2)}) async-start(), calls=%async_computation.19 | async-start | bytes 1179648 | tf_op jit(solution)/shard_map/all_gather | solution.py:543
  221.3 77.5 %reduce-scatter.5.cloned.1.call-start = ((), (), s32[]{:S(2)}) async-start(), calls=%async_computation.16 | async-start | bytes 1179648 | tf_op jit(solution)/shard_map/reduce_scatter | solution.py:533
  266.6 4.6 %copy-start.3 = (bf16[64,1024]{1,0:T(8,128)(2,1)S(1)}, bf16[64,1024]{1,0:T(8,128)(2,1)}, u32[]{:S(2)}) copy-start(bf16[64,1024]{1,0:T(8,128)(2,1)} %get-tuple-element.67) | copy-start | bytes 393220
  266.6 32.2 %all-to-all-start.10 = ((bf16[16,64,1024]{2,1,0:T(8,128)(2,1)}), bf16[16,64,1024]{2,1,0:T(8,128)(2,1)}, u32[]{:S(2)}, u32[]{:S(2)}) async-start(bf16[16,64,1024]{2,1,0:T(8,128)(2,1)} %apply_tiles.7), calls=%async_computation.11 | async-start | bytes 4194304 | tf_op jit(solution)/shard_map/all_to_all | solution.py:366
  (4 other events, 6.4 us)
Sparse Core Ops, SparseCore 0:
  9.5 77.1 all-gather.6
  90.4 63.1 all-gather.8
  157.3 31.1 reduce-scatter.2
  223.0 22.3 all-gather.10
  258.7 26.4 reduce-scatter.4

commit v4 on v2

--- a/solution.py
+++ b/solution.py
@@ -10,7 +10,8 @@
 
 ITERS = 2
 LOG2E = math.log2(math.e)
-VMEM = 48 * 1024 * 1024
+VMEM = 60 * 1024 * 1024
+SMALL = 24 * 1024 * 1024
 HIGH = lax.Precision.HIGHEST
 RIDGE = 1e-6
 
@@ -91,11 +92,11 @@
     return jnp.dot(matrix, vectors, precision=HIGH, preferred_element_type=jnp.float32)
 
 
-def call(kernel, name, out_shape):
+def call(kernel, name, out_shape, grant=SMALL):
     return pl.pallas_call(
         kernel,
         out_shape=out_shape,
-        compiler_params=pltpu.CompilerParams(vmem_limit_bytes=VMEM),
+        compiler_params=pltpu.CompilerParams(vmem_limit_bytes=grant),
         name=name,
     )
 
@@ -138,9 +139,8 @@
     factor[...] = inverse_factor(jnp.sum(grams[...], axis=0), True)
 
 
-def degree_kernel(own_degree, row_parts, col_parts, roots, root):
-    total = jnp.sum(row_parts[...], axis=0) + jnp.sum(col_parts[...], axis=0)
-    value = lax.rsqrt(total + pack_row(own_degree[...]))
+def degree_kernel(own_degree, parts, roots, root):
+    value = lax.rsqrt(jnp.sum(parts[...], axis=0) + pack_row(own_degree[...]))
     roots[...] = jnp.broadcast_to(value[None], roots.shape)
     root[...] = unpack_row(value)
 
@@ -169,7 +169,7 @@
     inverse = inverse_factor(jnp.sum(grams[...], axis=0), False)
     scaled = transform(inverse, subspace[...]) * math.sqrt(points_all)
     mean = jnp.mean(scaled * scaled, axis=0, keepdims=True)
-    embedding[...] = (scaled * lax.rsqrt(mean + 1e-06)).T
+    embedding[...] = scaled * lax.rsqrt(mean + 1e-06)
 
 
 def relay_kernel(grams, copies):
@@ -189,7 +189,7 @@
     vecs = seeds.shape[0]
 
     def last(step, live_ref):
-        return jnp.minimum(step, live_ref[0] - 1)
+        return jnp.maximum(jnp.minimum(step, live_ref[0] - 1), 0)
 
     return pl.pallas_call(
         vectors_kernel,
@@ -212,13 +212,12 @@
     )(first, second, live, row_band, col_band, seeds, factor)
 
 
-def form_kernel(chunk, first, second, live, left, right, tile, row_deg, col_deg):
+def form_kernel(chunk, first, second, owners, live, left, right, tile, degrees):
     step = pl.program_id(0)
 
     @pl.when(step == 0)
     def clear():
-        row_deg[...] = jnp.zeros_like(row_deg)
-        col_deg[...] = jnp.zeros_like(col_deg)
+        degrees[...] = jnp.zeros_like(degrees)
 
     @pl.when(step < live[0])
     def work():
@@ -232,44 +231,41 @@
             tile[0, start : start + chunk, :] = value.astype(jnp.bfloat16)
             col_total = col_total + jnp.sum(value, axis=0, keepdims=True)
             row_totals.append(lane_sums(value))
-        row_slot = first[step]
-        col_slot = second[step]
+        left_owner = owners[2 * step]
+        right_owner = owners[2 * step + 1]
         row_total = jnp.concatenate(row_totals, axis=1)
-        row_deg[row_slot] = row_deg[row_slot] + pack_row(row_total)
-        col_deg[col_slot] = col_deg[col_slot] + pack_row(col_total)
-
-
-def form_tiles(first, second, live, row_band, col_band):
+        degrees[left_owner] = degrees[left_owner] + pack_row(row_total)
+        degrees[right_owner] = degrees[right_owner] + pack_row(col_total)
+
+
+def form_tiles(first, second, owners, live, row_band, col_band):
     col_devices, rows, depth = row_band.shape
-    row_devices = col_band.shape[0]
+    all_devices = col_devices * col_band.shape[0]
     slots = first.shape[0]
 
     def last(step, live_ref):
-        return jnp.minimum(step, live_ref[0] - 1)
+        return jnp.maximum(jnp.minimum(step, live_ref[0] - 1), 0)
 
     return pl.pallas_call(
         functools.partial(form_kernel, min(256, rows)),
         grid_spec=pltpu.PrefetchScalarGridSpec(
-            num_scalar_prefetch=3,
+            num_scalar_prefetch=4,
             grid=(slots,),
             in_specs=[
-                pl.BlockSpec((1, rows, depth), lambda s, f, g, n: (f[last(s, n)], 0, 0)),
-                pl.BlockSpec((1, rows, depth), lambda s, f, g, n: (g[last(s, n)], 0, 0)),
+                pl.BlockSpec((1, rows, depth), lambda s, f, g, o, n: (f[last(s, n)], 0, 0)),
+                pl.BlockSpec((1, rows, depth), lambda s, f, g, o, n: (g[last(s, n)], 0, 0)),
             ],
             out_specs=[
-                pl.BlockSpec((1, rows, rows), lambda s, f, g, n: (last(s, n), 0, 0)),
-                pl.BlockSpec((col_devices, rows // 128, 128), lambda s, f, g, n: (0, 0, 0)),
-                pl.BlockSpec((row_devices, rows // 128, 128), lambda s, f, g, n: (0, 0, 0)),
+                pl.BlockSpec((1, rows, rows), lambda s, f, g, o, n: (last(s, n), 0, 0)),
+                pl.BlockSpec(
+                    (all_devices, rows // 128, 128), lambda s, f, g, o, n: (0, 0, 0)
+                ),
             ],
         ),
-        out_shape=[
-            bf16(slots, rows, rows),
-            f32(col_devices, rows // 128, 128),
-            f32(row_devices, rows // 128, 128),
-        ],
+        out_shape=[bf16(slots, rows, rows), f32(all_devices, rows // 128, 128)],
         compiler_params=pltpu.CompilerParams(vmem_limit_bytes=VMEM),
         name="form_tiles",
-    )(first, second, live, row_band, col_band)
+    )(first, second, owners, live, row_band, col_band)
 
 
 def diagonal_kernel(chunk, own, tile, degree):
@@ -292,7 +288,7 @@
             jax.ShapeDtypeStruct((rows, rows), jnp.bfloat16),
             jax.ShapeDtypeStruct((1, rows), jnp.float32),
         ],
-        compiler_params=pltpu.CompilerParams(vmem_limit_bytes=VMEM),
+        compiler_params=pltpu.CompilerParams(vmem_limit_bytes=SMALL),
         name="form_diagonal",
     )(own)
 
@@ -325,7 +321,7 @@
     vecs = vectors.shape[1]
 
     def last(step, live_ref):
-        return jnp.minimum(step, live_ref[0] - 1)
+        return jnp.maximum(jnp.minimum(step, live_ref[0] - 1), 0)
 
     def by_task(s, f, g, n):
         return (last(s, n), 0, 0)
@@ -370,11 +366,78 @@
     return lax.optimization_barrier(arrays)
 
 
-def place_in_row(index):
-    here = lax.axis_index("row")
-    apart = (index // 2 - here // 2) % 4
+def place_in_row(index, here):
+    apart = (index // 2 - here // 2 + 4) % 4
     order = jnp.where(apart == 0, 0, jnp.where(apart == 3, 1, jnp.where(apart == 1, 2, 3)))
-    return order + 4 * ((index - here) % 2)
+    return order + 4 * ((index + here) % 2)
+
+
+def assign_kernel(slots, cols, here, table, first, second, place, owners, live):
+    devices = table.shape[1]
+    me = here[0]
+    filler = jnp.zeros((devices - table.shape[0], devices), jnp.float32)
+    by_device = jnp.concatenate([table[...], filler], axis=0).T
+    device = lax.broadcasted_iota(jnp.int32, (devices, devices), 0)
+    lane = lax.broadcasted_iota(jnp.int32, (devices, devices), 1)
+    same = jnp.where(device == lane, 1.0, 0.0)
+    count = by_device[:, slots : slots + 1]
+    load = jnp.zeros((1, devices), jnp.float32)
+    moves = []
+    taken = []
+    listed = []
+    for slot in range(slots):
+        partner = by_device[:, slot : slot + 1]
+        is_listed = jnp.where(count > slot, 1.0, 0.0)
+        picks = jnp.where(lane.astype(jnp.float32) == partner, 1.0, 0.0)
+        move = (picks - same) * is_listed
+        apart = jnp.sum(move * load, axis=1, keepdims=True)
+        take = jnp.where(apart <= 0, is_listed, 0.0)
+        load = load + jnp.sum(same * is_listed + move * take, axis=0, keepdims=True)
+        moves.append(move)
+        taken.append(take)
+        listed.append(is_listed)
+    for slot in range(slots):
+        apart = jnp.sum(moves[slot] * load, axis=1, keepdims=True)
+        give = jnp.where(apart < -1, listed[slot] * (1.0 - taken[slot]), 0.0)
+        back = jnp.where(apart > 1, taken[slot], 0.0)
+        load = load + jnp.sum(moves[slot] * (give - back), axis=0, keepdims=True)
+        taken[slot] = taken[slot] + give - back
+    shared = jnp.where(jnp.max(load) <= slots, 1.0, 0.0)
+    code = jnp.zeros((devices, devices), jnp.float32)
+    number = device.astype(jnp.float32)
+    for slot in range(slots):
+        partner = by_device[:, slot : slot + 1]
+        take = taken[slot] * shared
+        kept = jnp.where(device == me, listed[slot] - take, 0.0)
+        come = jnp.where(partner == me.astype(jnp.float32), take, 0.0)
+        other = kept * partner + come * number
+        cell = (kept + come) * (number * slots + (slot + 1)) * devices + other
+        code = jnp.where(lane == slot, cell, code)
+    live[0] = jnp.sum(jnp.where(code > 0, 1.0, 0.0)).astype(jnp.int32)
+    for slot in range(slots):
+        top = jnp.max(code)
+        partner = lax.rem(top.astype(jnp.int32), devices)
+        code = jnp.where(code == top, 0.0, code)
+        first_slot = lax.rem(partner, cols)
+        second_slot = lax.div(partner, cols)
+        first[slot] = first_slot
+        second[slot] = second_slot
+        place[slot] = place_in_row(second_slot, lax.div(me, cols))
+        owners[2 * slot] = lax.div(me, cols) * cols + first_slot
+        owners[2 * slot + 1] = second_slot * cols + lax.rem(me, cols)
+
+
+def assign_tasks(self_index, table, slots, cols):
+    smem = pl.BlockSpec(memory_space=pltpu.SMEM)
+    sizes = (slots, slots, slots, 2 * slots, 1)
+    return pl.pallas_call(
+        functools.partial(assign_kernel, slots, cols),
+        in_specs=[smem, pl.BlockSpec(memory_space=pltpu.VMEM)],
+        out_specs=[smem] * len(sizes),
+        out_shape=[jax.ShapeDtypeStruct((size,), jnp.int32) for size in sizes],
+        compiler_params=pltpu.CompilerParams(vmem_limit_bytes=SMALL),
+        name="assign_tasks",
+    )(self_index.reshape(1), table)
 
 
 def shards(points, feature_scale, tile_tasks, task_count, seed_ids):
@@ -387,11 +450,7 @@
     weighted = (points.astype(jnp.float32) * feature_scale[None, :]).astype(jnp.bfloat16)
     row_band = lax.all_gather(weighted, "col", axis=0)
     listed = tile_tasks.reshape(-1)
-    live = task_count.reshape(1)
-    used = jnp.where(jnp.arange(listed.shape[0]) < live, listed, 0)
-    first = used % col_devices
-    second_device = used // col_devices
-    second = place_in_row(second_device)
+    slots = listed.shape[0]
 
     def shift(array, by):
         return lax.ppermute(
@@ -403,16 +462,25 @@
     picked = jnp.where(
         inside[:, None], jnp.take(weighted, jnp.clip(local_seed, 0, rows - 1), axis=0), 0
     ).astype(jnp.bfloat16)
+    own_line = jnp.concatenate(
+        [listed, task_count.reshape(-1), jnp.zeros((slots - 1,), jnp.int32)]
+    )
+    lines = jnp.where(
+        (jnp.arange(weighted.shape[1]) == self_index)[None, :], own_line[:, None], 0
+    ).astype(jnp.bfloat16)
+    picked = jnp.concatenate([picked, lines], axis=0)
     seed_parts = spread_to(picked, "row")
-    before = shift(weighted, 2)
-    after = shift(weighted, -2)
-    before, after, seed_parts = together(before, after, seed_parts)
+    sent, seed_parts = together(weighted, seed_parts)
+    before = shift(sent, 2)
+    after = shift(sent, -2)
     half = rows // 2
     across_low = shift(before[:half], 2)
     across_high = shift(after[half:], -2)
     seed_parts = spread_to(jnp.sum(seed_parts, axis=0), "col")
-    across_low, across_high, seed_parts = together(across_low, across_high, seed_parts)
-    seeds = jnp.sum(seed_parts, axis=0)
+    seed_sum = jnp.sum(seed_parts, axis=0)
+    seeds = seed_sum[:vecs]
+    table = seed_sum[vecs:, :all_devices].astype(jnp.float32)
+    assigned = assign_tasks(self_index, table, slots, col_devices)
     across = jnp.concatenate([across_low, across_high], axis=0)
     mine = jnp.stack([weighted, before, after, across])
     other = lax.ppermute(mine, "row", [(i, i ^ 1) for i in range(row_devices)])
@@ -421,9 +489,10 @@
         start_kernel, "start", [f32(vecs, rows), f32(row_devices, vecs // 2, 2 * vecs)]
     )(seeds, weighted)
     grams = exchange(grams, "row")
-    col_band, grams = together(jnp.concatenate([mine, other], axis=0), grams)
+    grams, first, second_device, second, owners, live = together(grams, *assigned)
     grams = call(relay_kernel, "relay", f32(col_devices, vecs // 2, 2 * vecs))(grams)
     grams = exchange(grams, "col")
+    col_band, grams = together(jnp.concatenate([mine, other], axis=0), grams)
     diagonal, own_degree = form_diagonal(weighted)
     factor, subspace, later_gram = call(
         first_factor_kernel,
@@ -432,14 +501,10 @@
     )(grams, start, diagonal, own_degree)
     later_grams = lax.all_gather(later_gram, ("row", "col"), axis=0)
 
-    tiles, row_deg, col_deg = form_tiles(first, second, live, row_band, col_band)
-    row_places = place_in_row(jnp.arange(row_devices))
-    col_deg = jnp.take(col_deg, row_places, axis=0)
-    row_parts = exchange(row_deg, "col")
-    col_parts = exchange(col_deg, "row")
+    tiles, degrees = form_tiles(first, second, owners, live, row_band, col_band)
     roots, inv_root = call(
         degree_kernel, "degree", [f32(col_devices, rows // 128, 128), f32(1, rows)]
-    )(own_degree, row_parts, col_parts)
+    )(own_degree, exchange(degrees, ("row", "col")))
     from_first, from_second = start_vectors(
         first, second, live, row_band, col_band, seeds, factor
     )
@@ -462,7 +527,7 @@
         if iteration + 1 < ITERS:
             later_factor = call(later_factor_kernel, "later_factor", f32(vecs, vecs))(later_grams)
             copies, spread = call(
-                between_kernel, "between", [bf16(col_devices, vecs, rows), bf16(vecs, rows)]
+                between_kernel, "between", [bf16(col_devices, vecs, rows), bf16(vecs, rows)], VMEM
             )(own_part, first_parts, second_part, inv_root, later_factor)
             from_second = lax.all_gather(spread, "row", axis=0)
             from_first = exchange(copies, "col")
@@ -474,8 +539,8 @@
     grams = call(relay_kernel, "relay", f32(col_devices, vecs // 2, 2 * vecs))(grams)
     grams = exchange(grams, "col")
     return call(
-        functools.partial(final_kernel, all_devices * rows), "final", f32(rows, vecs)
-    )(grams, subspace)
+        functools.partial(final_kernel, all_devices * rows), "final", f32(vecs, rows)
+    )(grams, subspace).T
 
 
 def solution(mesh):

time: 346 us -> 338 us (0.977)
  starting transfers between devices: 74.5 us -> 51.8 us
  waiting for transfers between devices: 93.4 us -> 112 us
  Pallas kernels: 46 us -> 61.4 us
  local copies, waits for them, and re-layouts: 24.2 us -> 14.6 us
  blocking collectives: 80.4 us -> 71.8 us
    all_to_all x6, starting transfers between devices: 59.6 us -> 39.1 us  [exchange(): return lax.all_to_all(copies, axis, 0, 0, tiled=True)]
    ppermute x4, waiting for transfers between devices: 5.29 us -> 19.9 us  [shift(): lax.ppermute(array, 'row', [(i, (i + by) % row_devices) for i in range(ro...]
    all_to_all x1, waiting for transfers between devices: 2.41 us -> 14.4 us  [spread_to(): return lax.all_to_all(copies, axis, 0, 0, tiled=True)]
    unnamed x30 -> x38, local copies, waits for them, and re-layouts: 16.2 us -> 8.02 us
    all_to_all x5 -> x4, blocking collectives: 66.6 us -> 59.4 us  [exchange(): return lax.all_to_all(copies, axis, 0, 0, tiled=True)]
    all_to_all x6, waiting for transfers between devices: 83.6 us -> 77.3 us  [exchange(): return lax.all_to_all(copies, axis, 0, 0, tiled=True)]
    pallas_call x4, Pallas kernels: 18.2 us -> 24.1 us  [apply_tiles(): pl.pallas_call(functools.partial(apply_kernel, contract), grid_spec=pltpu...]
    pallas_call x1 -> x2, Pallas kernels: 2.26 us -> 8.16 us  [the longest x1 5.35 us: assign_tasks(): pl.pallas_call(functools.partial(assign_kernel, slots, cols), in_specs=[s...]
  transfers between devices with their start and end apart: 17 -> 17, of which waited for: 9 -> 9; matrix products, arithmetic and copies ran while one was open for 4% -> 5% of each run, Pallas kernels for 11% -> 16%
where the time goes in v4:
time: 338 us; the launch traced here: 335 us
  waiting for transfers between devices  112 us (33%)
  blocking collectives  71.8 us (21%)
  Pallas kernels  61.4 us (18%)
  starting transfers between devices  51.8 us (15%)
  local copies, waits for them, and re-layouts  14.6 us (4%)
  between operations  14.1 us (4%)
  other arithmetic  7.1 us (2%)
    all_to_all x6, waiting for transfers between devices, exchange(): return lax.all_to_all(copies, axis, 0, 0, tiled=True)  77.3 us
    all_to_all x4, blocking collectives, exchange(): return lax.all_to_all(copies, axis, 0, 0, tiled=True)  59.4 us
    all_to_all x6, starting transfers between devices, exchange(): return lax.all_to_all(copies, axis, 0, 0, tiled=True)  39.1 us
    pallas_call x4, Pallas kernels, apply_tiles(): pl.pallas_call(functools.partial(apply_kernel, contract), grid_spec=pltpu...  24.1 us
    ppermute x4, waiting for transfers between devices, shift(): lax.ppermute(array, 'row', [(i, (i + by) % row_devices) for i in range(ro...  19.9 us
    all_to_all x1, waiting for transfers between devices, spread_to(): return lax.all_to_all(copies, axis, 0, 0, tiled=True)  14.4 us
    all_to_all x1, blocking collectives, spread_to(): return lax.all_to_all(copies, axis, 0, 0, tiled=True)  12.4 us
    unnamed x38, local copies, waits for them, and re-layouts  8.02 us
  transfers between devices with their start and end apart: 17, of which 9 were waited for; matrix products, arithmetic and copies ran while one was open for 5% of the time, Pallas kernels for 16%

profile of v4, /device:TPU:0, one launch (start us, length us, event | category | flops | bytes accessed | tf_op | source)
XLA Modules:
  0.0 334.8 jit_solution(6948692724578213275)
XLA Ops:
  11.6 12.4 %all_to_all.60 = bf16[8,80,256]{2,1,0:T(8,128)(2,1)S(1)} all-to-all(bf16[8,80,256]{2,1,0:T(8,128)(2,1)S(1)} %broadcast_in_dim.68), channel_id=1, replica_groups=mesh['row'=8,'col'=16] {'row'}, dimensions={0} | all-to-all | bytes 655360 | tf_op jit(solution)/shard_map/all_to_all | solution.py:358
  26.0 11.8 %collective-permute-done.1 = bf16[1024,256]{1,0:T(8,128)(2,1)S(1)} collective-permute-done((bf16[1024,256]{1,0:T(8,128)(2,1)}, bf16[1024,256]{1,0:T(8,128)(2,1)S(1)}, u32[]{:S(2)}, u32[]{:S(2)}) %collective-permute-start.1) | collective-permute-done | bytes 524320 | tf_op jit(solution)/shard_map/ppermute | solution.py:456
  40.4 4.7 %collective-permute-done.3 = bf16[512,256]{1,0:T(8,128)(2,1)S(1)} collective-permute-done((bf16[512,256]{1,0:T(8,128)(2,1)S(1)}, bf16[512,256]{1,0:T(8,128)(2,1)S(1)}, u32[]{:S(2)}, u32[]{:S(2)}) %collective-permute-start.3) | collective-permute-done | bytes 262176 | tf_op jit(solution)/shard_map/ppermute | solution.py:456
  51.1 8.0 %all-to-all-start.1 = ((bf16[16,80,256]{2,1,0:T(8,128)(2,1)}), bf16[16,80,256]{2,1,0:T(8,128)(2,1)}, u32[]{:S(2)}, u32[]{:S(2)}) async-start(bf16[16,80,256]{2,1,0:T(8,128)(2,1)} %broadcast_in_dim.69), calls=%async_computation.1 | async-start | bytes 1310720 | tf_op jit(solution)/shard_map/all_to_all | solution.py:358
  63.1 14.4 %all-to-all-done.1 = bf16[16,80,256]{2,1,0:T(8,128)(2,1)} async-done(((bf16[16,80,256]{2,1,0:T(8,128)(2,1)}), bf16[16,80,256]{2,1,0:T(8,128)(2,1)}, u32[]{:S(2)}, u32[]{:S(2)}) %all-to-all-start.1) | async-done | bytes 655392 | tf_op jit(solution)/shard_map/all_to_all | solution.py:358
  83.6 5.3 %assign_tasks.1 = (s32[8]{0:T(128)S(1)}, s32[8]{0:T(128)S(1)}, s32[8]{0:T(128)S(1)}, s32[16]{0:T(128)S(1)}, s32[1]{0:T(128)}) custom-call(s32[1]{0:T(128)} %bitcast.6.here, f32[16,128]{1,0:T(8,128)S(1)} %slice_convert_fusion.table), custom_call_target="tpu_custom_call" | custom-call | tf_op jit(solution)/shard_map/assign_tasks/pallas_call | solution.py:433
  91.8 6.2 %all-to-all-start.3 = ((f32[16,32,128]{2,1,0:T(8,128)}), f32[16,32,128]{2,1,0:T(8,128)S(1)}, u32[]{:S(2)}, u32[]{:S(2)}) async-start(f32[16,32,128]{2,1,0:T(8,128)} %relay.2), calls=%async_computation.3 | async-start | bytes 524288 | tf_op jit(solution)/shard_map/all_to_all | solution.py:362
  103.0 4.1 %all-to-all-done.3.grams = f32[16,32,128]{2,1,0:T(8,128)S(1)} async-done(((f32[16,32,128]{2,1,0:T(8,128)}), f32[16,32,128]{2,1,0:T(8,128)S(1)}, u32[]{:S(2)}, u32[]{:S(2)}) %all-to-all-start.3) | async-done | bytes 262176 | tf_op jit(solution)/shard_map/all_to_all | solution.py:362
  110.7 7.3 %form_tiles.1 = (bf16[8,1024,1024]{2,1,0:T(8,128)(2,1)}, f32[128,8,128]{2,1,0:T(8,128)}) custom-call(s32[8]{0:T(128)} %copy-done.8, s32[8]{0:T(128)} %copy-done.10, s32[16]{0:T(128)} %copy-done.11, s32[1]{0:T(128)} %get-tuple-element.58.live, bf16[16,1024,256]{2,1,0:T(8,128)(2,1)} %bitcast.28, bf16[8,1024,256]{2,1,0:T(8,128)(2,1)} %constant_dynamic-update-slice_fusion.right), custom_call_target="tpu_custom_call" | custom-call | tf_op jit(solution)/shard_map/form_tiles/pallas_call | solution.py:249
  118.0 22.9 %all_to_all.61.parts = f32[128,8,128]{2,1,0:T(8,128)S(1)} all-to-all(f32[128,8,128]{2,1,0:T(8,128)} %get-tuple-element.60), channel_id=1, replica_groups=mesh['row'=8,'col'=16] {'row','col'}, dimensions={0} | all-to-all | bytes 1048576 | tf_op jit(solution)/shard_map/all_to_all | solution.py:362
  145.2 5.9 %start_vectors.1 = (f32[8,64,1024]{2,1,0:T(8,128)}, f32[8,64,1024]{2,1,0:T(8,128)}) custom-call(s32[8]{0:T(128)} %copy-done.8, s32[8]{0:T(128)} %copy-done.10, s32[1]{0:T(128)} %get-tuple-element.58.live, bf16[16,1024,256]{2,1,0:T(8,128)(2,1)} %bitcast.29, bf16[8,1024,256]{2,1,0:T(8,128)(2,1)} %constant_dynamic-update-slice_fusion.right, ...), custom_call_target="tpu_custom_call" | custom-call | tf_op jit(solution)/shard_map/start_vectors/pallas_call | solution.py:194
  153.3 5.6 %apply_tiles.4 = bf16[8,64,1024]{2,1,0:T(8,128)(2,1)} custom-call(s32[8]{0:T(128)} %copy-done.8, s32[8]{0:T(128)} %copy-done.9, s32[1]{0:T(128)} %get-tuple-element.58.live, bf16[8,1024,1024]{2,1,0:T(8,128)(2,1)} %get-tuple-element.63.tile, f32[8,64,1024]{2,1,0:T(8,128)} %get-tuple-element.65.vectors, f32[16,8,128]{2,1,0:T(8,128)} %copy-done.15), custom_call_target="tpu_custom_call" | custom-call | tf_op jit(solution)/shard_map/apply_tiles/pallas_call | solution.py:340
  159.7 9.4 %all_to_all.62.rest_0_ = f32[8,8,128]{2,1,0:T(8,128)} all-to-all(f32[8,8,128]{2,1,0:T(8,128)S(1)} %slice.19), channel_id=1, replica_groups=mesh['row'=8,'col'=16] {'row'}, dimensions={0} | all-to-all | bytes 65536 | tf_op jit(solution)/shard_map/all_to_all | solution.py:362
  169.1 6.7 %apply_tiles.5 = bf16[16,64,1024]{2,1,0:T(8,128)(2,1)} custom-call(s32[8]{0:T(128)} %copy-done.9, s32[8]{0:T(128)} %copy-done.8, s32[1]{0:T(128)} %get-tuple-element.58.live, bf16[8,1024,1024]{2,1,0:T(8,128)(2,1)} %get-tuple-element.63.tile, f32[8,64,1024]{2,1,0:T(8,128)} %get-tuple-element.68.vectors, f32[8,8,128]{2,1,0:T(8,128)} %all_to_all.62.rest_0_), custom_call_target="tpu_custom_call" | custom-call | tf_op jit(solution)/shard_map/apply_tiles/pallas_call | solution.py:340
  175.8 11.9 %all-to-all-start.7 = ((bf16[16,64,1024]{2,1,0:T(8,128)(2,1)}), bf16[16,64,1024]{2,1,0:T(8,128)(2,1)}, u32[]{:S(2)}, u32[]{:S(2)}) async-start(bf16[16,64,1024]{2,1,0:T(8,128)(2,1)} %apply_tiles.5), calls=%async_computation.7 | async-start | bytes 4194304 | tf_op jit(solution)/shard_map/all_to_all | solution.py:362
  192.6 22.8 %all-to-all-done.7.first_parts = bf16[16,64,1024]{2,1,0:T(8,128)(2,1)} async-done(((bf16[16,64,1024]{2,1,0:T(8,128)(2,1)}), bf16[16,64,1024]{2,1,0:T(8,128)(2,1)}, u32[]{:S(2)}, u32[]{:S(2)}) %all-to-all-start.7) | async-done | bytes 2097184 | tf_op jit(solution)/shard_map/all_to_all | solution.py:362
  219.2 4.5 %all-to-all-start.8 = ((bf16[16,64,1024]{2,1,0:T(8,128)(2,1)}), bf16[16,64,1024]{2,1,0:T(8,128)(2,1)}, u32[]{:S(2)}, u32[]{:S(2)}) async-start(bf16[16,64,1024]{2,1,0:T(8,128)(2,1)} %get-tuple-element.72), calls=%async_computation.9 | async-start | bytes 4194304 | tf_op jit(solution)/shard_map/all_to_all | solution.py:362
  224.4 26.7 %all-to-all-done.8.vectors = bf16[16,64,1024]{2,1,0:T(8,128)(2,1)} async-done(((bf16[16,64,1024]{2,1,0:T(8,128)(2,1)}), bf16[16,64,1024]{2,1,0:T(8,128)(2,1)}, u32[]{:S(2)}, u32[]{:S(2)}) %all-to-all-start.8) | async-done | bytes 2097184 | tf_op jit(solution)/shard_map/all_to_all | solution.py:362
  251.1 5.4 %apply_tiles.6 = bf16[8,64,1024]{2,1,0:T(8,128)(2,1)} custom-call(s32[8]{0:T(128)} %copy-done.8, s32[8]{0:T(128)} %copy-done.9, s32[1]{0:T(128)} %get-tuple-element.58.live, bf16[8,1024,1024]{2,1,0:T(8,128)(2,1)} %get-tuple-element.63.tile, bf16[16,64,1024]{2,1,0:T(8,128)(2,1)} %all-to-all-done.8.vectors), custom_call_target="tpu_custom_call" | custom-call | tf_op jit(solution)/shard_map/apply_tiles/pallas_call | solution.py:340
  256.5 6.5 %apply_tiles.7 = bf16[16,64,1024]{2,1,0:T(8,128)(2,1)} custom-call(s32[8]{0:T(128)} %copy-done.9, s32[8]{0:T(128)} %copy-done.8, s32[1]{0:T(128)} %get-tuple-element.58.live, bf16[8,1024,1024]{2,1,0:T(8,128)(2,1)} %get-tuple-element.63.tile, bf16[8,64,1024]{2,1,0:T(8,128)(2,1)} %bitcast.32), custom_call_target="tpu_custom_call" | custom-call | tf_op jit(solution)/shard_map/apply_tiles/pallas_call | solution.py:340
  263.0 9.6 %all-to-all-start.9 = ((bf16[16,64,1024]{2,1,0:T(8,128)(2,1)}), bf16[16,64,1024]{2,1,0:T(8,128)(2,1)}, u32[]{:S(2)}, u32[]{:S(2)}) async-start(bf16[16,64,1024]{2,1,0:T(8,128)(2,1)} %apply_tiles.7), calls=%async_computation.10 | async-start | bytes 4194304 | tf_op jit(solution)/shard_map/all_to_all | solution.py:362
  273.1 22.0 %all-to-all-done.9.first_parts = bf16[16,64,1024]{2,1,0:T(8,128)(2,1)} async-done(((bf16[16,64,1024]{2,1,0:T(8,128)(2,1)}), bf16[16,64,1024]{2,1,0:T(8,128)(2,1)}, u32[]{:S(2)}, u32[]{:S(2)}) %all-to-all-start.9) | async-done | bytes 2097184 | tf_op jit(solution)/shard_map/all_to_all | solution.py:362
  298.3 14.9 %all_to_all.63.grams = f32[8,32,128]{2,1,0:T(8,128)S(1)} all-to-all(f32[8,32,128]{2,1,0:T(8,128)S(1)} %get-tuple-element.75), channel_id=1, replica_groups=mesh['row'=8,'col'=16] {'row'}, dimensions={0} | all-to-all | bytes 262144 | tf_op jit(solution)/shard_map/all_to_all | solution.py:362
  313.2 12.3 %all_to_all.64.grams = f32[16,32,128]{2,1,0:T(8,128)S(1)} all-to-all(f32[16,32,128]{2,1,0:T(8,128)S(1)} %relay.3), channel_id=1, replica_groups=mesh['row'=8,'col'=16] {'col'}, dimensions={0} | all-to-all | bytes 524288 | tf_op jit(solution)/shard_map/all_to_all | solution.py:362
  (100 shorter events, 59.5 us)
Async XLA Ops:
  6.5 104.1 %all-gather.7.cloned.1.call-start = ((), (), s32[]{:S(2)}) async-start(), calls=%async_computation.16 | async-start | bytes 8912896 | tf_op jit(solution)/shard_map/all_gather | solution.py:451
  8.7 39.8 %copy-start = (bf16[1024,256]{1,0:T(8,128)(2,1)S(1)}, bf16[1024,256]{1,0:T(8,128)(2,1)}, u32[]{:S(2)}) copy-start(bf16[1024,256]{1,0:T(8,128)(2,1)} %get-tuple-element.41.own) | copy-start | bytes 1572868
  24.0 13.8 %collective-permute-start.1 = (bf16[1024,256]{1,0:T(8,128)(2,1)}, bf16[1024,256]{1,0:T(8,128)(2,1)S(1)}, u32[]{:S(2)}, u32[]{:S(2)}) collective-permute-start(bf16[1024,256]{1,0:T(8,128)(2,1)} %get-tuple-element.41.own), channel_id=1, source_target_pairs={{0,96},{16,112},{32,0},{48,16},{64,32},{80,48},{96,64},{112,80},{1... | collective-permute-start | bytes 1572872 | tf_op jit(solution)/shard_map/ppermute | solution.py:456
  25.2 15.1 %collective-permute-start = (bf16[1024,256]{1,0:T(8,128)(2,1)}, bf16[1024,256]{1,0:T(8,128)(2,1)S(1)}, u32[]{:S(2)}, u32[]{:S(2)}) collective-permute-start(bf16[1024,256]{1,0:T(8,128)(2,1)} %get-tuple-element.41.own), channel_id=1, source_target_pairs={{0,32},{16,48},{32,64},{48,80},{64,96},{80,112},{96,0},{112,16},{1... | collective-permute-start | bytes 1572872 | tf_op jit(solution)/shard_map/ppermute | solution.py:456
  37.8 7.3 %collective-permute-start.3 = (bf16[512,256]{1,0:T(8,128)(2,1)S(1)}, bf16[512,256]{1,0:T(8,128)(2,1)S(1)}, u32[]{:S(2)}, u32[]{:S(2)}) collective-permute-start(bf16[512,256]{1,0:T(8,128)(2,1)S(1)} %slice.23), channel_id=1, source_target_pairs={{0,96},{16,112},{32,0},{48,16},{64,32},{80,48},{96,64},{112,80},{1... | collective-permute-start | bytes 786440 | tf_op jit(solution)/shard_map/ppermute | solution.py:456
  40.3 9.9 %copy-start.12 = (bf16[1024,256]{1,0:T(8,128)(2,1)}, bf16[1024,256]{1,0:T(8,128)(2,1)S(1)}, u32[]{:S(2)}) copy-start(bf16[1024,256]{1,0:T(8,128)(2,1)S(1)} %collective-permute-done) | copy-start | bytes 1572868
  40.3 8.2 %collective-permute-start.2 = (bf16[512,256]{1,0:T(8,128)(2,1)S(1)}, bf16[512,256]{1,0:T(8,128)(2,1)S(1)}, u32[]{:S(2)}, u32[]{:S(2)}) collective-permute-start(bf16[512,256]{1,0:T(8,128)(2,1)S(1)} %slice.22), channel_id=1, source_target_pairs={{0,32},{16,48},{32,64},{48,80},{64,96},{80,112},{96,0},{112,16},{1... | collective-permute-start | bytes 786440 | tf_op jit(solution)/shard_map/ppermute | solution.py:456
  50.2 49.6 %collective-permute-start.4 = (bf16[4,1024,256]{2,1,0:T(8,128)(2,1)}, bf16[4,1024,256]{2,1,0:T(8,128)(2,1)}, u32[]{:S(2)}, u32[]{:S(2)}) collective-permute-start(bf16[4,1024,256]{2,1,0:T(8,128)(2,1)} %pad_maximum_fusion), channel_id=1, source_target_pairs={{0,16},{16,0},{32,48},{48,32},{64,80},{80,64},{96,112},{112,96},{1... | collective-permute-start | bytes 6291464 | tf_op jit(solution)/shard_map/ppermute | solution.py:486
  51.1 26.4 %all-to-all-start.1 = ((bf16[16,80,256]{2,1,0:T(8,128)(2,1)}), bf16[16,80,256]{2,1,0:T(8,128)(2,1)}, u32[]{:S(2)}, u32[]{:S(2)}) async-start(bf16[16,80,256]{2,1,0:T(8,128)(2,1)} %broadcast_in_dim.69), calls=%async_computation.1 | async-start | bytes 1310720 | tf_op jit(solution)/shard_map/all_to_all | solution.py:358
  78.7 24.3 %copy-start.2 = (bf16[64,256]{1,0:T(8,128)(2,1)}, bf16[64,256]{1,0:T(8,128)(2,1)S(1)}, u32[]{:S(2)}) copy-start(bf16[64,256]{1,0:T(8,128)(2,1)S(1)} %slice.24.seeds) | copy-start | bytes 98308
  80.2 10.9 %all-to-all-start.2 = ((f32[8,32,128]{2,1,0:T(8,128)}), f32[8,32,128]{2,1,0:T(8,128)S(1)}, u32[]{:S(2)}, u32[]{:S(2)}) async-start(f32[8,32,128]{2,1,0:T(8,128)} %get-tuple-element.43), calls=%async_computation.2 | async-start | bytes 262144 | tf_op jit(solution)/shard_map/all_to_all | solution.py:362
  91.8 15.3 %all-to-all-start.3 = ((f32[16,32,128]{2,1,0:T(8,128)}), f32[16,32,128]{2,1,0:T(8,128)S(1)}, u32[]{:S(2)}, u32[]{:S(2)}) async-start(f32[16,32,128]{2,1,0:T(8,128)} %relay.2), calls=%async_computation.3 | async-start | bytes 524288 | tf_op jit(solution)/shard_map/all_to_all | solution.py:362
  98.0 89.7 %all-gather.9.cloned.1.call-start = ((), (), s32[]{:S(2)}) async-start(), calls=%async_computation.17 | async-start | bytes 2113536 | tf_op jit(solution)/shard_map/all_gather | solution.py:502
  141.6 49.8 %copy-start.5 = (f32[1,1024]{1,0:T(1,128)}, f32[1,1024]{1,0:T(1,128)S(1)}, u32[]{:S(2)}) copy-start(f32[1,1024]{1,0:T(1,128)S(1)} %get-tuple-element.61.root) | copy-start | bytes 12292
  141.6 11.1 %all-to-all-start.5 = ((f32[16,8,128]{2,1,0:T(8,128)}), f32[16,8,128]{2,1,0:T(8,128)S(1)}, u32[]{:S(2)}, u32[]{:S(2)}) async-start(f32[16,8,128]{2,1,0:T(8,128)} %get-tuple-element.66), calls=%async_computation.5 | async-start | bytes 131072 | tf_op jit(solution)/shard_map/all_to_all | solution.py:362
  145.1 70.3 %reduce-scatter.3.cloned.1.call-start = ((), (), s32[]{:S(2)}) async-start(), calls=%async_computation.14 | async-start | bytes 1179648 | tf_op jit(solution)/shard_map/reduce_scatter | solution.py:522
  175.8 39.6 %all-to-all-start.7 = ((bf16[16,64,1024]{2,1,0:T(8,128)(2,1)}), bf16[16,64,1024]{2,1,0:T(8,128)(2,1)}, u32[]{:S(2)}, u32[]{:S(2)}) async-start(bf16[16,64,1024]{2,1,0:T(8,128)(2,1)} %apply_tiles.5), calls=%async_computation.7 | async-start | bytes 4194304 | tf_op jit(solution)/shard_map/all_to_all | solution.py:362
  191.4 24.0 %copy-start.3 = (f32[64,64]{1,0:T(8,128)}, f32[64,64]{1,0:T(8,128)S(1)}, u32[]{:S(2)}) copy-start(f32[64,64]{1,0:T(8,128)S(1)} %later_factor.1.factor) | copy-start | bytes 49156
  219.2 31.9 %all-to-all-start.8 = ((bf16[16,64,1024]{2,1,0:T(8,128)(2,1)}), bf16[16,64,1024]{2,1,0:T(8,128)(2,1)}, u32[]{:S(2)}, u32[]{:S(2)}) async-start(bf16[16,64,1024]{2,1,0:T(8,128)(2,1)} %get-tuple-element.72), calls=%async_computation.9 | async-start | bytes 4194304 | tf_op jit(solution)/shard_map/all_to_all | solution.py:362
  223.7 32.7 %all-gather.11.cloned.1.call-start = ((), (), s32[]{:S(2)}) async-start(), calls=%async_computation.18 | async-start | bytes 1179648 | tf_op jit(solution)/shard_map/all_gather | solution.py:532
  224.3 70.8 %reduce-scatter.5.cloned.1.call-start = ((), (), s32[]{:S(2)}) async-start(), calls=%async_computation.15 | async-start | bytes 1179648 | tf_op jit(solution)/shard_map/reduce_scatter | solution.py:522
  263.0 9.6 %copy-start.14 = (bf16[64,1024]{1,0:T(8,128)(2,1)S(1)}, bf16[64,1024]{1,0:T(8,128)(2,1)}, u32[]{:S(2)}) copy-start(bf16[64,1024]{1,0:T(8,128)(2,1)} %get-tuple-element.71) | copy-start | bytes 393220
  263.0 32.1 %all-to-all-start.9 = ((bf16[16,64,1024]{2,1,0:T(8,128)(2,1)}), bf16[16,64,1024]{2,1,0:T(8,128)(2,1)}, u32[]{:S(2)}, u32[]{:S(2)}) async-start(bf16[16,64,1024]{2,1,0:T(8,128)(2,1)} %apply_tiles.7), calls=%async_computation.10 | async-start | bytes 4194304 | tf_op jit(solution)/shard_map/all_to_all | solution.py:362
  272.6 22.5 %copy-start.6 = (f32[1,1024]{1,0:T(1,128)S(1)}, f32[1,1024]{1,0:T(1,128)}, u32[]{:S(2)}) copy-start(f32[1,1024]{1,0:T(1,128)} %copy-done.5) | copy-start | bytes 12292
  (11 other events, 22.0 us)
Sparse Core Ops, SparseCore 0:
  9.5 80.3 all-gather.6
  110.8 64.3 all-gather.8
  177.5 30.1 reduce-scatter.2
  226.0 25.0 all-gather.10
  256.6 33.1 reduce-scatter.4

commit v5 on v4

--- a/solution.py
+++ b/solution.py
@@ -21,6 +21,14 @@
     for start in range(128, values.shape[1], 128):
         part = part + values[:, start : start + 128]
     return jnp.sum(part.T, axis=0, keepdims=True)
+
+
+def task_lists(slots):
+    return 0, slots, 2 * slots, 3 * slots, 5 * slots
+
+
+def live_step(step, lists, slots):
+    return jnp.maximum(jnp.minimum(step, lists[5 * slots] - 1), 0)
 
 
 def half_squares(rows):
@@ -176,50 +184,45 @@
     copies[...] = jnp.broadcast_to(jnp.sum(grams[...], axis=0)[None], copies.shape)
 
 
-def vectors_kernel(first, second, live, left, right, seeds, factor, from_first, from_second):
-    @pl.when(pl.program_id(0) < live[0])
+def vectors_kernel(slots, lists, block, seeds, factor, out):
+    @pl.when(pl.program_id(0) < lists[5 * slots])
     def work():
-        for block, out in ((left, from_first), (right, from_second)):
-            out[0] = transform(factor[...], seed_kernel_rows(seeds[...], block[0]))
-
-
-def start_vectors(first, second, live, row_band, col_band, seeds, factor):
-    unused, rows, depth = row_band.shape
-    slots = first.shape[0]
+        out[0] = transform(factor[...], seed_kernel_rows(seeds[...], block[0]))
+
+
+def start_vectors(lists, slots, source, band, seeds, factor):
+    unused, rows, depth = band.shape
     vecs = seeds.shape[0]
-
-    def last(step, live_ref):
-        return jnp.maximum(jnp.minimum(step, live_ref[0] - 1), 0)
-
     return pl.pallas_call(
-        vectors_kernel,
+        functools.partial(vectors_kernel, slots),
         grid_spec=pltpu.PrefetchScalarGridSpec(
-            num_scalar_prefetch=3,
+            num_scalar_prefetch=1,
             grid=(slots,),
             in_specs=[
-                pl.BlockSpec((1, rows, depth), lambda s, f, g, n: (f[last(s, n)], 0, 0)),
-                pl.BlockSpec((1, rows, depth), lambda s, f, g, n: (g[last(s, n)], 0, 0)),
-                pl.BlockSpec((vecs, depth), lambda s, f, g, n: (0, 0)),
-                pl.BlockSpec((vecs, vecs), lambda s, f, g, n: (0, 0)),
+                pl.BlockSpec(
+                    (1, rows, depth), lambda s, t: (t[source + live_step(s, t, slots)], 0, 0)
+                ),
+                pl.BlockSpec((vecs, depth), lambda s, t: (0, 0)),
+                pl.BlockSpec((vecs, vecs), lambda s, t: (0, 0)),
             ],
-            out_specs=[
-                pl.BlockSpec((1, vecs, rows), lambda s, f, g, n: (last(s, n), 0, 0))
-            ] * 2,
+            out_specs=pl.BlockSpec(
+                (1, vecs, rows), lambda s, t: (live_step(s, t, slots), 0, 0)
+            ),
         ),
-        out_shape=[f32(slots, vecs, rows)] * 2,
+        out_shape=f32(slots, vecs, rows),
         compiler_params=pltpu.CompilerParams(vmem_limit_bytes=VMEM),
         name="start_vectors",
-    )(first, second, live, row_band, col_band, seeds, factor)
-
-
-def form_kernel(chunk, first, second, owners, live, left, right, tile, degrees):
+    )(lists, band, seeds, factor)
+
+
+def form_kernel(chunk, slots, lists, left, right, tile, degrees):
     step = pl.program_id(0)
 
     @pl.when(step == 0)
     def clear():
         degrees[...] = jnp.zeros_like(degrees)
 
-    @pl.when(step < live[0])
+    @pl.when(step < lists[5 * slots])
     def work():
         rows = left.shape[1]
         right_rows = right[0]
@@ -231,41 +234,40 @@
             tile[0, start : start + chunk, :] = value.astype(jnp.bfloat16)
             col_total = col_total + jnp.sum(value, axis=0, keepdims=True)
             row_totals.append(lane_sums(value))
-        left_owner = owners[2 * step]
-        right_owner = owners[2 * step + 1]
+        left_owner = lists[3 * slots + 2 * step]
+        right_owner = lists[3 * slots + 2 * step + 1]
         row_total = jnp.concatenate(row_totals, axis=1)
         degrees[left_owner] = degrees[left_owner] + pack_row(row_total)
         degrees[right_owner] = degrees[right_owner] + pack_row(col_total)
 
 
-def form_tiles(first, second, owners, live, row_band, col_band):
+def form_tiles(lists, slots, row_band, col_band):
     col_devices, rows, depth = row_band.shape
     all_devices = col_devices * col_band.shape[0]
-    slots = first.shape[0]
-
-    def last(step, live_ref):
-        return jnp.maximum(jnp.minimum(step, live_ref[0] - 1), 0)
+    firsts, unused, places, owners, live = task_lists(slots)
 
     return pl.pallas_call(
-        functools.partial(form_kernel, min(256, rows)),
+        functools.partial(form_kernel, min(256, rows), slots),
         grid_spec=pltpu.PrefetchScalarGridSpec(
-            num_scalar_prefetch=4,
+            num_scalar_prefetch=1,
             grid=(slots,),
             in_specs=[
-                pl.BlockSpec((1, rows, depth), lambda s, f, g, o, n: (f[last(s, n)], 0, 0)),
-                pl.BlockSpec((1, rows, depth), lambda s, f, g, o, n: (g[last(s, n)], 0, 0)),
+                pl.BlockSpec(
+                    (1, rows, depth), lambda s, t: (t[firsts + live_step(s, t, slots)], 0, 0)
+                ),
+                pl.BlockSpec(
+                    (1, rows, depth), lambda s, t: (t[places + live_step(s, t, slots)], 0, 0)
+                ),
             ],
             out_specs=[
-                pl.BlockSpec((1, rows, rows), lambda s, f, g, o, n: (last(s, n), 0, 0)),
-                pl.BlockSpec(
-                    (all_devices, rows // 128, 128), lambda s, f, g, o, n: (0, 0, 0)
-                ),
+                pl.BlockSpec((1, rows, rows), lambda s, t: (live_step(s, t, slots), 0, 0)),
+                pl.BlockSpec((all_devices, rows // 128, 128), lambda s, t: (0, 0, 0)),
             ],
         ),
         out_shape=[bf16(slots, rows, rows), f32(all_devices, rows // 128, 128)],
         compiler_params=pltpu.CompilerParams(vmem_limit_bytes=VMEM),
         name="form_tiles",
-    )(first, second, owners, live, row_band, col_band)
+    )(lists, row_band, col_band)
 
 
 def diagonal_kernel(chunk, own, tile, degree):
@@ -293,41 +295,35 @@
     )(own)
 
 
-def apply_kernel(contract, source, target, live, tile, vectors, *rest):
+def apply_kernel(contract, slots, target, lists, tile, vectors, *rest):
     step = pl.program_id(0)
-    roots, out, total = rest if len(rest) == 3 else (None,) + rest
+    roots, out = rest if len(rest) == 2 else (None,) + rest
 
     @pl.when(step == 0)
     def clear():
-        total[...] = jnp.zeros_like(total)
-
-    @pl.when(step < live[0])
+        out[...] = jnp.zeros_like(out)
+
+    @pl.when(step < lists[5 * slots])
     def work():
-        slot = target[step]
+        slot = lists[target + step]
         block = vectors[0]
         if roots is not None:
             block = (block * unpack_row(roots[0])).astype(jnp.bfloat16)
-        total[slot] = total[slot] + lax.dot_general(
+        product = lax.dot_general(
             block, tile[0], (((1,), (contract,)), ((), ())), preferred_element_type=jnp.float32
         )
-
-    @pl.when(step == pl.num_programs(0) - 1)
-    def store():
-        out[...] = total[...].astype(jnp.bfloat16)
-
-
-def apply_tiles(contract, source, target, live, tiles, vectors, roots, targets):
+        out[slot] = (out[slot].astype(jnp.float32) + product).astype(jnp.bfloat16)
+
+
+def apply_tiles(contract, lists, source, target, tiles, vectors, roots, targets):
     slots, rows, unused = tiles.shape
     vecs = vectors.shape[1]
 
-    def last(step, live_ref):
-        return jnp.maximum(jnp.minimum(step, live_ref[0] - 1), 0)
-
-    def by_task(s, f, g, n):
-        return (last(s, n), 0, 0)
-
-    def by_block(s, f, g, n):
-        return (f[last(s, n)], 0, 0)
+    def by_task(s, t):
+        return (live_step(s, t, slots), 0, 0)
+
+    def by_block(s, t):
+        return (t[source + live_step(s, t, slots)], 0, 0)
 
     in_specs = [
         pl.BlockSpec((1, rows, rows), by_task),
@@ -338,18 +334,17 @@
         in_specs.append(pl.BlockSpec((1, rows // 128, 128), by_block))
         operands.append(roots)
     return pl.pallas_call(
-        functools.partial(apply_kernel, contract),
+        functools.partial(apply_kernel, contract, slots, target),
         grid_spec=pltpu.PrefetchScalarGridSpec(
-            num_scalar_prefetch=3,
+            num_scalar_prefetch=1,
             grid=(slots,),
             in_specs=in_specs,
-            out_specs=pl.BlockSpec((targets, vecs, rows), lambda s, f, g, n: (0, 0, 0)),
-            scratch_shapes=[pltpu.VMEM((targets, vecs, rows), jnp.float32)],
+            out_specs=pl.BlockSpec((targets, vecs, rows), lambda s, t: (0, 0, 0)),
         ),
         out_shape=bf16(targets, vecs, rows),
         compiler_params=pltpu.CompilerParams(vmem_limit_bytes=VMEM),
         name="apply_tiles",
-    )(source, target, live, *operands)
+    )(lists, *operands)
 
 
 def spread_to(array, axis):
@@ -372,7 +367,7 @@
     return order + 4 * ((index + here) % 2)
 
 
-def assign_kernel(slots, cols, here, table, first, second, place, owners, live):
+def assign_kernel(slots, cols, here, table, lists):
     devices = table.shape[1]
     me = here[0]
     filler = jnp.zeros((devices - table.shape[0], devices), jnp.float32)
@@ -413,28 +408,27 @@
         other = kept * partner + come * number
         cell = (kept + come) * (number * slots + (slot + 1)) * devices + other
         code = jnp.where(lane == slot, cell, code)
-    live[0] = jnp.sum(jnp.where(code > 0, 1.0, 0.0)).astype(jnp.int32)
+    lists[5 * slots] = jnp.sum(jnp.where(code > 0, 1.0, 0.0)).astype(jnp.int32)
     for slot in range(slots):
         top = jnp.max(code)
         partner = lax.rem(top.astype(jnp.int32), devices)
         code = jnp.where(code == top, 0.0, code)
         first_slot = lax.rem(partner, cols)
         second_slot = lax.div(partner, cols)
-        first[slot] = first_slot
-        second[slot] = second_slot
-        place[slot] = place_in_row(second_slot, lax.div(me, cols))
-        owners[2 * slot] = lax.div(me, cols) * cols + first_slot
-        owners[2 * slot + 1] = second_slot * cols + lax.rem(me, cols)
+        lists[slot] = first_slot
+        lists[slots + slot] = second_slot
+        lists[2 * slots + slot] = place_in_row(second_slot, lax.div(me, cols))
+        lists[3 * slots + 2 * slot] = lax.div(me, cols) * cols + first_slot
+        lists[3 * slots + 2 * slot + 1] = second_slot * cols + lax.rem(me, cols)
 
 
 def assign_tasks(self_index, table, slots, cols):
     smem = pl.BlockSpec(memory_space=pltpu.SMEM)
-    sizes = (slots, slots, slots, 2 * slots, 1)
     return pl.pallas_call(
         functools.partial(assign_kernel, slots, cols),
         in_specs=[smem, pl.BlockSpec(memory_space=pltpu.VMEM)],
-        out_specs=[smem] * len(sizes),
-        out_shape=[jax.ShapeDtypeStruct((size,), jnp.int32) for size in sizes],
+        out_specs=smem,
+        out_shape=jax.ShapeDtypeStruct((6 * slots,), jnp.int32),
         compiler_params=pltpu.CompilerParams(vmem_limit_bytes=SMALL),
         name="assign_tasks",
     )(self_index.reshape(1), table)
@@ -470,30 +464,31 @@
     ).astype(jnp.bfloat16)
     picked = jnp.concatenate([picked, lines], axis=0)
     seed_parts = spread_to(picked, "row")
-    sent, seed_parts = together(weighted, seed_parts)
-    before = shift(sent, 2)
-    after = shift(sent, -2)
+    before = shift(weighted, 2)
+    after = shift(weighted, -2)
+    before, after, seed_parts = together(before, after, seed_parts)
     half = rows // 2
     across_low = shift(before[:half], 2)
     across_high = shift(after[half:], -2)
     seed_parts = spread_to(jnp.sum(seed_parts, axis=0), "col")
+    diagonal, own_degree = form_diagonal(weighted)
     seed_sum = jnp.sum(seed_parts, axis=0)
     seeds = seed_sum[:vecs]
     table = seed_sum[vecs:, :all_devices].astype(jnp.float32)
-    assigned = assign_tasks(self_index, table, slots, col_devices)
-    across = jnp.concatenate([across_low, across_high], axis=0)
-    mine = jnp.stack([weighted, before, after, across])
-    other = lax.ppermute(mine, "row", [(i, i ^ 1) for i in range(row_devices)])
-
     start, grams = call(
         start_kernel, "start", [f32(vecs, rows), f32(row_devices, vecs // 2, 2 * vecs)]
     )(seeds, weighted)
+    across_low, across_high, grams = together(across_low, across_high, grams)
     grams = exchange(grams, "row")
-    grams, first, second_device, second, owners, live = together(grams, *assigned)
+    across = jnp.concatenate([across_low, across_high], axis=0)
+    mine = jnp.stack([weighted, before, after, across])
+    mine, grams = together(mine, grams)
+    other = lax.ppermute(mine, "row", [(i, i ^ 1) for i in range(row_devices)])
     grams = call(relay_kernel, "relay", f32(col_devices, vecs // 2, 2 * vecs))(grams)
     grams = exchange(grams, "col")
+    lists = assign_tasks(self_index, table, slots, col_devices)
+    firsts, seconds, places, unused, unused = task_lists(slots)
     col_band, grams = together(jnp.concatenate([mine, other], axis=0), grams)
-    diagonal, own_degree = form_diagonal(weighted)
     factor, subspace, later_gram = call(
         first_factor_kernel,
         "first_factor",
@@ -501,27 +496,28 @@
     )(grams, start, diagonal, own_degree)
     later_grams = lax.all_gather(later_gram, ("row", "col"), axis=0)
 
-    tiles, degrees = form_tiles(first, second, owners, live, row_band, col_band)
+    tiles, degrees = form_tiles(lists, slots, row_band, col_band)
     roots, inv_root = call(
         degree_kernel, "degree", [f32(col_devices, rows // 128, 128), f32(1, rows)]
     )(own_degree, exchange(degrees, ("row", "col")))
-    from_first, from_second = start_vectors(
-        first, second, live, row_band, col_band, seeds, factor
-    )
+    row_roots = exchange(roots, "col")
+    from_first = start_vectors(lists, slots, firsts, row_band, seeds, factor)
+    row_roots, from_first, roots = together(row_roots, from_first, roots)
     col_roots = exchange(roots[:row_devices], "row")
-    row_roots = exchange(roots, "col")
+    from_second = start_vectors(lists, slots, places, col_band, seeds, factor)
+    row_roots, col_roots, from_second = together(row_roots, col_roots, from_second)
     spread = (subspace * inv_root).astype(jnp.bfloat16)
     for iteration in range(ITERS):
         own_part = lax.dot_general(
             spread, diagonal, (((1,), (0,)), ((), ())), preferred_element_type=jnp.float32
         )
         to_second = apply_tiles(
-            0, first, second_device, live, tiles, from_first, row_roots, row_devices
+            0, lists, firsts, seconds, tiles, from_first, row_roots, row_devices
         )
         to_second, from_second = together(to_second, from_second)
         second_part = lax.psum_scatter(to_second, "row", scatter_dimension=0, tiled=False)
         to_first = apply_tiles(
-            1, second_device, first, live, tiles, from_second, col_roots, col_devices
+            1, lists, seconds, firsts, tiles, from_second, col_roots, col_devices
         )
         first_parts = exchange(to_first, "col")
         if iteration + 1 < ITERS:

time: 338 us -> 313 us (0.926)
  waiting for transfers between devices: 112 us -> 102 us
  blocking collectives: 71.8 us -> 63.4 us
  local copies, waits for them, and re-layouts: 14.6 us -> 8 us
  other arithmetic: 7.1 us -> 12.3 us
    ppermute x4, waiting for transfers between devices: 19.9 us -> 0.01 us  [shift(): lax.ppermute(array, 'row', [(i, (i + by) % row_devices) for i in range(ro...]
    all_to_all x6 -> x7, waiting for transfers between devices: 77.3 us -> 92 us  [exchange(): return lax.all_to_all(copies, axis, 0, 0, tiled=True)]
    all_to_all x4 -> x3, blocking collectives: 59.4 us -> 51.1 us  [exchange(): return lax.all_to_all(copies, axis, 0, 0, tiled=True)]
    all_to_all x1, waiting for transfers between devices: 14.4 us -> 8.76 us  [spread_to(): return lax.all_to_all(copies, axis, 0, 0, tiled=True)]
    unnamed x38 -> x30, local copies, waits for them, and re-layouts: 8.02 us -> 3.15 us
    concatenate x0 -> x1, other arithmetic: none -> 4.8 us  [shards(): col_band, grams = together(jnp.concatenate([mine, other], axis=0), grams)]
    unnamed x2 -> x0, other arithmetic: 3.96 us -> none
    all_to_all x6 -> x7, starting transfers between devices: 39.1 us -> 35.6 us  [exchange(): return lax.all_to_all(copies, axis, 0, 0, tiled=True)]
  transfers between devices with their start and end apart: 17 -> 18, of which waited for: 9 -> 9; matrix products, arithmetic and copies ran while one was open for 5% -> 5% of each run, Pallas kernels for 16% -> 16%
where the time goes in v5:
time: 313 us; the launch traced here: 312 us
  waiting for transfers between devices  102 us (33%)
  blocking collectives  63.4 us (20%)
  Pallas kernels  59.6 us (19%)
  starting transfers between devices  50.6 us (16%)
  between operations  14.1 us (5%)
  other arithmetic  12.3 us (4%)
  local copies, waits for them, and re-layouts  8 us (3%)
    all_to_all x7, waiting for transfers between devices, exchange(): return lax.all_to_all(copies, axis, 0, 0, tiled=True)  92 us
    all_to_all x3, blocking collectives, exchange(): return lax.all_to_all(copies, axis, 0, 0, tiled=True)  51.1 us
    all_to_all x7, starting transfers between devices, exchange(): return lax.all_to_all(copies, axis, 0, 0, tiled=True)  35.6 us
    pallas_call x4, Pallas kernels, apply_tiles(): pl.pallas_call(functools.partial(apply_kernel, contract, slots, target),...  20.8 us
    all_to_all x1, blocking collectives, spread_to(): return lax.all_to_all(copies, axis, 0, 0, tiled=True)  12.3 us
    all_to_all x1, waiting for transfers between devices, spread_to(): return lax.all_to_all(copies, axis, 0, 0, tiled=True)  8.76 us
    all_to_all x1, starting transfers between devices, spread_to(): return lax.all_to_all(copies, axis, 0, 0, tiled=True)  8.18 us
    pallas_call x2, Pallas kernels, start_vectors(): pl.pallas_call(functools.partial(vectors_kernel, slots), grid_spec=pltpu....  7.97 us
  transfers between devices with their start and end apart: 18, of which 9 were waited for; matrix products, arithmetic and copies ran while one was open for 5% of the time, Pallas kernels for 16%

profile of v5, /device:TPU:0, one launch (start us, length us, event | category | flops | bytes accessed | tf_op | source)
XLA Modules:
  0.0 311.5 jit_solution(12002724867508261844)
XLA Ops:
  15.9 12.3 %all_to_all.60 = bf16[8,80,256]{2,1,0:T(8,128)(2,1)S(1)} all-to-all(bf16[8,80,256]{2,1,0:T(8,128)(2,1)S(1)} %broadcast_in_dim.68), channel_id=1, replica_groups=mesh['row'=8,'col'=16] {'row'}, dimensions={0} | all-to-all | bytes 655360 | tf_op jit(solution)/shard_map/all_to_all | solution.py:353
  29.3 8.2 %all-to-all-start.1 = ((bf16[16,80,256]{2,1,0:T(8,128)(2,1)}), bf16[16,80,256]{2,1,0:T(8,128)(2,1)S(1)}, u32[]{:S(2)}, u32[]{:S(2)}) async-start(bf16[16,80,256]{2,1,0:T(8,128)(2,1)} %broadcast_in_dim.69), calls=%async_computation.1 | async-start | bytes 1310720 | tf_op jit(solution)/shard_map/all_to_all | solution.py:353
  41.6 8.8 %all-to-all-done.1 = bf16[16,80,256]{2,1,0:T(8,128)(2,1)S(1)} async-done(((bf16[16,80,256]{2,1,0:T(8,128)(2,1)}), bf16[16,80,256]{2,1,0:T(8,128)(2,1)S(1)}, u32[]{:S(2)}, u32[]{:S(2)}) %all-to-all-start.1) | async-done | bytes 655392 | tf_op jit(solution)/shard_map/all_to_all | solution.py:353
  67.1 4.8 %pad_maximum_fusion.right.block = bf16[8,1024,256]{2,1,0:T(8,128)(2,1)} fusion(bf16[4,1024,256]{2,1,0:T(8,128)(2,1)} %collective-permute-done.4, bf16[4,1024,256]{2,1,0:T(8,128)(2,1)} %pad_maximum_fusion.1), kind=kLoop, calls=%fused_computation.1 | loop fusion | flops 2097152 | bytes 8388608 | tf_op jit(solution)/shard_map/concatenate | solution.py:491
  71.9 5.3 %all-to-all-done.3.grams = f32[16,32,128]{2,1,0:T(8,128)S(1)} async-done(((f32[16,32,128]{2,1,0:T(8,128)}), f32[16,32,128]{2,1,0:T(8,128)S(1)}, u32[]{:S(2)}, u32[]{:S(2)}) %all-to-all-start.3) | async-done | bytes 262176 | tf_op jit(solution)/shard_map/all_to_all | solution.py:357
  80.8 5.3 %assign_tasks.1.lists = s32[48]{0:T(128)S(1)} custom-call(s32[1]{0:T(128)} %bitcast.6.here, f32[16,128]{1,0:T(8,128)S(1)} %slice_convert_fusion.table), custom_call_target="tpu_custom_call" | custom-call | tf_op jit(solution)/shard_map/assign_tasks/pallas_call | solution.py:427
  86.7 6.7 %form_tiles.1 = (bf16[8,1024,1024]{2,1,0:T(8,128)(2,1)}, f32[128,8,128]{2,1,0:T(8,128)}) custom-call(s32[48]{0:T(128)} %copy-done.8, bf16[16,1024,256]{2,1,0:T(8,128)(2,1)} %bitcast.23, bf16[8,1024,256]{2,1,0:T(8,128)(2,1)} %pad_maximum_fusion.right.block), custom_call_target="tpu_custom_call" | custom-call | tf_op jit(solution)/shard_map/form_tiles/pallas_call | solution.py:249
  93.4 23.1 %all_to_all.61.parts = f32[128,8,128]{2,1,0:T(8,128)S(1)} all-to-all(f32[128,8,128]{2,1,0:T(8,128)} %get-tuple-element.55), channel_id=1, replica_groups=mesh['row'=8,'col'=16] {'row','col'}, dimensions={0} | all-to-all | bytes 1048576 | tf_op jit(solution)/shard_map/all_to_all | solution.py:357
  120.7 4.0 %start_vectors.2.vectors = f32[8,64,1024]{2,1,0:T(8,128)} custom-call(s32[48]{0:T(128)} %copy-done.8, bf16[16,1024,256]{2,1,0:T(8,128)(2,1)} %bitcast.24, bf16[64,256]{1,0:T(8,128)(2,1)} %copy-done.2, f32[64,64]{1,0:T(8,128)} %copy-done.3), custom_call_target="tpu_custom_call" | custom-call | tf_op jit(solution)/shard_map/start_vectors/pallas_call | solution.py:196
  124.7 3.6 %all-to-all-done.5.rest_0_ = f32[16,8,128]{2,1,0:T(8,128)S(1)} async-done(((f32[16,8,128]{2,1,0:T(8,128)}), f32[16,8,128]{2,1,0:T(8,128)S(1)}, u32[]{:S(2)}, u32[]{:S(2)}) %all-to-all-start.5) | async-done | bytes 65568 | tf_op jit(solution)/shard_map/all_to_all | solution.py:357
  133.1 4.0 %start_vectors.3.vectors = f32[8,64,1024]{2,1,0:T(8,128)} custom-call(s32[48]{0:T(128)} %copy-done.8, bf16[8,1024,256]{2,1,0:T(8,128)(2,1)} %pad_maximum_fusion.right.block, bf16[64,256]{1,0:T(8,128)(2,1)} %copy-done.2, f32[64,64]{1,0:T(8,128)} %copy-done.3), custom_call_target="tpu_custom_call" | custom-call | tf_op jit(solution)/shard_map/start_vectors/pallas_call | solution.py:196
  138.4 4.9 %apply_tiles.4 = bf16[8,64,1024]{2,1,0:T(8,128)(2,1)} custom-call(s32[48]{0:T(128)} %copy-done.8, bf16[8,1024,1024]{2,1,0:T(8,128)(2,1)} %get-tuple-element.57.tile, f32[8,64,1024]{2,1,0:T(8,128)} %start_vectors.2.vectors, f32[16,8,128]{2,1,0:T(8,128)} %copy-done.12), custom_call_target="tpu_custom_call" | custom-call | tf_op jit(solution)/shard_map/apply_tiles/pallas_call | solution.py:336
  143.3 5.7 %apply_tiles.5 = bf16[16,64,1024]{2,1,0:T(8,128)(2,1)} custom-call(s32[48]{0:T(128)} %copy-done.8, bf16[8,1024,1024]{2,1,0:T(8,128)(2,1)} %get-tuple-element.57.tile, f32[8,64,1024]{2,1,0:T(8,128)} %start_vectors.3.vectors, f32[8,8,128]{2,1,0:T(8,128)} %copy-done.13), custom_call_target="tpu_custom_call" | custom-call | tf_op jit(solution)/shard_map/apply_tiles/pallas_call | solution.py:336
  149.0 8.3 %all-to-all-start.7 = ((bf16[16,64,1024]{2,1,0:T(8,128)(2,1)}), bf16[16,64,1024]{2,1,0:T(8,128)(2,1)}, u32[]{:S(2)}, u32[]{:S(2)}) async-start(bf16[16,64,1024]{2,1,0:T(8,128)(2,1)} %apply_tiles.5), calls=%async_computation.7 | async-start | bytes 4194304 | tf_op jit(solution)/shard_map/all_to_all | solution.py:357
  162.8 24.5 %all-to-all-done.7.first_parts = bf16[16,64,1024]{2,1,0:T(8,128)(2,1)} async-done(((bf16[16,64,1024]{2,1,0:T(8,128)(2,1)}), bf16[16,64,1024]{2,1,0:T(8,128)(2,1)}, u32[]{:S(2)}, u32[]{:S(2)}) %all-to-all-start.7) | async-done | bytes 2097184 | tf_op jit(solution)/shard_map/all_to_all | solution.py:357
  187.3 3.8 %between.1 = (bf16[16,64,1024]{2,1,0:T(8,128)(2,1)}, bf16[64,1024]{1,0:T(8,128)(2,1)}) custom-call(f32[64,1024]{1,0:T(8,128)} %fusion.own_part, bf16[16,64,1024]{2,1,0:T(8,128)(2,1)} %all-to-all-done.7.first_parts, bf16[64,1024]{1,0:T(8,128)(2,1)} %bitcast.28, f32[1,1024]{1,0:T(1,128)} %copy-done.6, f32[64,64]{1,0:T(8,128)} %copy-done.4), custom_call_target="tpu_custom_call" | custom-call | tf_op jit(solution)/shard_map/between/pallas_call | solution.py:525
  191.1 6.6 %all-to-all-start.8 = ((bf16[16,64,1024]{2,1,0:T(8,128)(2,1)}), bf16[16,64,1024]{2,1,0:T(8,128)(2,1)}, u32[]{:S(2)}, u32[]{:S(2)}) async-start(bf16[16,64,1024]{2,1,0:T(8,128)(2,1)} %get-tuple-element.70), calls=%async_computation.9 | async-start | bytes 4194304 | tf_op jit(solution)/shard_map/all_to_all | solution.py:357
  198.4 27.4 %all-to-all-done.8.vectors = bf16[16,64,1024]{2,1,0:T(8,128)(2,1)} async-done(((bf16[16,64,1024]{2,1,0:T(8,128)(2,1)}), bf16[16,64,1024]{2,1,0:T(8,128)(2,1)}, u32[]{:S(2)}, u32[]{:S(2)}) %all-to-all-start.8) | async-done | bytes 2097184 | tf_op jit(solution)/shard_map/all_to_all | solution.py:357
  225.8 4.7 %apply_tiles.6 = bf16[8,64,1024]{2,1,0:T(8,128)(2,1)} custom-call(s32[48]{0:T(128)} %copy-done.8, bf16[8,1024,1024]{2,1,0:T(8,128)(2,1)} %get-tuple-element.57.tile, bf16[16,64,1024]{2,1,0:T(8,128)(2,1)} %all-to-all-done.8.vectors), custom_call_target="tpu_custom_call" | custom-call | tf_op jit(solution)/shard_map/apply_tiles/pallas_call | solution.py:336
  230.5 5.6 %apply_tiles.7 = bf16[16,64,1024]{2,1,0:T(8,128)(2,1)} custom-call(s32[48]{0:T(128)} %copy-done.8, bf16[8,1024,1024]{2,1,0:T(8,128)(2,1)} %get-tuple-element.57.tile, bf16[8,64,1024]{2,1,0:T(8,128)(2,1)} %bitcast.27), custom_call_target="tpu_custom_call" | custom-call | tf_op jit(solution)/shard_map/apply_tiles/pallas_call | solution.py:336
  236.0 6.9 %all-to-all-start.9 = ((bf16[16,64,1024]{2,1,0:T(8,128)(2,1)}), bf16[16,64,1024]{2,1,0:T(8,128)(2,1)}, u32[]{:S(2)}, u32[]{:S(2)}) async-start(bf16[16,64,1024]{2,1,0:T(8,128)(2,1)} %apply_tiles.7), calls=%async_computation.10 | async-start | bytes 4194304 | tf_op jit(solution)/shard_map/all_to_all | solution.py:357
  243.5 27.4 %all-to-all-done.9.first_parts = bf16[16,64,1024]{2,1,0:T(8,128)(2,1)} async-done(((bf16[16,64,1024]{2,1,0:T(8,128)(2,1)}), bf16[16,64,1024]{2,1,0:T(8,128)(2,1)}, u32[]{:S(2)}, u32[]{:S(2)}) %all-to-all-start.9) | async-done | bytes 2097184 | tf_op jit(solution)/shard_map/all_to_all | solution.py:357
  274.1 15.6 %all_to_all.62.grams = f32[8,32,128]{2,1,0:T(8,128)S(1)} all-to-all(f32[8,32,128]{2,1,0:T(8,128)S(1)} %get-tuple-element.73), channel_id=1, replica_groups=mesh['row'=8,'col'=16] {'row'}, dimensions={0} | all-to-all | bytes 262144 | tf_op jit(solution)/shard_map/all_to_all | solution.py:357
  289.8 12.4 %all_to_all.63.grams = f32[16,32,128]{2,1,0:T(8,128)S(1)} all-to-all(f32[16,32,128]{2,1,0:T(8,128)S(1)} %relay.3), channel_id=1, replica_groups=mesh['row'=8,'col'=16] {'col'}, dimensions={0} | all-to-all | bytes 524288 | tf_op jit(solution)/shard_map/all_to_all | solution.py:357
  (94 shorter events, 57.5 us)
Async XLA Ops:
  6.5 80.1 %all-gather.7.cloned.1.call-start = ((), (), s32[]{:S(2)}) async-start(), calls=%async_computation.16 | async-start | bytes 8912896 | tf_op jit(solution)/shard_map/all_gather | solution.py:445
  8.5 19.7 %collective-permute-start = (bf16[1024,256]{1,0:T(8,128)(2,1)}, bf16[1024,256]{1,0:T(8,128)(2,1)S(1)}, u32[]{:S(2)}, u32[]{:S(2)}) collective-permute-start(bf16[1024,256]{1,0:T(8,128)(2,1)} %multiply_convert_fusion.own), channel_id=1, source_target_pairs={{0,32},{16,48},{32,64},{48,80},{64,96},{80,112},{96,0},{112,16},{1... | collective-permute-start | bytes 1572872 | tf_op jit(solution)/shard_map/ppermute | solution.py:450
  10.2 18.1 %collective-permute-start.1 = (bf16[1024,256]{1,0:T(8,128)(2,1)}, bf16[1024,256]{1,0:T(8,128)(2,1)S(1)}, u32[]{:S(2)}, u32[]{:S(2)}) collective-permute-start(bf16[1024,256]{1,0:T(8,128)(2,1)} %multiply_convert_fusion.own), channel_id=1, source_target_pairs={{0,96},{16,112},{32,0},{48,16},{64,32},{80,48},{96,64},{112,80},{1... | collective-permute-start | bytes 1572872 | tf_op jit(solution)/shard_map/ppermute | solution.py:450
  15.9 25.6 %copy-start.9 = (bf16[1024,256]{1,0:T(8,128)(2,1)S(1)}, bf16[1024,256]{1,0:T(8,128)(2,1)}, u32[]{:S(2)}) copy-start(bf16[1024,256]{1,0:T(8,128)(2,1)} %param.5) | copy-start | bytes 1572868
  15.9 25.6 %copy-start.14 = (f32[256]{0:T(256)S(1)}, f32[256]{0:T(256)}, u32[]{:S(2)}) copy-start(f32[256]{0:T(256)} %param.6) | copy-start | bytes 3076
  29.3 21.2 %copy-start = (bf16[1024,256]{1,0:T(8,128)(2,1)S(1)}, bf16[1024,256]{1,0:T(8,128)(2,1)}, u32[]{:S(2)}) copy-start(bf16[1024,256]{1,0:T(8,128)(2,1)} %multiply_convert_fusion.own) | copy-start | bytes 1572868
  29.3 21.1 %all-to-all-start.1 = ((bf16[16,80,256]{2,1,0:T(8,128)(2,1)}), bf16[16,80,256]{2,1,0:T(8,128)(2,1)S(1)}, u32[]{:S(2)}, u32[]{:S(2)}) async-start(bf16[16,80,256]{2,1,0:T(8,128)(2,1)} %broadcast_in_dim.69), calls=%async_computation.1 | async-start | bytes 1310720 | tf_op jit(solution)/shard_map/all_to_all | solution.py:353
  37.5 14.5 %collective-permute-start.2 = (bf16[512,256]{1,0:T(8,128)(2,1)S(1)}, bf16[512,256]{1,0:T(8,128)(2,1)}, u32[]{:S(2)}, u32[]{:S(2)}) collective-permute-start(bf16[512,256]{1,0:T(8,128)(2,1)S(1)} %slice.15), channel_id=1, source_target_pairs={{0,32},{16,48},{32,64},{48,80},{64,96},{80,112},{96,0},{112,16},{1... | collective-permute-start | bytes 786440 | tf_op jit(solution)/shard_map/ppermute | solution.py:450
  39.4 12.6 %collective-permute-start.3 = (bf16[512,256]{1,0:T(8,128)(2,1)}, bf16[512,256]{1,0:T(8,128)(2,1)}, u32[]{:S(2)}, u32[]{:S(2)}) collective-permute-start(bf16[512,256]{1,0:T(8,128)(2,1)} %slice.16), channel_id=1, source_target_pairs={{0,96},{16,112},{32,0},{48,16},{64,32},{80,48},{96,64},{112,80},{1... | collective-permute-start | bytes 786440 | tf_op jit(solution)/shard_map/ppermute | solution.py:450
  52.0 9.6 %all-to-all-start.2 = ((f32[8,32,128]{2,1,0:T(8,128)}), f32[8,32,128]{2,1,0:T(8,128)S(1)}, u32[]{:S(2)}, u32[]{:S(2)}) async-start(f32[8,32,128]{2,1,0:T(8,128)} %get-tuple-element.46), calls=%async_computation.2 | async-start | bytes 262144 | tf_op jit(solution)/shard_map/all_to_all | solution.py:357
  61.5 5.6 %collective-permute-start.4 = (bf16[4,1024,256]{2,1,0:T(8,128)(2,1)}, bf16[4,1024,256]{2,1,0:T(8,128)(2,1)}, u32[]{:S(2)}, u32[]{:S(2)}) collective-permute-start(bf16[4,1024,256]{2,1,0:T(8,128)(2,1)} %pad_maximum_fusion.1), channel_id=1, source_target_pairs={{0,16},{16,0},{32,48},{48,32},{64,80},{80,64},{96,112},{112,96},{1... | collective-permute-start | bytes 6291464 | tf_op jit(solution)/shard_map/ppermute | solution.py:486
  62.3 14.9 %all-to-all-start.3 = ((f32[16,32,128]{2,1,0:T(8,128)}), f32[16,32,128]{2,1,0:T(8,128)S(1)}, u32[]{:S(2)}, u32[]{:S(2)}) async-start(f32[16,32,128]{2,1,0:T(8,128)} %relay.2), calls=%async_computation.3 | async-start | bytes 524288 | tf_op jit(solution)/shard_map/all_to_all | solution.py:357
  65.8 91.5 %all-gather.9.cloned.1.call-start = ((), (), s32[]{:S(2)}) async-start(), calls=%async_computation.17 | async-start | bytes 2113536 | tf_op jit(solution)/shard_map/all_gather | solution.py:497
  80.8 12.6 %copy-start.3 = (f32[64,64]{1,0:T(8,128)}, f32[64,64]{1,0:T(8,128)S(1)}, u32[]{:S(2)}) copy-start(f32[64,64]{1,0:T(8,128)S(1)} %get-tuple-element.59.factor) | copy-start | bytes 49156
  117.2 44.4 %copy-start.6 = (f32[1,1024]{1,0:T(1,128)}, f32[1,1024]{1,0:T(1,128)S(1)}, u32[]{:S(2)}) copy-start(f32[1,1024]{1,0:T(1,128)S(1)} %get-tuple-element.56.root) | copy-start | bytes 12292
  117.2 11.1 %all-to-all-start.5 = ((f32[16,8,128]{2,1,0:T(8,128)}), f32[16,8,128]{2,1,0:T(8,128)S(1)}, u32[]{:S(2)}, u32[]{:S(2)}) async-start(f32[16,8,128]{2,1,0:T(8,128)} %get-tuple-element.62), calls=%async_computation.5 | async-start | bytes 131072 | tf_op jit(solution)/shard_map/all_to_all | solution.py:357
  129.7 8.7 %all-to-all-start.6 = ((f32[8,8,128]{2,1,0:T(8,128)}), f32[8,8,128]{2,1,0:T(8,128)S(1)}, u32[]{:S(2)}, u32[]{:S(2)}) async-start(f32[8,8,128]{2,1,0:T(8,128)} %slice.19), calls=%async_computation.6 | async-start | bytes 65536 | tf_op jit(solution)/shard_map/all_to_all | solution.py:357
  133.0 54.3 %reduce-scatter.3.cloned.1.call-start = ((), (), s32[]{:S(2)}) async-start(), calls=%async_computation.14 | async-start | bytes 1179648 | tf_op jit(solution)/shard_map/reduce_scatter | solution.py:518
  149.0 38.3 %all-to-all-start.7 = ((bf16[16,64,1024]{2,1,0:T(8,128)(2,1)}), bf16[16,64,1024]{2,1,0:T(8,128)(2,1)}, u32[]{:S(2)}, u32[]{:S(2)}) async-start(bf16[16,64,1024]{2,1,0:T(8,128)(2,1)} %apply_tiles.5), calls=%async_computation.7 | async-start | bytes 4194304 | tf_op jit(solution)/shard_map/all_to_all | solution.py:357
  191.1 34.6 %all-to-all-start.8 = ((bf16[16,64,1024]{2,1,0:T(8,128)(2,1)}), bf16[16,64,1024]{2,1,0:T(8,128)(2,1)}, u32[]{:S(2)}, u32[]{:S(2)}) async-start(bf16[16,64,1024]{2,1,0:T(8,128)(2,1)} %get-tuple-element.70), calls=%async_computation.9 | async-start | bytes 4194304 | tf_op jit(solution)/shard_map/all_to_all | solution.py:357
  197.8 32.7 %all-gather.11.cloned.1.call-start = ((), (), s32[]{:S(2)}) async-start(), calls=%async_computation.18 | async-start | bytes 1179648 | tf_op jit(solution)/shard_map/all_gather | solution.py:528
  198.3 72.6 %reduce-scatter.5.cloned.1.call-start = ((), (), s32[]{:S(2)}) async-start(), calls=%async_computation.15 | async-start | bytes 1179648 | tf_op jit(solution)/shard_map/reduce_scatter | solution.py:518
  236.0 34.9 %all-to-all-start.9 = ((bf16[16,64,1024]{2,1,0:T(8,128)(2,1)}), bf16[16,64,1024]{2,1,0:T(8,128)(2,1)}, u32[]{:S(2)}, u32[]{:S(2)}) async-start(bf16[16,64,1024]{2,1,0:T(8,128)(2,1)} %apply_tiles.7), calls=%async_computation.10 | async-start | bytes 4194304 | tf_op jit(solution)/shard_map/all_to_all | solution.py:357
  243.0 28.0 %copy-start.7 = (f32[1,1024]{1,0:T(1,128)S(1)}, f32[1,1024]{1,0:T(1,128)}, u32[]{:S(2)}) copy-start(f32[1,1024]{1,0:T(1,128)} %copy-done.6) | copy-start | bytes 12292
  (9 other events, 44.0 us)
Sparse Core Ops, SparseCore 0:
  9.5 77.1 all-gather.6
  89.6 64.8 all-gather.8
  156.9 30.1 reduce-scatter.2
  200.0 23.6 all-gather.10
  230.6 33.9 reduce-scatter.4

commit v6 on v5

--- a/solution.py
+++ b/solution.py
@@ -42,14 +42,6 @@
     )
     left_half = jnp.sum(half_squares(left), axis=1, keepdims=True)
     return jnp.exp2(dots * LOG2E - left_half - right_half)
-
-
-def pack_row(row):
-    return jnp.concatenate([row[:, i : i + 128] for i in range(0, row.shape[1], 128)], axis=0)
-
-
-def unpack_row(block):
-    return jnp.concatenate([block[i : i + 1, :] for i in range(block.shape[0])], axis=1)
 
 
 def packed_gram(vectors):
@@ -143,14 +135,32 @@
     later_gram[...] = packed_gram(product * root)
 
 
-def later_factor_kernel(grams, factor):
-    factor[...] = inverse_factor(jnp.sum(grams[...], axis=0), True)
-
-
-def degree_kernel(own_degree, parts, roots, root):
-    value = lax.rsqrt(jnp.sum(parts[...], axis=0) + pack_row(own_degree[...]))
-    roots[...] = jnp.broadcast_to(value[None], roots.shape)
-    root[...] = unpack_row(value)
+def later_factor_kernel(gram_rows, factor):
+    factor[...] = inverse_factor(gram_rows[:, 0, :], True)
+
+
+def later_factor(lines, vecs):
+    half, width = vecs // 2, 2 * vecs
+    place = lines.shape[2] // width - 1
+    return pl.pallas_call(
+        later_factor_kernel,
+        grid=(1,),
+        in_specs=[pl.BlockSpec((half, 1, width), lambda s: (0, 0, place))],
+        out_specs=pl.BlockSpec((vecs, vecs), lambda s: (0, 0)),
+        out_shape=f32(vecs, vecs),
+        compiler_params=pltpu.CompilerParams(vmem_limit_bytes=SMALL),
+        name="later_factor",
+    )(lines)
+
+
+def degree_kernel(own_degree, parts, copies, root):
+    points = root.shape[1]
+    total = jnp.sum(parts[...], axis=0)
+    value = lax.rsqrt(total[:, :points] + own_degree[...])
+    root[...] = value
+    copies[...] = jnp.broadcast_to(
+        jnp.concatenate([value, total[:, points:]], axis=1)[None], copies.shape
+    )
 
 
 def gathered(own_part, first_parts, second_part, root):
@@ -165,6 +175,13 @@
     value = (value * root[...]).astype(jnp.bfloat16)
     spread[...] = value
     copies[...] = jnp.broadcast_to(value[None], copies.shape)
+
+
+def between(own_part, first_parts, second_part, root, factor):
+    copies, vecs, rows = first_parts.shape
+    return call(
+        between_kernel, "between", [bf16(copies, vecs, rows), bf16(vecs, rows)], VMEM
+    )(own_part, first_parts, second_part, root, factor)
 
 
 def last_kernel(own_part, first_parts, second_part, root, subspace, grams):
@@ -211,16 +228,22 @@
         ),
         out_shape=f32(slots, vecs, rows),
         compiler_params=pltpu.CompilerParams(vmem_limit_bytes=VMEM),
+        cost_estimate=pl.CostEstimate(
+            flops=4_000_000_000, bytes_accessed=10_000_000, transcendentals=0
+        ),
         name="start_vectors",
     )(lists, band, seeds, factor)
 
 
-def form_kernel(chunk, slots, lists, left, right, tile, degrees):
+def form_kernel(chunk, slots, lists, left, right, gram, tile, lines):
     step = pl.program_id(0)
+    points = left.shape[1]
 
     @pl.when(step == 0)
     def clear():
-        degrees[...] = jnp.zeros_like(degrees)
+        lines[...] = jnp.zeros_like(lines)
+        for index in range(gram.shape[0]):
+            lines[index, :, points:] = gram[index : index + 1, :]
 
     @pl.when(step < lists[5 * slots])
     def work():
@@ -237,13 +260,13 @@
         left_owner = lists[3 * slots + 2 * step]
         right_owner = lists[3 * slots + 2 * step + 1]
         row_total = jnp.concatenate(row_totals, axis=1)
-        degrees[left_owner] = degrees[left_owner] + pack_row(row_total)
-        degrees[right_owner] = degrees[right_owner] + pack_row(col_total)
-
-
-def form_tiles(lists, slots, row_band, col_band):
+        lines[left_owner, :, :points] = lines[left_owner, :, :points] + row_total
+        lines[right_owner, :, :points] = lines[right_owner, :, :points] + col_total
+
+
+def form_tiles(lists, slots, row_band, col_band, gram):
     col_devices, rows, depth = row_band.shape
-    all_devices = col_devices * col_band.shape[0]
+    line = (col_devices * col_band.shape[0], 1, rows + gram.shape[1])
     firsts, unused, places, owners, live = task_lists(slots)
 
     return pl.pallas_call(
@@ -258,16 +281,17 @@
                 pl.BlockSpec(
                     (1, rows, depth), lambda s, t: (t[places + live_step(s, t, slots)], 0, 0)
                 ),
+                pl.BlockSpec(gram.shape, lambda s, t: (0, 0)),
             ],
             out_specs=[
                 pl.BlockSpec((1, rows, rows), lambda s, t: (live_step(s, t, slots), 0, 0)),
-                pl.BlockSpec((all_devices, rows // 128, 128), lambda s, t: (0, 0, 0)),
+                pl.BlockSpec(line, lambda s, t: (0, 0, 0)),
             ],
         ),
-        out_shape=[bf16(slots, rows, rows), f32(all_devices, rows // 128, 128)],
+        out_shape=[bf16(slots, rows, rows), f32(*line)],
         compiler_params=pltpu.CompilerParams(vmem_limit_bytes=VMEM),
         name="form_tiles",
-    )(lists, row_band, col_band)
+    )(lists, row_band, col_band, gram)
 
 
 def diagonal_kernel(chunk, own, tile, degree):
@@ -295,56 +319,75 @@
     )(own)
 
 
-def apply_kernel(contract, slots, target, lists, tile, vectors, *rest):
+def apply_kernel(slots, lists, tile, left, right, *rest):
     step = pl.program_id(0)
-    roots, out = rest if len(rest) == 2 else (None,) + rest
+    left_roots, right_roots, to_first, to_second = rest if len(rest) == 4 else (None, None) + rest
+
+    def scaled(vectors, roots):
+        if roots is None:
+            return vectors[0]
+        return (vectors[0] * roots[0, :, : vectors.shape[2]]).astype(jnp.bfloat16)
+
+    def add(out, slot, vectors, contract):
+        product = lax.dot_general(
+            vectors, tile[0], (((1,), (contract,)), ((), ())), preferred_element_type=jnp.float32
+        )
+        out[slot] = (out[slot].astype(jnp.float32) + product).astype(jnp.bfloat16)
 
     @pl.when(step == 0)
     def clear():
-        out[...] = jnp.zeros_like(out)
+        to_first[...] = jnp.zeros_like(to_first)
+        to_second[...] = jnp.zeros_like(to_second)
 
     @pl.when(step < lists[5 * slots])
     def work():
-        slot = lists[target + step]
-        block = vectors[0]
-        if roots is not None:
-            block = (block * unpack_row(roots[0])).astype(jnp.bfloat16)
-        product = lax.dot_general(
-            block, tile[0], (((1,), (contract,)), ((), ())), preferred_element_type=jnp.float32
-        )
-        out[slot] = (out[slot].astype(jnp.float32) + product).astype(jnp.bfloat16)
-
-
-def apply_tiles(contract, lists, source, target, tiles, vectors, roots, targets):
+        add(to_second, lists[slots + step], scaled(left, left_roots), 0)
+        add(to_first, lists[step], scaled(right, right_roots), 1)
+
+
+def apply_tiles(lists, tiles, from_first, from_second, roots, col_devices, row_devices):
     slots, rows, unused = tiles.shape
-    vecs = vectors.shape[1]
+    vecs = from_first.shape[1]
 
     def by_task(s, t):
         return (live_step(s, t, slots), 0, 0)
 
-    def by_block(s, t):
-        return (t[source + live_step(s, t, slots)], 0, 0)
-
+    def by_first(s, t):
+        return (t[live_step(s, t, slots)], 0, 0)
+
+    def by_second(s, t):
+        return (t[slots + live_step(s, t, slots)], 0, 0)
+
+    def by_owner(side):
+        return lambda s, t: (t[3 * slots + 2 * live_step(s, t, slots) + side], 0, 0)
+
+    block = (1, vecs, rows)
+    by_slot = roots is not None
     in_specs = [
         pl.BlockSpec((1, rows, rows), by_task),
-        pl.BlockSpec((1, vecs, rows), by_block if roots is None else by_task),
+        pl.BlockSpec(block, by_task if by_slot else by_first),
+        pl.BlockSpec(block, by_task if by_slot else by_second),
     ]
-    operands = [tiles, vectors]
-    if roots is not None:
-        in_specs.append(pl.BlockSpec((1, rows // 128, 128), by_block))
-        operands.append(roots)
-    return pl.pallas_call(
-        functools.partial(apply_kernel, contract, slots, target),
+    operands = [lists, tiles, from_first, from_second]
+    if by_slot:
+        for side in range(2):
+            in_specs.append(pl.BlockSpec((1,) + roots.shape[1:], by_owner(side)))
+            operands.append(roots)
+    return pl.pallas_call(
+        functools.partial(apply_kernel, slots),
         grid_spec=pltpu.PrefetchScalarGridSpec(
             num_scalar_prefetch=1,
             grid=(slots,),
             in_specs=in_specs,
-            out_specs=pl.BlockSpec((targets, vecs, rows), lambda s, t: (0, 0, 0)),
+            out_specs=[
+                pl.BlockSpec((col_devices, vecs, rows), lambda s, t: (0, 0, 0)),
+                pl.BlockSpec((row_devices, vecs, rows), lambda s, t: (0, 0, 0)),
+            ],
         ),
-        out_shape=bf16(targets, vecs, rows),
+        out_shape=[bf16(col_devices, vecs, rows), bf16(row_devices, vecs, rows)],
         compiler_params=pltpu.CompilerParams(vmem_limit_bytes=VMEM),
         name="apply_tiles",
-    )(lists, *operands)
+    )(*operands)
 
 
 def spread_to(array, axis):
@@ -494,40 +537,32 @@
         "first_factor",
         [f32(vecs, vecs), f32(vecs, rows), f32(vecs // 2, 2 * vecs)],
     )(grams, start, diagonal, own_degree)
-    later_grams = lax.all_gather(later_gram, ("row", "col"), axis=0)
-
-    tiles, degrees = form_tiles(lists, slots, row_band, col_band)
-    roots, inv_root = call(
-        degree_kernel, "degree", [f32(col_devices, rows // 128, 128), f32(1, rows)]
-    )(own_degree, exchange(degrees, ("row", "col")))
-    row_roots = exchange(roots, "col")
+
+    tiles, lines = form_tiles(lists, slots, row_band, col_band, later_gram)
+    copies, inv_root = call(degree_kernel, "degree", [f32(*lines.shape), f32(1, rows)])(
+        own_degree, exchange(lines, ("row", "col"))
+    )
+    lines = exchange(copies, ("row", "col"))
+    roots = lines
     from_first = start_vectors(lists, slots, firsts, row_band, seeds, factor)
-    row_roots, from_first, roots = together(row_roots, from_first, roots)
-    col_roots = exchange(roots[:row_devices], "row")
     from_second = start_vectors(lists, slots, places, col_band, seeds, factor)
-    row_roots, col_roots, from_second = together(row_roots, col_roots, from_second)
     spread = (subspace * inv_root).astype(jnp.bfloat16)
     for iteration in range(ITERS):
         own_part = lax.dot_general(
             spread, diagonal, (((1,), (0,)), ((), ())), preferred_element_type=jnp.float32
         )
-        to_second = apply_tiles(
-            0, lists, firsts, seconds, tiles, from_first, row_roots, row_devices
+        to_first, to_second = apply_tiles(
+            lists, tiles, from_first, from_second, roots, col_devices, row_devices
         )
-        to_second, from_second = together(to_second, from_second)
         second_part = lax.psum_scatter(to_second, "row", scatter_dimension=0, tiled=False)
-        to_first = apply_tiles(
-            1, lists, seconds, firsts, tiles, from_second, col_roots, col_devices
-        )
         first_parts = exchange(to_first, "col")
         if iteration + 1 < ITERS:
-            later_factor = call(later_factor_kernel, "later_factor", f32(vecs, vecs))(later_grams)
-            copies, spread = call(
-                between_kernel, "between", [bf16(col_devices, vecs, rows), bf16(vecs, rows)], VMEM
-            )(own_part, first_parts, second_part, inv_root, later_factor)
+            copies, spread = between(
+                own_part, first_parts, second_part, inv_root, later_factor(lines, vecs)
+            )
             from_second = lax.all_gather(spread, "row", axis=0)
             from_first = exchange(copies, "col")
-            row_roots = col_roots = None
+            roots = None
     subspace, grams = call(
         last_kernel, "last", [f32(vecs, rows), f32(row_devices, vecs // 2, 2 * vecs)]
     )(own_part, first_parts, second_part, inv_root)

time: 313 us -> 302 us (0.965)
  starting transfers between devices: 50.6 us -> 42.4 us
  blocking collectives: 63.4 us -> 57.4 us
  waiting for transfers between devices: 102 us -> 107 us
    all_gather x1, waiting for transfers between devices: 0.01 us -> 24.7 us  [shards(): from_second = lax.all_gather(spread, 'row', axis=0)]
    all_to_all x7 -> x6, waiting for transfers between devices: 92 us -> 68.7 us  [exchange(): return lax.all_to_all(copies, axis, 0, 0, tiled=True)]
    all_to_all x7 -> x6, starting transfers between devices: 35.6 us -> 27.4 us  [exchange(): return lax.all_to_all(copies, axis, 0, 0, tiled=True)]
    all_to_all x3, blocking collectives: 51.1 us -> 45 us  [exchange(): return lax.all_to_all(copies, axis, 0, 0, tiled=True)]
    all_gather x1, waiting for transfers between devices: 0.5 us -> 4.65 us  [shards(): row_band = lax.all_gather(weighted, 'col', axis=0)]
    pallas_call x7 -> x5, Pallas kernels: 27.5 us -> 24.2 us  [the longest x2 17.1 us: apply_tiles(): pl.pallas_call(functools.partial(apply_kernel, slots), grid_spec=pltpu.Pr...]
  transfers between devices with their start and end apart: 18 -> 16, of which waited for: 9 -> 9; matrix products, arithmetic and copies ran while one was open for 5% -> 5% of each run, Pallas kernels for 16% -> 8%
where the time goes in v6:
time: 302 us; the launch traced here: 301 us
  waiting for transfers between devices  107 us (35%)
  Pallas kernels  58.9 us (20%)
  blocking collectives  57.4 us (19%)
  starting transfers between devices  42.4 us (14%)
  between operations  14.1 us (5%)
  other arithmetic  12.2 us (4%)
  local copies, waits for them, and re-layouts  6.81 us (2%)
    all_to_all x6, waiting for transfers between devices, exchange(): return lax.all_to_all(copies, axis, 0, 0, tiled=True)  68.7 us
    all_to_all x3, blocking collectives, exchange(): return lax.all_to_all(copies, axis, 0, 0, tiled=True)  45 us
    all_to_all x6, starting transfers between devices, exchange(): return lax.all_to_all(copies, axis, 0, 0, tiled=True)  27.4 us
    all_gather x1, waiting for transfers between devices, shards(): from_second = lax.all_gather(spread, 'row', axis=0)  24.7 us
    pallas_call x2, Pallas kernels, apply_tiles(): pl.pallas_call(functools.partial(apply_kernel, slots), grid_spec=pltpu.Pr...  17.1 us
    all_to_all x1, blocking collectives, spread_to(): return lax.all_to_all(copies, axis, 0, 0, tiled=True)  12.3 us
    pallas_call x2, Pallas kernels, start_vectors(): pl.pallas_call(functools.partial(vectors_kernel, slots), grid_spec=pltpu....  9.63 us
    all_to_all x1, waiting for transfers between devices, spread_to(): return lax.all_to_all(copies, axis, 0, 0, tiled=True)  8.45 us
  transfers between devices with their start and end apart: 16, of which 9 were waited for; matrix products, arithmetic and copies ran while one was open for 5% of the time, Pallas kernels for 8%

profile of v6, /device:TPU:0, one launch (start us, length us, event | category | flops | bytes accessed | tf_op | source)
XLA Modules:
  0.0 300.7 jit_solution(12719523212418061967)
XLA Ops:
  15.9 12.3 %all_to_all.55 = bf16[8,80,256]{2,1,0:T(8,128)(2,1)S(1)} all-to-all(bf16[8,80,256]{2,1,0:T(8,128)(2,1)S(1)} %broadcast_in_dim.68), channel_id=1, replica_groups=mesh['row'=8,'col'=16] {'row'}, dimensions={0} | all-to-all | bytes 655360 | tf_op jit(solution)/shard_map/all_to_all | solution.py:396
  29.3 8.2 %all-to-all-start.1 = ((bf16[16,80,256]{2,1,0:T(8,128)(2,1)}), bf16[16,80,256]{2,1,0:T(8,128)(2,1)S(1)}, u32[]{:S(2)}, u32[]{:S(2)}) async-start(bf16[16,80,256]{2,1,0:T(8,128)(2,1)} %broadcast_in_dim.69), calls=%async_computation.1 | async-start | bytes 1310720 | tf_op jit(solution)/shard_map/all_to_all | solution.py:396
  41.9 8.4 %all-to-all-done.1 = bf16[16,80,256]{2,1,0:T(8,128)(2,1)S(1)} async-done(((bf16[16,80,256]{2,1,0:T(8,128)(2,1)}), bf16[16,80,256]{2,1,0:T(8,128)(2,1)S(1)}, u32[]{:S(2)}, u32[]{:S(2)}) %all-to-all-start.1) | async-done | bytes 655392 | tf_op jit(solution)/shard_map/all_to_all | solution.py:396
  67.1 5.3 %assign_tasks.1.lists = s32[48]{0:T(128)S(1)} custom-call(s32[1]{0:T(128)} %bitcast.6.here, f32[16,128]{1,0:T(8,128)S(1)} %slice_convert_fusion.table), custom_call_target="tpu_custom_call" | custom-call | tf_op jit(solution)/shard_map/assign_tasks/pallas_call | solution.py:470
  72.4 4.7 %pad_maximum_fusion.right.block = bf16[8,1024,256]{2,1,0:T(8,128)(2,1)} fusion(bf16[4,1024,256]{2,1,0:T(8,128)(2,1)} %collective-permute-done.4, bf16[4,1024,256]{2,1,0:T(8,128)(2,1)} %pad_maximum_fusion.1), kind=kLoop, calls=%fused_computation.1 | loop fusion | flops 2097152 | bytes 8388608 | tf_op jit(solution)/shard_map/concatenate | solution.py:534
  82.0 4.6 %all-gather.5.cloned.1.call-done = bf16[16384,256]{1,0:T(8,128)(2,1)} async-done(((bf16[1024,256]{1,0:T(8,128)(2,1)}), bf16[16384,256]{1,0:T(8,128)(2,1)}) %all-gather.5.cloned.1.call-update) | async-done | bytes 8388624 | tf_op jit(solution)/shard_map/all_gather | solution.py:488
  86.7 8.3 %form_tiles.1 = (bf16[8,1024,1024]{2,1,0:T(8,128)(2,1)}, f32[128,1,1152]{2,1,0:T(1,128)}) custom-call(s32[48]{0:T(128)} %copy-done.9, bf16[16,1024,256]{2,1,0:T(8,128)(2,1)} %bitcast.21, bf16[8,1024,256]{2,1,0:T(8,128)(2,1)} %pad_maximum_fusion.right.block, f32[32,128]{1,0:T(8,128)} %copy-done.8), custom_call_target="tpu_custom_call" | custom-call | tf_op jit(solution)/shard_map/form_tiles/pallas_call | solution.py:272
  95.0 23.4 %all_to_all.56.parts = f32[128,1,1152]{2,1,0:T(1,128)S(1)} all-to-all(f32[128,1,1152]{2,1,0:T(1,128)} %get-tuple-element.50), channel_id=1, replica_groups=mesh['row'=8,'col'=16] {'row','col'}, dimensions={0} | all-to-all | bytes 1179648 | tf_op jit(solution)/shard_map/all_to_all | solution.py:400
  119.7 4.6 %all-to-all-start.5 = ((f32[128,1,1152]{2,1,0:T(1,128)}), f32[128,1,1152]{2,1,0:T(1,128)S(1)}, u32[]{:S(2)}, u32[]{:S(2)}) async-start(f32[128,1,1152]{2,1,0:T(1,128)} %get-tuple-element.54), calls=%async_computation.5 | async-start | bytes 1179648 | tf_op jit(solution)/shard_map/all_to_all | solution.py:400
  124.4 4.6 %start_vectors.3.right = f32[8,64,1024]{2,1,0:T(8,128)} custom-call(s32[48]{0:T(128)} %copy-done.9, bf16[8,1024,256]{2,1,0:T(8,128)(2,1)} %pad_maximum_fusion.right.block, bf16[64,256]{1,0:T(8,128)(2,1)} %copy-done.5, f32[64,64]{1,0:T(8,128)} %copy-done.10), custom_call_target="tpu_custom_call" | custom-call | flops 4000000000 | bytes 10000000 | tf_op jit(solution)/shard_map/start_vectors/pallas_call | solution.py:213
  129.0 5.0 %start_vectors.2.left = f32[8,64,1024]{2,1,0:T(8,128)} custom-call(s32[48]{0:T(128)} %copy-done.9, bf16[16,1024,256]{2,1,0:T(8,128)(2,1)} %bitcast.22, bf16[64,256]{1,0:T(8,128)(2,1)} %copy-done.5, f32[64,64]{1,0:T(8,128)} %copy-done.10), custom_call_target="tpu_custom_call" | custom-call | flops 4000000000 | bytes 10000000 | tf_op jit(solution)/shard_map/start_vectors/pallas_call | solution.py:213
  134.0 4.6 %all-to-all-done.5.rest_0_.rest_1_.gram_rows = f32[128,1,1152]{2,1,0:T(1,128)S(1)} async-done(((f32[128,1,1152]{2,1,0:T(1,128)}), f32[128,1,1152]{2,1,0:T(1,128)S(1)}, u32[]{:S(2)}, u32[]{:S(2)}) %all-to-all-start.5) | async-done | bytes 589856 | tf_op jit(solution)/shard_map/all_to_all | solution.py:400
  139.4 8.7 %apply_tiles.2 = (bf16[16,64,1024]{2,1,0:T(8,128)(2,1)}, bf16[8,64,1024]{2,1,0:T(8,128)(2,1)}) custom-call(s32[48]{0:T(128)} %copy-done.9, bf16[8,1024,1024]{2,1,0:T(8,128)(2,1)} %get-tuple-element.52.tile, f32[8,64,1024]{2,1,0:T(8,128)} %start_vectors.2.left, f32[8,64,1024]{2,1,0:T(8,128)} %start_vectors.3.right, f32[128,1,1152]{2,1,0:T(1,128)} %copy-done.1, ...), custom_call_target="tpu_custom_call" | custom-call | tf_op jit(solution)/shard_map/apply_tiles/pallas_call | solution.py:376
  148.1 4.4 %all-to-all-start.6 = ((bf16[16,64,1024]{2,1,0:T(8,128)(2,1)}), bf16[16,64,1024]{2,1,0:T(8,128)(2,1)}, u32[]{:S(2)}, u32[]{:S(2)}) async-start(bf16[16,64,1024]{2,1,0:T(8,128)(2,1)} %get-tuple-element.55), calls=%async_computation.6 | async-start | bytes 4194304 | tf_op jit(solution)/shard_map/all_to_all | solution.py:400
  156.4 27.0 %all-to-all-done.6.first_parts = bf16[16,64,1024]{2,1,0:T(8,128)(2,1)} async-done(((bf16[16,64,1024]{2,1,0:T(8,128)(2,1)}), bf16[16,64,1024]{2,1,0:T(8,128)(2,1)}, u32[]{:S(2)}, u32[]{:S(2)}) %all-to-all-start.6) | async-done | bytes 2097184 | tf_op jit(solution)/shard_map/all_to_all | solution.py:400
  183.4 3.9 %between.1 = (bf16[16,64,1024]{2,1,0:T(8,128)(2,1)}, bf16[64,1024]{1,0:T(8,128)(2,1)}) custom-call(f32[64,1024]{1,0:T(8,128)} %fusion.own_part, bf16[16,64,1024]{2,1,0:T(8,128)(2,1)} %all-to-all-done.6.first_parts, bf16[64,1024]{1,0:T(8,128)(2,1)} %bitcast.26, f32[1,1024]{1,0:T(1,128)} %copy-done.6, f32[64,64]{1,0:T(8,128)} %copy-done.3), custom_call_target="tpu_custom_call" | custom-call | tf_op jit(solution)/shard_map/between/pallas_call | solution.py:182
  187.2 6.8 %all-to-all-start.7 = ((bf16[16,64,1024]{2,1,0:T(8,128)(2,1)}), bf16[16,64,1024]{2,1,0:T(8,128)(2,1)}, u32[]{:S(2)}, u32[]{:S(2)}) async-start(bf16[16,64,1024]{2,1,0:T(8,128)(2,1)} %get-tuple-element.58), calls=%async_computation.8 | async-start | bytes 4194304 | tf_op jit(solution)/shard_map/all_to_all | solution.py:400
  194.8 24.7 %all-gather.7.cloned.1.call-done = bf16[512,1024]{1,0:T(8,128)(2,1)} async-done(((bf16[64,1024]{1,0:T(8,128)(2,1)}), bf16[512,1024]{1,0:T(8,128)(2,1)}) %all-gather.7.cloned.1.call-update) | async-done | bytes 1048592 | tf_op jit(solution)/shard_map/all_gather | solution.py:563
  219.6 4.9 %all-to-all-done.7.left = bf16[16,64,1024]{2,1,0:T(8,128)(2,1)} async-done(((bf16[16,64,1024]{2,1,0:T(8,128)(2,1)}), bf16[16,64,1024]{2,1,0:T(8,128)(2,1)}, u32[]{:S(2)}, u32[]{:S(2)}) %all-to-all-start.7) | async-done | bytes 2097184 | tf_op jit(solution)/shard_map/all_to_all | solution.py:400
  224.5 8.5 %apply_tiles.3 = (bf16[16,64,1024]{2,1,0:T(8,128)(2,1)}, bf16[8,64,1024]{2,1,0:T(8,128)(2,1)}) custom-call(s32[48]{0:T(128)} %copy-done.9, bf16[8,1024,1024]{2,1,0:T(8,128)(2,1)} %get-tuple-element.52.tile, bf16[16,64,1024]{2,1,0:T(8,128)(2,1)} %all-to-all-done.7.left, bf16[8,64,1024]{2,1,0:T(8,128)(2,1)} %bitcast.25), custom_call_target="tpu_custom_call" | custom-call | tf_op jit(solution)/shard_map/apply_tiles/pallas_call | solution.py:376
  233.0 4.6 %all-to-all-start.8 = ((bf16[16,64,1024]{2,1,0:T(8,128)(2,1)}), bf16[16,64,1024]{2,1,0:T(8,128)(2,1)}, u32[]{:S(2)}, u32[]{:S(2)}) async-start(bf16[16,64,1024]{2,1,0:T(8,128)(2,1)} %get-tuple-element.59), calls=%async_computation.9 | async-start | bytes 4194304 | tf_op jit(solution)/shard_map/all_to_all | solution.py:400
  238.1 28.4 %all-to-all-done.8.first_parts = bf16[16,64,1024]{2,1,0:T(8,128)(2,1)} async-done(((bf16[16,64,1024]{2,1,0:T(8,128)(2,1)}), bf16[16,64,1024]{2,1,0:T(8,128)(2,1)}, u32[]{:S(2)}, u32[]{:S(2)}) %all-to-all-start.8) | async-done | bytes 2097184 | tf_op jit(solution)/shard_map/all_to_all | solution.py:400
  269.7 9.5 %all_to_all.57.grams = f32[8,32,128]{2,1,0:T(8,128)S(1)} all-to-all(f32[8,32,128]{2,1,0:T(8,128)S(1)} %get-tuple-element.61), channel_id=1, replica_groups=mesh['row'=8,'col'=16] {'row'}, dimensions={0} | all-to-all | bytes 262144 | tf_op jit(solution)/shard_map/all_to_all | solution.py:400
  279.2 12.2 %all_to_all.58.grams = f32[16,32,128]{2,1,0:T(8,128)S(1)} all-to-all(f32[16,32,128]{2,1,0:T(8,128)S(1)} %relay.3), channel_id=1, replica_groups=mesh['row'=8,'col'=16] {'col'}, dimensions={0} | all-to-all | bytes 524288 | tf_op jit(solution)/shard_map/all_to_all | solution.py:400
  (86 shorter events, 48.9 us)
Async XLA Ops:
  6.5 80.1 %all-gather.5.cloned.1.call-start = ((), (), s32[]{:S(2)}) async-start(), calls=%async_computation.15 | async-start | bytes 8912896 | tf_op jit(solution)/shard_map/all_gather | solution.py:488
  8.5 19.7 %collective-permute-start = (bf16[1024,256]{1,0:T(8,128)(2,1)}, bf16[1024,256]{1,0:T(8,128)(2,1)S(1)}, u32[]{:S(2)}, u32[]{:S(2)}) collective-permute-start(bf16[1024,256]{1,0:T(8,128)(2,1)} %multiply_convert_fusion.own), channel_id=1, source_target_pairs={{0,32},{16,48},{32,64},{48,80},{64,96},{80,112},{96,0},{112,16},{1... | collective-permute-start | bytes 1572872 | tf_op jit(solution)/shard_map/ppermute | solution.py:493
  10.1 18.1 %collective-permute-start.1 = (bf16[1024,256]{1,0:T(8,128)(2,1)}, bf16[1024,256]{1,0:T(8,128)(2,1)S(1)}, u32[]{:S(2)}, u32[]{:S(2)}) collective-permute-start(bf16[1024,256]{1,0:T(8,128)(2,1)} %multiply_convert_fusion.own), channel_id=1, source_target_pairs={{0,96},{16,112},{32,0},{48,16},{64,32},{80,48},{96,64},{112,80},{1... | collective-permute-start | bytes 1572872 | tf_op jit(solution)/shard_map/ppermute | solution.py:493
  15.9 26.0 %copy-start.11 = (bf16[1024,256]{1,0:T(8,128)(2,1)S(1)}, bf16[1024,256]{1,0:T(8,128)(2,1)}, u32[]{:S(2)}) copy-start(bf16[1024,256]{1,0:T(8,128)(2,1)} %param.5) | copy-start | bytes 1572868
  15.9 26.0 %copy-start.14 = (f32[256]{0:T(256)S(1)}, f32[256]{0:T(256)}, u32[]{:S(2)}) copy-start(f32[256]{0:T(256)} %param.6) | copy-start | bytes 3076
  29.3 21.2 %copy-start = (bf16[1024,256]{1,0:T(8,128)(2,1)S(1)}, bf16[1024,256]{1,0:T(8,128)(2,1)}, u32[]{:S(2)}) copy-start(bf16[1024,256]{1,0:T(8,128)(2,1)} %multiply_convert_fusion.own) | copy-start | bytes 1572868
  29.3 21.1 %all-to-all-start.1 = ((bf16[16,80,256]{2,1,0:T(8,128)(2,1)}), bf16[16,80,256]{2,1,0:T(8,128)(2,1)S(1)}, u32[]{:S(2)}, u32[]{:S(2)}) async-start(bf16[16,80,256]{2,1,0:T(8,128)(2,1)} %broadcast_in_dim.69), calls=%async_computation.1 | async-start | bytes 1310720 | tf_op jit(solution)/shard_map/all_to_all | solution.py:396
  37.5 14.5 %collective-permute-start.2 = (bf16[512,256]{1,0:T(8,128)(2,1)S(1)}, bf16[512,256]{1,0:T(8,128)(2,1)}, u32[]{:S(2)}, u32[]{:S(2)}) collective-permute-start(bf16[512,256]{1,0:T(8,128)(2,1)S(1)} %slice.12), channel_id=1, source_target_pairs={{0,32},{16,48},{32,64},{48,80},{64,96},{80,112},{96,0},{112,16},{1... | collective-permute-start | bytes 786440 | tf_op jit(solution)/shard_map/ppermute | solution.py:493
  39.7 12.3 %collective-permute-start.3 = (bf16[512,256]{1,0:T(8,128)(2,1)S(1)}, bf16[512,256]{1,0:T(8,128)(2,1)}, u32[]{:S(2)}, u32[]{:S(2)}) collective-permute-start(bf16[512,256]{1,0:T(8,128)(2,1)S(1)} %slice.13), channel_id=1, source_target_pairs={{0,96},{16,112},{32,0},{48,16},{64,32},{80,48},{96,64},{112,80},{1... | collective-permute-start | bytes 786440 | tf_op jit(solution)/shard_map/ppermute | solution.py:493
  50.5 8.6 %copy-start.5 = (bf16[64,256]{1,0:T(8,128)(2,1)}, bf16[64,256]{1,0:T(8,128)(2,1)S(1)}, u32[]{:S(2)}) copy-start(bf16[64,256]{1,0:T(8,128)(2,1)S(1)} %slice.18.seeds) | copy-start | bytes 98308
  52.0 9.5 %all-to-all-start.2 = ((f32[8,32,128]{2,1,0:T(8,128)}), f32[8,32,128]{2,1,0:T(8,128)S(1)}, u32[]{:S(2)}, u32[]{:S(2)}) async-start(f32[8,32,128]{2,1,0:T(8,128)} %get-tuple-element.40), calls=%async_computation.2 | async-start | bytes 262144 | tf_op jit(solution)/shard_map/all_to_all | solution.py:400
  61.5 10.9 %collective-permute-start.4 = (bf16[4,1024,256]{2,1,0:T(8,128)(2,1)}, bf16[4,1024,256]{2,1,0:T(8,128)(2,1)}, u32[]{:S(2)}, u32[]{:S(2)}) collective-permute-start(bf16[4,1024,256]{2,1,0:T(8,128)(2,1)} %pad_maximum_fusion.1), channel_id=1, source_target_pairs={{0,16},{16,0},{32,48},{48,32},{64,80},{80,64},{96,112},{112,96},{1... | collective-permute-start | bytes 6291464 | tf_op jit(solution)/shard_map/ppermute | solution.py:529
  63.5 15.0 %all-to-all-start.3 = ((f32[16,32,128]{2,1,0:T(8,128)}), f32[16,32,128]{2,1,0:T(8,128)S(1)}, u32[]{:S(2)}, u32[]{:S(2)}) async-start(f32[16,32,128]{2,1,0:T(8,128)} %relay.2), calls=%async_computation.3 | async-start | bytes 524288 | tf_op jit(solution)/shard_map/all_to_all | solution.py:400
  72.4 4.7 %copy-start.9 = (s32[48]{0:T(128)}, s32[48]{0:T(128)S(1)}, u32[]{:S(2)}) copy-start(s32[48]{0:T(128)S(1)} %assign_tasks.1.lists) | copy-start | bytes 580
  82.0 13.0 %copy-start.10 = (f32[64,64]{1,0:T(8,128)}, f32[64,64]{1,0:T(8,128)S(1)}, u32[]{:S(2)}) copy-start(f32[64,64]{1,0:T(8,128)S(1)} %get-tuple-element.53.factor) | copy-start | bytes 49156
  119.7 32.9 %copy-start.6 = (f32[1,1024]{1,0:T(1,128)}, f32[1,1024]{1,0:T(1,128)S(1)}, u32[]{:S(2)}) copy-start(f32[1,1024]{1,0:T(1,128)S(1)} %get-tuple-element.51.root) | copy-start | bytes 12292
  119.7 18.9 %all-to-all-start.5 = ((f32[128,1,1152]{2,1,0:T(1,128)}), f32[128,1,1152]{2,1,0:T(1,128)S(1)}, u32[]{:S(2)}, u32[]{:S(2)}) async-start(f32[128,1,1152]{2,1,0:T(1,128)} %get-tuple-element.54), calls=%async_computation.5 | async-start | bytes 1179648 | tf_op jit(solution)/shard_map/all_to_all | solution.py:400
  124.3 59.1 %reduce-scatter.3.cloned.1.call-start = ((), (), s32[]{:S(2)}) async-start(), calls=%async_computation.13 | async-start | bytes 1179648 | tf_op jit(solution)/shard_map/reduce_scatter | solution.py:557
  148.1 35.2 %all-to-all-start.6 = ((bf16[16,64,1024]{2,1,0:T(8,128)(2,1)}), bf16[16,64,1024]{2,1,0:T(8,128)(2,1)}, u32[]{:S(2)}, u32[]{:S(2)}) async-start(bf16[16,64,1024]{2,1,0:T(8,128)(2,1)} %get-tuple-element.55), calls=%async_computation.6 | async-start | bytes 4194304 | tf_op jit(solution)/shard_map/all_to_all | solution.py:400
  187.2 37.3 %all-to-all-start.7 = ((bf16[16,64,1024]{2,1,0:T(8,128)(2,1)}), bf16[16,64,1024]{2,1,0:T(8,128)(2,1)}, u32[]{:S(2)}, u32[]{:S(2)}) async-start(bf16[16,64,1024]{2,1,0:T(8,128)(2,1)} %get-tuple-element.58), calls=%async_computation.8 | async-start | bytes 4194304 | tf_op jit(solution)/shard_map/all_to_all | solution.py:400
  194.1 25.5 %all-gather.7.cloned.1.call-start = ((), (), s32[]{:S(2)}) async-start(), calls=%async_computation.16 | async-start | bytes 1179648 | tf_op jit(solution)/shard_map/all_gather | solution.py:563
  194.8 71.7 %reduce-scatter.5.cloned.1.call-start = ((), (), s32[]{:S(2)}) async-start(), calls=%async_computation.14 | async-start | bytes 1179648 | tf_op jit(solution)/shard_map/reduce_scatter | solution.py:557
  233.0 33.5 %all-to-all-start.8 = ((bf16[16,64,1024]{2,1,0:T(8,128)(2,1)}), bf16[16,64,1024]{2,1,0:T(8,128)(2,1)}, u32[]{:S(2)}, u32[]{:S(2)}) async-start(bf16[16,64,1024]{2,1,0:T(8,128)(2,1)} %get-tuple-element.59), calls=%async_computation.9 | async-start | bytes 4194304 | tf_op jit(solution)/shard_map/all_to_all | solution.py:400
  237.6 28.9 %copy-start.7 = (f32[1,1024]{1,0:T(1,128)S(1)}, f32[1,1024]{1,0:T(1,128)}, u32[]{:S(2)}) copy-start(f32[1,1024]{1,0:T(1,128)} %copy-done.6) | copy-start | bytes 12292
  (7 other events, 9.9 us)
Sparse Core Ops, SparseCore 0:
  9.5 77.1 all-gather.4
  148.3 32.0 reduce-scatter.2
  196.6 22.9 all-gather.6
  233.1 28.8 reduce-scatter.4

commit v7 on v6

--- a/solution.py
+++ b/solution.py
@@ -16,6 +16,10 @@
 RIDGE = 1e-6
 
 
+def weigh(block, scale):
+    return (block.astype(jnp.float32) * scale[...]).astype(jnp.bfloat16)
+
+
 def lane_sums(values):
     part = values[:, :128]
     for start in range(128, values.shape[1], 128):
@@ -42,6 +46,14 @@
     )
     left_half = jnp.sum(half_squares(left), axis=1, keepdims=True)
     return jnp.exp2(dots * LOG2E - left_half - right_half)
+
+
+def fold(block):
+    return jnp.concatenate([block[i : i + 8, :] for i in range(0, block.shape[0], 8)], axis=1)
+
+
+def unfold(lines):
+    return jnp.concatenate([lines[:, i : i + 32] for i in range(0, lines.shape[1], 32)], axis=0)
 
 
 def packed_gram(vectors):
@@ -53,13 +65,22 @@
         preferred_element_type=jnp.float32,
     )
     half = gram.shape[0] // 2
-    return jnp.concatenate([gram[:half], gram[half:]], axis=1)
+    quarters = (gram[:half, :half], gram[half:, :half], gram[half:, half:])
+    return jnp.concatenate([fold(quarter) for quarter in quarters], axis=0)
 
 
 def inverse_factor(packed, ridge):
-    half, width = packed.shape
-    size = 2 * half
-    state = jnp.concatenate([packed, pltpu.roll(packed, size, 1)], axis=0)
+    width = packed.shape[1]
+    size = width // 2
+    upper, lower_left, lower = (unfold(packed[i : i + 8, :]) for i in (0, 8, 16))
+    filler = jnp.zeros((size // 2, size), jnp.float32)
+    state = jnp.concatenate(
+        [
+            jnp.concatenate([upper, lower_left.T, filler], axis=1),
+            jnp.concatenate([lower_left, lower, filler], axis=1),
+        ],
+        axis=0,
+    )
     row_id = lax.broadcasted_iota(jnp.int32, state.shape, 0)
     lane_id = lax.broadcasted_iota(jnp.int32, state.shape, 1)
     state = jnp.where(lane_id < size, state, jnp.where(lane_id - size == row_id, 1.0, 0.0))
@@ -140,12 +161,12 @@
 
 
 def later_factor(lines, vecs):
-    half, width = vecs // 2, 2 * vecs
+    height, width = 3 * vecs // 8, 2 * vecs
     place = lines.shape[2] // width - 1
     return pl.pallas_call(
         later_factor_kernel,
         grid=(1,),
-        in_specs=[pl.BlockSpec((half, 1, width), lambda s: (0, 0, place))],
+        in_specs=[pl.BlockSpec((height, 1, width), lambda s: (0, 0, place))],
         out_specs=pl.BlockSpec((vecs, vecs), lambda s: (0, 0)),
         out_shape=f32(vecs, vecs),
         compiler_params=pltpu.CompilerParams(vmem_limit_bytes=SMALL),
@@ -201,13 +222,16 @@
     copies[...] = jnp.broadcast_to(jnp.sum(grams[...], axis=0)[None], copies.shape)
 
 
-def vectors_kernel(slots, lists, block, seeds, factor, out):
+def vectors_kernel(slots, lists, block, seeds, factor, *rest):
+    out = rest[-1]
+
     @pl.when(pl.program_id(0) < lists[5 * slots])
     def work():
-        out[0] = transform(factor[...], seed_kernel_rows(seeds[...], block[0]))
-
-
-def start_vectors(lists, slots, source, band, seeds, factor):
+        rows = block[0] if len(rest) == 1 else weigh(block[0], rest[0])
+        out[0] = transform(factor[...], seed_kernel_rows(seeds[...], rows))
+
+
+def start_vectors(lists, slots, source, band, seeds, factor, *scale):
     unused, rows, depth = band.shape
     vecs = seeds.shape[0]
     return pl.pallas_call(
@@ -221,7 +245,8 @@
                 ),
                 pl.BlockSpec((vecs, depth), lambda s, t: (0, 0)),
                 pl.BlockSpec((vecs, vecs), lambda s, t: (0, 0)),
-            ],
+            ]
+            + [pl.BlockSpec(one.shape, lambda s, t: (0, 0)) for one in scale],
             out_specs=pl.BlockSpec(
                 (1, vecs, rows), lambda s, t: (live_step(s, t, slots), 0, 0)
             ),
@@ -232,10 +257,10 @@
             flops=4_000_000_000, bytes_accessed=10_000_000, transcendentals=0
         ),
         name="start_vectors",
-    )(lists, band, seeds, factor)
-
-
-def form_kernel(chunk, slots, lists, left, right, gram, tile, lines):
+    )(lists, band, seeds, factor, *scale)
+
+
+def form_kernel(chunk, slots, lists, left, right, scale, gram, tile, lines):
     step = pl.program_id(0)
     points = left.shape[1]
 
@@ -253,7 +278,8 @@
         col_total = jnp.zeros((1, rows), jnp.float32)
         row_totals = []
         for start in range(0, rows, chunk):
-            value = tile_chunk(left[0, start : start + chunk, :], right_rows, right_half)
+            left_rows = weigh(left[0, start : start + chunk, :], scale)
+            value = tile_chunk(left_rows, right_rows, right_half)
             tile[0, start : start + chunk, :] = value.astype(jnp.bfloat16)
             col_total = col_total + jnp.sum(value, axis=0, keepdims=True)
             row_totals.append(lane_sums(value))
@@ -264,7 +290,7 @@
         lines[right_owner, :, :points] = lines[right_owner, :, :points] + col_total
 
 
-def form_tiles(lists, slots, row_band, col_band, gram):
+def form_tiles(lists, slots, row_band, col_band, scale, gram):
     col_devices, rows, depth = row_band.shape
     line = (col_devices * col_band.shape[0], 1, rows + gram.shape[1])
     firsts, unused, places, owners, live = task_lists(slots)
@@ -281,6 +307,7 @@
                 pl.BlockSpec(
                     (1, rows, depth), lambda s, t: (t[places + live_step(s, t, slots)], 0, 0)
                 ),
+                pl.BlockSpec(scale.shape, lambda s, t: (0, 0)),
                 pl.BlockSpec(gram.shape, lambda s, t: (0, 0)),
             ],
             out_specs=[
@@ -291,7 +318,7 @@
         out_shape=[bf16(slots, rows, rows), f32(*line)],
         compiler_params=pltpu.CompilerParams(vmem_limit_bytes=VMEM),
         name="form_tiles",
-    )(lists, row_band, col_band, gram)
+    )(lists, row_band, col_band, scale, gram)
 
 
 def diagonal_kernel(chunk, own, tile, degree):
@@ -480,12 +507,14 @@
 def shards(points, feature_scale, tile_tasks, task_count, seed_ids):
     rows = points.shape[0]
     vecs = seed_ids.shape[0]
+    packed = (3 * vecs // 8, 2 * vecs)
     row_devices = lax.axis_size("row")
     col_devices = lax.axis_size("col")
     all_devices = row_devices * col_devices
     self_index = lax.axis_index("row") * col_devices + lax.axis_index("col")
     weighted = (points.astype(jnp.float32) * feature_scale[None, :]).astype(jnp.bfloat16)
-    row_band = lax.all_gather(weighted, "col", axis=0)
+    row_band = lax.all_gather(points, "col", axis=0)
+    scale = feature_scale[None, :]
     listed = tile_tasks.reshape(-1)
     slots = listed.shape[0]
 
@@ -519,7 +548,7 @@
     seeds = seed_sum[:vecs]
     table = seed_sum[vecs:, :all_devices].astype(jnp.float32)
     start, grams = call(
-        start_kernel, "start", [f32(vecs, rows), f32(row_devices, vecs // 2, 2 * vecs)]
+        start_kernel, "start", [f32(vecs, rows), f32(row_devices, *packed)]
     )(seeds, weighted)
     across_low, across_high, grams = together(across_low, across_high, grams)
     grams = exchange(grams, "row")
@@ -527,7 +556,7 @@
     mine = jnp.stack([weighted, before, after, across])
     mine, grams = together(mine, grams)
     other = lax.ppermute(mine, "row", [(i, i ^ 1) for i in range(row_devices)])
-    grams = call(relay_kernel, "relay", f32(col_devices, vecs // 2, 2 * vecs))(grams)
+    grams = call(relay_kernel, "relay", f32(col_devices, *packed))(grams)
     grams = exchange(grams, "col")
     lists = assign_tasks(self_index, table, slots, col_devices)
     firsts, seconds, places, unused, unused = task_lists(slots)
@@ -535,16 +564,16 @@
     factor, subspace, later_gram = call(
         first_factor_kernel,
         "first_factor",
-        [f32(vecs, vecs), f32(vecs, rows), f32(vecs // 2, 2 * vecs)],
+        [f32(vecs, vecs), f32(vecs, rows), f32(*packed)],
     )(grams, start, diagonal, own_degree)
 
-    tiles, lines = form_tiles(lists, slots, row_band, col_band, later_gram)
+    tiles, lines = form_tiles(lists, slots, row_band, col_band, scale, later_gram)
     copies, inv_root = call(degree_kernel, "degree", [f32(*lines.shape), f32(1, rows)])(
         own_degree, exchange(lines, ("row", "col"))
     )
     lines = exchange(copies, ("row", "col"))
     roots = lines
-    from_first = start_vectors(lists, slots, firsts, row_band, seeds, factor)
+    from_first = start_vectors(lists, slots, firsts, row_band, seeds, factor, scale)
     from_second = start_vectors(lists, slots, places, col_band, seeds, factor)
     spread = (subspace * inv_root).astype(jnp.bfloat16)
     for iteration in range(ITERS):
@@ -564,10 +593,10 @@
             from_first = exchange(copies, "col")
             roots = None
     subspace, grams = call(
-        last_kernel, "last", [f32(vecs, rows), f32(row_devices, vecs // 2, 2 * vecs)]
+        last_kernel, "last", [f32(vecs, rows), f32(row_devices, *packed)]
     )(own_part, first_parts, second_part, inv_root)
     grams = exchange(grams, "row")
-    grams = call(relay_kernel, "relay", f32(col_devices, vecs // 2, 2 * vecs))(grams)
+    grams = call(relay_kernel, "relay", f32(col_devices, *packed))(grams)
     grams = exchange(grams, "col")
     return call(
         functools.partial(final_kernel, all_devices * rows), "final", f32(vecs, rows)

time: 302 us -> 300 us (level)
  Pallas kernels: 58.9 us -> 48.6 us
  blocking collectives: 57.4 us -> 63.5 us
  waiting for transfers between devices: 107 us -> 112 us
    all_to_all x6, waiting for transfers between devices: 68.7 us -> 76.2 us  [exchange(): return lax.all_to_all(copies, axis, 0, 0, tiled=True)]
    pallas_call x2, Pallas kernels: 17.1 us -> 11.8 us  [apply_tiles(): pl.pallas_call(functools.partial(apply_kernel, slots), grid_spec=pltpu.Pr...]
    all_to_all x3, blocking collectives: 45 us -> 50.3 us  [exchange(): return lax.all_to_all(copies, axis, 0, 0, tiled=True)]
    all_gather x1, waiting for transfers between devices: 4.65 us -> 0.17 us  [shards(): row_band = lax.all_gather(points, 'col', axis=0)]
  transfers between devices with their start and end apart: 16 -> 16, of which waited for: 9 -> 9; matrix products, arithmetic and copies ran while one was open for 5% -> 5% of each run, Pallas kernels for 8% -> 7%
where the time goes in v7:
time: 300 us
  waiting for transfers between devices  112 us (37%)
  blocking collectives  63.5 us (21%)
  Pallas kernels  48.6 us (16%)
  starting transfers between devices  44.3 us (15%)
  between operations  14.1 us (5%)
  other arithmetic  10.3 us (3%)
  local copies, waits for them, and re-layouts  5.49 us (2%)
    all_to_all x6, waiting for transfers between devices, exchange(): return lax.all_to_all(copies, axis, 0, 0, tiled=True)  76.2 us
    all_to_all x3, blocking collectives, exchange(): return lax.all_to_all(copies, axis, 0, 0, tiled=True)  50.3 us
    all_to_all x6, starting transfers between devices, exchange(): return lax.all_to_all(copies, axis, 0, 0, tiled=True)  29.5 us
    all_gather x1, waiting for transfers between devices, shards(): from_second = lax.all_gather(spread, 'row', axis=0)  25.6 us
    all_to_all x1, blocking collectives, spread_to(): return lax.all_to_all(copies, axis, 0, 0, tiled=True)  13.2 us
    pallas_call x2, Pallas kernels, apply_tiles(): pl.pallas_call(functools.partial(apply_kernel, slots), grid_spec=pltpu.Pr...  11.8 us
    all_to_all x1, waiting for transfers between devices, spread_to(): return lax.all_to_all(copies, axis, 0, 0, tiled=True)  8.76 us
    all_to_all x1, starting transfers between devices, spread_to(): return lax.all_to_all(copies, axis, 0, 0, tiled=True)  8.05 us
  transfers between devices with their start and end apart: 16, of which 9 were waited for; matrix products, arithmetic and copies ran while one was open for 5% of the time, Pallas kernels for 7%

profile of v7, /device:TPU:0, one launch (start us, length us, event | category | flops | bytes accessed | tf_op | source)
XLA Modules:
  0.0 300.0 jit_solution(12907933082329474018)
XLA Ops:
  14.7 13.2 %all_to_all.55 = bf16[8,80,256]{2,1,0:T(8,128)(2,1)S(1)} all-to-all(bf16[8,80,256]{2,1,0:T(8,128)(2,1)S(1)} %broadcast_in_dim.71), channel_id=1, replica_groups=mesh['row'=8,'col'=16] {'row'}, dimensions={0} | all-to-all | bytes 655360 | tf_op jit(solution)/shard_map/all_to_all | solution.py:423
  29.0 8.0 %all-to-all-start.1 = ((bf16[16,80,256]{2,1,0:T(8,128)(2,1)}), bf16[16,80,256]{2,1,0:T(8,128)(2,1)S(1)}, u32[]{:S(2)}, u32[]{:S(2)}) async-start(bf16[16,80,256]{2,1,0:T(8,128)(2,1)} %broadcast_in_dim.72), calls=%async_computation.1 | async-start | bytes 1310720 | tf_op jit(solution)/shard_map/all_to_all | solution.py:423
  41.2 8.8 %all-to-all-done.1 = bf16[16,80,256]{2,1,0:T(8,128)(2,1)S(1)} async-done(((bf16[16,80,256]{2,1,0:T(8,128)(2,1)}), bf16[16,80,256]{2,1,0:T(8,128)(2,1)S(1)}, u32[]{:S(2)}, u32[]{:S(2)}) %all-to-all-start.1) | async-done | bytes 655392 | tf_op jit(solution)/shard_map/all_to_all | solution.py:423
  61.9 5.3 %assign_tasks.1.lists = s32[48]{0:T(128)S(1)} custom-call(s32[1]{0:T(128)} %bitcast.6.here, f32[16,128]{1,0:T(8,128)S(1)} %slice_convert_fusion.table), custom_call_target="tpu_custom_call" | custom-call | tf_op jit(solution)/shard_map/assign_tasks/pallas_call | solution.py:497
  68.0 3.5 %all-to-all-start.3 = ((f32[16,24,128]{2,1,0:T(8,128)}), f32[16,24,128]{2,1,0:T(8,128)S(1)}, u32[]{:S(2)}, u32[]{:S(2)}) async-start(f32[16,24,128]{2,1,0:T(8,128)} %relay.2), calls=%async_computation.3 | async-start | bytes 393216 | tf_op jit(solution)/shard_map/all_to_all | solution.py:427
  71.5 4.7 %pad_maximum_fusion.right.block = bf16[8,1024,256]{2,1,0:T(8,128)(2,1)} fusion(bf16[4,1024,256]{2,1,0:T(8,128)(2,1)} %collective-permute-done.4, bf16[4,1024,256]{2,1,0:T(8,128)(2,1)} %pad_maximum_fusion.1), kind=kLoop, calls=%fused_computation.1 | loop fusion | flops 2097152 | bytes 8388608 | tf_op jit(solution)/shard_map/concatenate | solution.py:563
  76.2 5.7 %all-to-all-done.3.grams = f32[16,24,128]{2,1,0:T(8,128)S(1)} async-done(((f32[16,24,128]{2,1,0:T(8,128)}), f32[16,24,128]{2,1,0:T(8,128)S(1)}, u32[]{:S(2)}, u32[]{:S(2)}) %all-to-all-start.3) | async-done | bytes 196640 | tf_op jit(solution)/shard_map/all_to_all | solution.py:427
  85.8 5.5 %form_tiles.1 = (bf16[8,1024,1024]{2,1,0:T(8,128)(2,1)}, f32[128,1,1152]{2,1,0:T(1,128)}) custom-call(s32[48]{0:T(128)} %copy-done.8, bf16[16,1024,256]{2,1,0:T(8,128)(2,1)} %bitcast.22, bf16[8,1024,256]{2,1,0:T(8,128)(2,1)} %pad_maximum_fusion.right.block, f32[1,256]{1,0:T(1,128)} %bitcast.28, f32[24,128]{1,0:T(8,128)} %copy-done.7), custom_call_target="tpu_custom_call" | custom-call | tf_op jit(solution)/shard_map/form_tiles/pallas_call | solution.py:298
  91.3 25.6 %all_to_all.56.parts = f32[128,1,1152]{2,1,0:T(1,128)S(1)} all-to-all(f32[128,1,1152]{2,1,0:T(1,128)} %get-tuple-element.50), channel_id=1, replica_groups=mesh['row'=8,'col'=16] {'row','col'}, dimensions={0} | all-to-all | bytes 1179648 | tf_op jit(solution)/shard_map/all_to_all | solution.py:427
  118.1 4.6 %all-to-all-start.5 = ((f32[128,1,1152]{2,1,0:T(1,128)}), f32[128,1,1152]{2,1,0:T(1,128)S(1)}, u32[]{:S(2)}, u32[]{:S(2)}) async-start(f32[128,1,1152]{2,1,0:T(1,128)} %get-tuple-element.54), calls=%async_computation.5 | async-start | bytes 1179648 | tf_op jit(solution)/shard_map/all_to_all | solution.py:427
  122.8 3.4 %start_vectors.3.right = f32[8,64,1024]{2,1,0:T(8,128)} custom-call(s32[48]{0:T(128)} %copy-done.8, bf16[8,1024,256]{2,1,0:T(8,128)(2,1)} %pad_maximum_fusion.right.block, bf16[64,256]{1,0:T(8,128)(2,1)} %copy-done.4, f32[64,64]{1,0:T(8,128)} %copy-done.9), custom_call_target="tpu_custom_call" | custom-call | flops 4000000000 | bytes 10000000 | tf_op jit(solution)/shard_map/start_vectors/pallas_call | solution.py:237
  126.2 3.4 %start_vectors.2.left = f32[8,64,1024]{2,1,0:T(8,128)} custom-call(s32[48]{0:T(128)} %copy-done.8, bf16[16,1024,256]{2,1,0:T(8,128)(2,1)} %bitcast.23, bf16[64,256]{1,0:T(8,128)(2,1)} %copy-done.4, f32[64,64]{1,0:T(8,128)} %copy-done.9, f32[1,256]{1,0:T(1,128)} %bitcast.29), custom_call_target="tpu_custom_call" | custom-call | flops 4000000000 | bytes 10000000 | tf_op jit(solution)/shard_map/start_vectors/pallas_call | solution.py:237
  129.7 7.4 %all-to-all-done.5.rest_0_.rest_1_.gram_rows = f32[128,1,1152]{2,1,0:T(1,128)S(1)} async-done(((f32[128,1,1152]{2,1,0:T(1,128)}), f32[128,1,1152]{2,1,0:T(1,128)S(1)}, u32[]{:S(2)}, u32[]{:S(2)}) %all-to-all-start.5) | async-done | bytes 589856 | tf_op jit(solution)/shard_map/all_to_all | solution.py:427
  137.9 6.0 %apply_tiles.2 = (bf16[16,64,1024]{2,1,0:T(8,128)(2,1)}, bf16[8,64,1024]{2,1,0:T(8,128)(2,1)}) custom-call(s32[48]{0:T(128)} %copy-done.8, bf16[8,1024,1024]{2,1,0:T(8,128)(2,1)} %get-tuple-element.52.tile, f32[8,64,1024]{2,1,0:T(8,128)} %start_vectors.2.left, f32[8,64,1024]{2,1,0:T(8,128)} %start_vectors.3.right, f32[128,1,1152]{2,1,0:T(1,128)} %copy-done, ...), custom_call_target="tpu_custom_call" | custom-call | tf_op jit(solution)/shard_map/apply_tiles/pallas_call | solution.py:403
  143.9 5.5 %all-to-all-start.6 = ((bf16[16,64,1024]{2,1,0:T(8,128)(2,1)}), bf16[16,64,1024]{2,1,0:T(8,128)(2,1)}, u32[]{:S(2)}, u32[]{:S(2)}) async-start(bf16[16,64,1024]{2,1,0:T(8,128)(2,1)} %get-tuple-element.55), calls=%async_computation.6 | async-start | bytes 4194304 | tf_op jit(solution)/shard_map/all_to_all | solution.py:427
  153.4 26.8 %all-to-all-done.6.first_parts = bf16[16,64,1024]{2,1,0:T(8,128)(2,1)} async-done(((bf16[16,64,1024]{2,1,0:T(8,128)(2,1)}), bf16[16,64,1024]{2,1,0:T(8,128)(2,1)}, u32[]{:S(2)}, u32[]{:S(2)}) %all-to-all-start.6) | async-done | bytes 2097184 | tf_op jit(solution)/shard_map/all_to_all | solution.py:427
  180.2 3.9 %between.1 = (bf16[16,64,1024]{2,1,0:T(8,128)(2,1)}, bf16[64,1024]{1,0:T(8,128)(2,1)}) custom-call(f32[64,1024]{1,0:T(8,128)} %fusion.own_part, bf16[16,64,1024]{2,1,0:T(8,128)(2,1)} %all-to-all-done.6.first_parts, bf16[64,1024]{1,0:T(8,128)(2,1)} %bitcast.27, f32[1,1024]{1,0:T(1,128)} %copy-done.5, f32[64,64]{1,0:T(8,128)} %copy-done.2), custom_call_target="tpu_custom_call" | custom-call | tf_op jit(solution)/shard_map/between/pallas_call | solution.py:203
  184.0 5.8 %all-to-all-start.7 = ((bf16[16,64,1024]{2,1,0:T(8,128)(2,1)}), bf16[16,64,1024]{2,1,0:T(8,128)(2,1)}, u32[]{:S(2)}, u32[]{:S(2)}) async-start(bf16[16,64,1024]{2,1,0:T(8,128)(2,1)} %get-tuple-element.58), calls=%async_computation.8 | async-start | bytes 4194304 | tf_op jit(solution)/shard_map/all_to_all | solution.py:427
  190.6 25.6 %all-gather.7.cloned.1.call-done = bf16[512,1024]{1,0:T(8,128)(2,1)} async-done(((bf16[64,1024]{1,0:T(8,128)(2,1)}), bf16[512,1024]{1,0:T(8,128)(2,1)}) %all-gather.7.cloned.1.call-update) | async-done | bytes 1048592 | tf_op jit(solution)/shard_map/all_gather | solution.py:592
  219.5 5.8 %apply_tiles.3 = (bf16[16,64,1024]{2,1,0:T(8,128)(2,1)}, bf16[8,64,1024]{2,1,0:T(8,128)(2,1)}) custom-call(s32[48]{0:T(128)} %copy-done.8, bf16[8,1024,1024]{2,1,0:T(8,128)(2,1)} %get-tuple-element.52.tile, bf16[16,64,1024]{2,1,0:T(8,128)(2,1)} %all-to-all-done.7.left, bf16[8,64,1024]{2,1,0:T(8,128)(2,1)} %bitcast.26), custom_call_target="tpu_custom_call" | custom-call | tf_op jit(solution)/shard_map/apply_tiles/pallas_call | solution.py:403
  225.3 6.7 %all-to-all-start.8 = ((bf16[16,64,1024]{2,1,0:T(8,128)(2,1)}), bf16[16,64,1024]{2,1,0:T(8,128)(2,1)}, u32[]{:S(2)}, u32[]{:S(2)}) async-start(bf16[16,64,1024]{2,1,0:T(8,128)(2,1)} %get-tuple-element.59), calls=%async_computation.9 | async-start | bytes 4194304 | tf_op jit(solution)/shard_map/all_to_all | solution.py:427
  232.6 29.9 %all-to-all-done.8.first_parts = bf16[16,64,1024]{2,1,0:T(8,128)(2,1)} async-done(((bf16[16,64,1024]{2,1,0:T(8,128)(2,1)}), bf16[16,64,1024]{2,1,0:T(8,128)(2,1)}, u32[]{:S(2)}, u32[]{:S(2)}) %all-to-all-start.8) | async-done | bytes 2097184 | tf_op jit(solution)/shard_map/all_to_all | solution.py:427
  265.7 10.3 %all_to_all.57.grams = f32[8,24,128]{2,1,0:T(8,128)S(1)} all-to-all(f32[8,24,128]{2,1,0:T(8,128)S(1)} %get-tuple-element.61), channel_id=1, replica_groups=mesh['row'=8,'col'=16] {'row'}, dimensions={0} | all-to-all | bytes 196608 | tf_op jit(solution)/shard_map/all_to_all | solution.py:427
  276.0 14.4 %all_to_all.58.grams = f32[16,24,128]{2,1,0:T(8,128)S(1)} all-to-all(f32[16,24,128]{2,1,0:T(8,128)S(1)} %relay.3), channel_id=1, replica_groups=mesh['row'=8,'col'=16] {'col'}, dimensions={0} | all-to-all | bytes 393216 | tf_op jit(solution)/shard_map/all_to_all | solution.py:427
  (86 shorter events, 46.2 us)
Async XLA Ops:
  6.5 79.3 %all-gather.5.cloned.1.call-start = ((), (), s32[]{:S(2)}) async-start(), calls=%async_computation.15 | async-start | bytes 8912896 | tf_op jit(solution)/shard_map/all_gather | solution.py:516
  8.4 19.5 %collective-permute-start = (bf16[1024,256]{1,0:T(8,128)(2,1)S(1)}, bf16[1024,256]{1,0:T(8,128)(2,1)S(1)}, u32[]{:S(2)}, u32[]{:S(2)}) collective-permute-start(bf16[1024,256]{1,0:T(8,128)(2,1)S(1)} %multiply_convert_fusion.own), channel_id=1, source_target_pairs={{0,32},{16,48},{32,64},{48,80},{64,96},{80,112},{96,0},{112,16},{1... | collective-permute-start | bytes 1572872 | tf_op jit(solution)/shard_map/ppermute | solution.py:522
  10.0 17.9 %collective-permute-start.1 = (bf16[1024,256]{1,0:T(8,128)(2,1)S(1)}, bf16[1024,256]{1,0:T(8,128)(2,1)S(1)}, u32[]{:S(2)}, u32[]{:S(2)}) collective-permute-start(bf16[1024,256]{1,0:T(8,128)(2,1)S(1)} %multiply_convert_fusion.own), channel_id=1, source_target_pairs={{0,96},{16,112},{32,0},{48,16},{64,32},{80,48},{96,64},{112,80},{1... | collective-permute-start | bytes 1572872 | tf_op jit(solution)/shard_map/ppermute | solution.py:522
  14.7 26.4 %copy-start.10 = (bf16[1024,256]{1,0:T(8,128)(2,1)S(1)}, bf16[1024,256]{1,0:T(8,128)(2,1)}, u32[]{:S(2)}) copy-start(bf16[1024,256]{1,0:T(8,128)(2,1)} %param.5) | copy-start | bytes 1572868
  14.7 26.4 %copy-start.14 = (f32[256]{0:T(256)S(1)}, f32[256]{0:T(256)}, u32[]{:S(2)}) copy-start(f32[256]{0:T(256)} %param.6) | copy-start | bytes 3076
  27.9 11.0 %copy-start.11 = (bf16[1024,256]{1,0:T(8,128)(2,1)}, bf16[1024,256]{1,0:T(8,128)(2,1)S(1)}, u32[]{:S(2)}) copy-start(bf16[1024,256]{1,0:T(8,128)(2,1)S(1)} %collective-permute-done.1) | copy-start | bytes 1572868
  29.0 21.0 %all-to-all-start.1 = ((bf16[16,80,256]{2,1,0:T(8,128)(2,1)}), bf16[16,80,256]{2,1,0:T(8,128)(2,1)S(1)}, u32[]{:S(2)}, u32[]{:S(2)}) async-start(bf16[16,80,256]{2,1,0:T(8,128)(2,1)} %broadcast_in_dim.72), calls=%async_computation.1 | async-start | bytes 1310720 | tf_op jit(solution)/shard_map/all_to_all | solution.py:423
  37.0 14.5 %collective-permute-start.2 = (bf16[512,256]{1,0:T(8,128)(2,1)S(1)}, bf16[512,256]{1,0:T(8,128)(2,1)}, u32[]{:S(2)}, u32[]{:S(2)}) collective-permute-start(bf16[512,256]{1,0:T(8,128)(2,1)S(1)} %slice.12), channel_id=1, source_target_pairs={{0,32},{16,48},{32,64},{48,80},{64,96},{80,112},{96,0},{112,16},{1... | collective-permute-start | bytes 786440 | tf_op jit(solution)/shard_map/ppermute | solution.py:522
  39.0 12.6 %collective-permute-start.3 = (bf16[512,256]{1,0:T(8,128)(2,1)}, bf16[512,256]{1,0:T(8,128)(2,1)}, u32[]{:S(2)}, u32[]{:S(2)}) collective-permute-start(bf16[512,256]{1,0:T(8,128)(2,1)} %slice.13), channel_id=1, source_target_pairs={{0,96},{16,112},{32,0},{48,16},{64,32},{80,48},{96,64},{112,80},{1... | collective-permute-start | bytes 786440 | tf_op jit(solution)/shard_map/ppermute | solution.py:522
  50.1 7.5 %copy-start.4 = (bf16[64,256]{1,0:T(8,128)(2,1)}, bf16[64,256]{1,0:T(8,128)(2,1)S(1)}, u32[]{:S(2)}) copy-start(bf16[64,256]{1,0:T(8,128)(2,1)S(1)} %slice.18.seeds) | copy-start | bytes 98308
  51.5 9.2 %all-to-all-start.2 = ((f32[8,24,128]{2,1,0:T(8,128)}), f32[8,24,128]{2,1,0:T(8,128)S(1)}, u32[]{:S(2)}, u32[]{:S(2)}) async-start(f32[8,24,128]{2,1,0:T(8,128)} %get-tuple-element.40), calls=%async_computation.2 | async-start | bytes 196608 | tf_op jit(solution)/shard_map/all_to_all | solution.py:427
  60.7 10.8 %collective-permute-start.4 = (bf16[4,1024,256]{2,1,0:T(8,128)(2,1)}, bf16[4,1024,256]{2,1,0:T(8,128)(2,1)}, u32[]{:S(2)}, u32[]{:S(2)}) collective-permute-start(bf16[4,1024,256]{2,1,0:T(8,128)(2,1)} %pad_maximum_fusion.1), channel_id=1, source_target_pairs={{0,16},{16,0},{32,48},{48,32},{64,80},{80,64},{96,112},{112,96},{1... | collective-permute-start | bytes 6291464 | tf_op jit(solution)/shard_map/ppermute | solution.py:558
  67.3 8.9 %copy-start.8 = (s32[48]{0:T(128)}, s32[48]{0:T(128)S(1)}, u32[]{:S(2)}) copy-start(s32[48]{0:T(128)S(1)} %assign_tasks.1.lists) | copy-start | bytes 580
  68.0 13.9 %all-to-all-start.3 = ((f32[16,24,128]{2,1,0:T(8,128)}), f32[16,24,128]{2,1,0:T(8,128)S(1)}, u32[]{:S(2)}, u32[]{:S(2)}) async-start(f32[16,24,128]{2,1,0:T(8,128)} %relay.2), calls=%async_computation.3 | async-start | bytes 393216 | tf_op jit(solution)/shard_map/all_to_all | solution.py:427
  118.1 31.3 %copy-start.5 = (f32[1,1024]{1,0:T(1,128)}, f32[1,1024]{1,0:T(1,128)S(1)}, u32[]{:S(2)}) copy-start(f32[1,1024]{1,0:T(1,128)S(1)} %get-tuple-element.51.root) | copy-start | bytes 12292
  118.1 18.9 %all-to-all-start.5 = ((f32[128,1,1152]{2,1,0:T(1,128)}), f32[128,1,1152]{2,1,0:T(1,128)S(1)}, u32[]{:S(2)}, u32[]{:S(2)}) async-start(f32[128,1,1152]{2,1,0:T(1,128)} %get-tuple-element.54), calls=%async_computation.5 | async-start | bytes 1179648 | tf_op jit(solution)/shard_map/all_to_all | solution.py:427
  122.8 57.4 %reduce-scatter.3.cloned.1.call-start = ((), (), s32[]{:S(2)}) async-start(), calls=%async_computation.13 | async-start | bytes 1179648 | tf_op jit(solution)/shard_map/reduce_scatter | solution.py:586
  143.9 36.2 %all-to-all-start.6 = ((bf16[16,64,1024]{2,1,0:T(8,128)(2,1)}), bf16[16,64,1024]{2,1,0:T(8,128)(2,1)}, u32[]{:S(2)}, u32[]{:S(2)}) async-start(bf16[16,64,1024]{2,1,0:T(8,128)(2,1)} %get-tuple-element.55), calls=%async_computation.6 | async-start | bytes 4194304 | tf_op jit(solution)/shard_map/all_to_all | solution.py:427
  184.0 35.5 %all-to-all-start.7 = ((bf16[16,64,1024]{2,1,0:T(8,128)(2,1)}), bf16[16,64,1024]{2,1,0:T(8,128)(2,1)}, u32[]{:S(2)}, u32[]{:S(2)}) async-start(bf16[16,64,1024]{2,1,0:T(8,128)(2,1)} %get-tuple-element.58), calls=%async_computation.8 | async-start | bytes 4194304 | tf_op jit(solution)/shard_map/all_to_all | solution.py:427
  189.8 26.4 %all-gather.7.cloned.1.call-start = ((), (), s32[]{:S(2)}) async-start(), calls=%async_computation.16 | async-start | bytes 1179648 | tf_op jit(solution)/shard_map/all_gather | solution.py:592
  190.5 71.9 %reduce-scatter.5.cloned.1.call-start = ((), (), s32[]{:S(2)}) async-start(), calls=%async_computation.14 | async-start | bytes 1179648 | tf_op jit(solution)/shard_map/reduce_scatter | solution.py:586
  225.3 6.8 %copy-start.13 = (bf16[64,1024]{1,0:T(8,128)(2,1)S(1)}, bf16[64,1024]{1,0:T(8,128)(2,1)}, u32[]{:S(2)}) copy-start(bf16[64,1024]{1,0:T(8,128)(2,1)} %get-tuple-element.57) | copy-start | bytes 393220
  225.3 37.1 %all-to-all-start.8 = ((bf16[16,64,1024]{2,1,0:T(8,128)(2,1)}), bf16[16,64,1024]{2,1,0:T(8,128)(2,1)}, u32[]{:S(2)}, u32[]{:S(2)}) async-start(bf16[16,64,1024]{2,1,0:T(8,128)(2,1)} %get-tuple-element.59), calls=%async_computation.9 | async-start | bytes 4194304 | tf_op jit(solution)/shard_map/all_to_all | solution.py:427
  232.1 30.4 %copy-start.6 = (f32[1,1024]{1,0:T(1,128)S(1)}, f32[1,1024]{1,0:T(1,128)}, u32[]{:S(2)}) copy-start(f32[1,1024]{1,0:T(1,128)} %copy-done.5) | copy-start | bytes 12292
  (7 other events, 15.8 us)
Sparse Core Ops, SparseCore 0:
  9.5 76.2 all-gather.4
  144.0 33.9 reduce-scatter.2
  192.3 23.7 all-gather.6
  225.4 35.0 reduce-scatter.4

commit v8 on v7

--- a/solution.py
+++ b/solution.py
@@ -13,7 +13,37 @@
 VMEM = 60 * 1024 * 1024
 SMALL = 24 * 1024 * 1024
 HIGH = lax.Precision.HIGHEST
-RIDGE = 1e-6
+RIDGE = 1e-5
+
+
+def for_each_task(body, lists, slots, counter, in_specs, out_specs, refs):
+    live = lists[5 * slots]
+    counter[0] = 0
+
+    def one(*blocks):
+        step = counter[0]
+        counter[0] = step + 1
+
+        @pl.when(step < live)
+        def work():
+            body(step, *blocks)
+
+    pltpu.emit_pipeline(
+        one, grid=(jnp.maximum(live, 1),), in_specs=in_specs, out_specs=out_specs
+    )(*refs)
+
+
+def task_call(kernel, name, operands, anywhere, out_specs, out_shape):
+    places = [pltpu.SMEM] + [pl.ANY if flag else pltpu.VMEM for flag in anywhere]
+    return pl.pallas_call(
+        kernel,
+        in_specs=[pl.BlockSpec(memory_space=place) for place in places],
+        out_specs=out_specs,
+        out_shape=out_shape,
+        scratch_shapes=[pltpu.SMEM((1,), jnp.int32)],
+        compiler_params=pltpu.CompilerParams(vmem_limit_bytes=VMEM),
+        name=name,
+    )(*operands)
 
 
 def weigh(block, scale):
@@ -346,75 +376,72 @@
     )(own)
 
 
-def apply_kernel(slots, lists, tile, left, right, *rest):
-    step = pl.program_id(0)
-    left_roots, right_roots, to_first, to_second = rest if len(rest) == 4 else (None, None) + rest
-
-    def scaled(vectors, roots):
-        if roots is None:
-            return vectors[0]
-        return (vectors[0] * roots[0, :, : vectors.shape[2]]).astype(jnp.bfloat16)
-
-    def add(out, slot, vectors, contract):
-        product = lax.dot_general(
-            vectors, tile[0], (((1,), (contract,)), ((), ())), preferred_element_type=jnp.float32
-        )
-        out[slot] = (out[slot].astype(jnp.float32) + product).astype(jnp.bfloat16)
-
-    @pl.when(step == 0)
-    def clear():
-        to_first[...] = jnp.zeros_like(to_first)
-        to_second[...] = jnp.zeros_like(to_second)
-
-    @pl.when(step < lists[5 * slots])
-    def work():
-        add(to_second, lists[slots + step], scaled(left, left_roots), 0)
-        add(to_first, lists[step], scaled(right, right_roots), 1)
+def apply_kernel(slots, lists, tiles, from_first, from_second, *rest):
+    roots, (to_first, to_second, counter) = rest[:-3], rest[-3:]
+    rows = tiles.shape[1]
+    to_first[...] = jnp.zeros_like(to_first)
+    to_second[...] = jnp.zeros_like(to_second)
+
+    def body(step, tile, left, right, *task_roots):
+        def scaled(vectors, which):
+            if not task_roots:
+                return vectors[0]
+            return (vectors[0] * task_roots[which][0, :, :rows]).astype(jnp.bfloat16)
+
+        def add(out, slot, vectors, contract):
+            product = lax.dot_general(
+                vectors,
+                tile[0],
+                (((1,), (contract,)), ((), ())),
+                preferred_element_type=jnp.float32,
+            )
+            out[slot] = (out[slot].astype(jnp.float32) + product).astype(jnp.bfloat16)
+
+        add(to_second, lists[slots + step], scaled(left, 0), 0)
+        add(to_first, lists[step], scaled(right, 1), 1)
+
+    def by_task(s):
+        return (s, 0, 0)
+
+    def by_first(s):
+        return (lists[s], 0, 0)
+
+    def by_second(s):
+        return (lists[slots + s], 0, 0)
+
+    def by_owner(side):
+        return lambda s: (lists[3 * slots + 2 * s + side], 0, 0)
+
+    block = (1,) + from_first.shape[1:]
+    for_each_task(
+        body,
+        lists,
+        slots,
+        counter,
+        [
+            pl.BlockSpec((1, rows, rows), by_task),
+            pl.BlockSpec(block, by_task if roots else by_first),
+            pl.BlockSpec(block, by_task if roots else by_second),
+        ]
+        + [pl.BlockSpec((1,) + ref.shape[1:], by_owner(side)) for side, ref in enumerate(roots)],
+        [],
+        (tiles, from_first, from_second, *roots),
+    )
 
 
 def apply_tiles(lists, tiles, from_first, from_second, roots, col_devices, row_devices):
     slots, rows, unused = tiles.shape
     vecs = from_first.shape[1]
-
-    def by_task(s, t):
-        return (live_step(s, t, slots), 0, 0)
-
-    def by_first(s, t):
-        return (t[live_step(s, t, slots)], 0, 0)
-
-    def by_second(s, t):
-        return (t[slots + live_step(s, t, slots)], 0, 0)
-
-    def by_owner(side):
-        return lambda s, t: (t[3 * slots + 2 * live_step(s, t, slots) + side], 0, 0)
-
-    block = (1, vecs, rows)
-    by_slot = roots is not None
-    in_specs = [
-        pl.BlockSpec((1, rows, rows), by_task),
-        pl.BlockSpec(block, by_task if by_slot else by_first),
-        pl.BlockSpec(block, by_task if by_slot else by_second),
-    ]
-    operands = [lists, tiles, from_first, from_second]
-    if by_slot:
-        for side in range(2):
-            in_specs.append(pl.BlockSpec((1,) + roots.shape[1:], by_owner(side)))
-            operands.append(roots)
-    return pl.pallas_call(
+    vmem = pl.BlockSpec(memory_space=pltpu.VMEM)
+    lines = () if roots is None else (roots, roots)
+    return task_call(
         functools.partial(apply_kernel, slots),
-        grid_spec=pltpu.PrefetchScalarGridSpec(
-            num_scalar_prefetch=1,
-            grid=(slots,),
-            in_specs=in_specs,
-            out_specs=[
-                pl.BlockSpec((col_devices, vecs, rows), lambda s, t: (0, 0, 0)),
-                pl.BlockSpec((row_devices, vecs, rows), lambda s, t: (0, 0, 0)),
-            ],
-        ),
-        out_shape=[bf16(col_devices, vecs, rows), bf16(row_devices, vecs, rows)],
-        compiler_params=pltpu.CompilerParams(vmem_limit_bytes=VMEM),
-        name="apply_tiles",
-    )(*operands)
+        "apply_tiles",
+        (lists, tiles, from_first, from_second, *lines),
+        (True,) * (3 + len(lines)),
+        [vmem, vmem],
+        [bf16(col_devices, vecs, rows), bf16(row_devices, vecs, rows)],
+    )
 
 
 def spread_to(array, axis):

time: 300 us -> 300 us (level)
  Pallas kernels: 48.6 us -> 64.7 us
  blocking collectives: 63.5 us -> 54.2 us
  waiting for transfers between devices: 112 us -> 105 us
    all_to_all x3, blocking collectives: 50.3 us -> 41 us  [exchange(): return lax.all_to_all(copies, axis, 0, 0, tiled=True)]
    all_to_all x6, waiting for transfers between devices: 76.2 us -> 67.8 us  [exchange(): return lax.all_to_all(copies, axis, 0, 0, tiled=True)]
    pallas_call x2, Pallas kernels: 11.8 us -> 18.7 us  [task_call(): pl.pallas_call(kernel, in_specs=[pl.BlockSpec(memory_space=place) for pla...]
    pallas_call x1, Pallas kernels: 5.48 us -> 10.2 us  [form_tiles(): pl.pallas_call(functools.partial(form_kernel, min(256, rows), slots), gri...]
    pallas_call x2, Pallas kernels: 6.86 us -> 11.4 us  [start_vectors(): pl.pallas_call(functools.partial(vectors_kernel, slots), grid_spec=pltpu....]
  transfers between devices with their start and end apart: 16 -> 16, of which waited for: 9 -> 8; matrix products, arithmetic and copies ran while one was open for 5% -> 5% of each run, Pallas kernels for 7% -> 8%
where the time goes in v8:
time: 300 us; the launch traced here: 298 us
  waiting for transfers between devices  105 us (35%)
  Pallas kernels  64.7 us (22%)
  blocking collectives  54.2 us (18%)
  starting transfers between devices  42.1 us (14%)
  between operations  14.1 us (5%)
  other arithmetic  10.3 us (3%)
  local copies, waits for them, and re-layouts  5.49 us (2%)
    all_to_all x6, waiting for transfers between devices, exchange(): return lax.all_to_all(copies, axis, 0, 0, tiled=True)  67.8 us
    all_to_all x3, blocking collectives, exchange(): return lax.all_to_all(copies, axis, 0, 0, tiled=True)  41 us
    all_to_all x6, starting transfers between devices, exchange(): return lax.all_to_all(copies, axis, 0, 0, tiled=True)  27.3 us
    all_gather x1, waiting for transfers between devices, shards(): from_second = lax.all_gather(spread, 'row', axis=0)  27 us
    pallas_call x2, Pallas kernels, task_call(): pl.pallas_call(kernel, in_specs=[pl.BlockSpec(memory_space=place) for pla...  18.7 us
    all_to_all x1, blocking collectives, spread_to(): return lax.all_to_all(copies, axis, 0, 0, tiled=True)  13.2 us
    pallas_call x2, Pallas kernels, start_vectors(): pl.pallas_call(functools.partial(vectors_kernel, slots), grid_spec=pltpu....  11.4 us
    pallas_call x1, Pallas kernels, form_tiles(): pl.pallas_call(functools.partial(form_kernel, min(256, rows), slots), gri...  10.2 us
  transfers between devices with their start and end apart: 16, of which 8 were waited for; matrix products, arithmetic and copies ran while one was open for 5% of the time, Pallas kernels for 8%

profile of v8, /device:TPU:0, one launch (start us, length us, event | category | flops | bytes accessed | tf_op | source)
XLA Modules:
  0.0 297.7 jit_solution(475680698318467671)
XLA Ops:
  14.7 13.2 %all_to_all.55 = bf16[8,80,256]{2,1,0:T(8,128)(2,1)S(1)} all-to-all(bf16[8,80,256]{2,1,0:T(8,128)(2,1)S(1)} %broadcast_in_dim.71), channel_id=1, replica_groups=mesh['row'=8,'col'=16] {'row'}, dimensions={0} | all-to-all | bytes 655360 | tf_op jit(solution)/shard_map/all_to_all | solution.py:450
  29.0 8.0 %all-to-all-start.1 = ((bf16[16,80,256]{2,1,0:T(8,128)(2,1)}), bf16[16,80,256]{2,1,0:T(8,128)(2,1)S(1)}, u32[]{:S(2)}, u32[]{:S(2)}) async-start(bf16[16,80,256]{2,1,0:T(8,128)(2,1)} %broadcast_in_dim.72), calls=%async_computation.1 | async-start | bytes 1310720 | tf_op jit(solution)/shard_map/all_to_all | solution.py:450
  41.2 8.8 %all-to-all-done.1 = bf16[16,80,256]{2,1,0:T(8,128)(2,1)S(1)} async-done(((bf16[16,80,256]{2,1,0:T(8,128)(2,1)}), bf16[16,80,256]{2,1,0:T(8,128)(2,1)S(1)}, u32[]{:S(2)}, u32[]{:S(2)}) %all-to-all-start.1) | async-done | bytes 655392 | tf_op jit(solution)/shard_map/all_to_all | solution.py:450
  51.5 3.4 %all-to-all-start.2 = ((f32[8,24,128]{2,1,0:T(8,128)}), f32[8,24,128]{2,1,0:T(8,128)S(1)}, u32[]{:S(2)}, u32[]{:S(2)}) async-start(f32[8,24,128]{2,1,0:T(8,128)} %get-tuple-element.40), calls=%async_computation.2 | async-start | bytes 196608 | tf_op jit(solution)/shard_map/all_to_all | solution.py:454
  61.9 5.3 %assign_tasks.1.lists = s32[48]{0:T(128)S(1)} custom-call(s32[1]{0:T(128)} %bitcast.6.here, f32[16,128]{1,0:T(8,128)S(1)} %slice_convert_fusion.table), custom_call_target="tpu_custom_call" | custom-call | tf_op jit(solution)/shard_map/assign_tasks/pallas_call | solution.py:524
  68.0 3.5 %all-to-all-start.3 = ((f32[16,24,128]{2,1,0:T(8,128)}), f32[16,24,128]{2,1,0:T(8,128)S(1)}, u32[]{:S(2)}, u32[]{:S(2)}) async-start(f32[16,24,128]{2,1,0:T(8,128)} %relay.2), calls=%async_computation.3 | async-start | bytes 393216 | tf_op jit(solution)/shard_map/all_to_all | solution.py:454
  71.5 4.7 %pad_maximum_fusion.right.block = bf16[8,1024,256]{2,1,0:T(8,128)(2,1)} fusion(bf16[4,1024,256]{2,1,0:T(8,128)(2,1)} %collective-permute-done.4, bf16[4,1024,256]{2,1,0:T(8,128)(2,1)} %pad_maximum_fusion.1), kind=kLoop, calls=%fused_computation.1 | loop fusion | flops 2097152 | bytes 8388608 | tf_op jit(solution)/shard_map/concatenate | solution.py:590
  76.2 5.7 %all-to-all-done.3.grams = f32[16,24,128]{2,1,0:T(8,128)S(1)} async-done(((f32[16,24,128]{2,1,0:T(8,128)}), f32[16,24,128]{2,1,0:T(8,128)S(1)}, u32[]{:S(2)}, u32[]{:S(2)}) %all-to-all-start.3) | async-done | bytes 196640 | tf_op jit(solution)/shard_map/all_to_all | solution.py:454
  85.8 10.2 %form_tiles.1 = (bf16[8,1024,1024]{2,1,0:T(8,128)(2,1)}, f32[128,1,1152]{2,1,0:T(1,128)}) custom-call(s32[48]{0:T(128)} %copy-done.8, bf16[16,1024,256]{2,1,0:T(8,128)(2,1)} %bitcast.22, bf16[8,1024,256]{2,1,0:T(8,128)(2,1)} %pad_maximum_fusion.right.block, f32[1,256]{1,0:T(1,128)} %bitcast.28, f32[24,128]{1,0:T(8,128)} %copy-done.7), custom_call_target="tpu_custom_call" | custom-call | tf_op jit(solution)/shard_map/form_tiles/pallas_call | solution.py:328
  96.1 20.2 %all_to_all.56.parts = f32[128,1,1152]{2,1,0:T(1,128)S(1)} all-to-all(f32[128,1,1152]{2,1,0:T(1,128)} %get-tuple-element.50), channel_id=1, replica_groups=mesh['row'=8,'col'=16] {'row','col'}, dimensions={0} | all-to-all | bytes 1179648 | tf_op jit(solution)/shard_map/all_to_all | solution.py:454
  117.6 4.6 %all-to-all-start.5 = ((f32[128,1,1152]{2,1,0:T(1,128)}), f32[128,1,1152]{2,1,0:T(1,128)S(1)}, u32[]{:S(2)}, u32[]{:S(2)}) async-start(f32[128,1,1152]{2,1,0:T(1,128)} %get-tuple-element.54), calls=%async_computation.5 | async-start | bytes 1179648 | tf_op jit(solution)/shard_map/all_to_all | solution.py:454
  122.3 5.6 %start_vectors.3.from_second = f32[8,64,1024]{2,1,0:T(8,128)} custom-call(s32[48]{0:T(128)} %copy-done.8, bf16[8,1024,256]{2,1,0:T(8,128)(2,1)} %pad_maximum_fusion.right.block, bf16[64,256]{1,0:T(8,128)(2,1)} %copy-done.4, f32[64,64]{1,0:T(8,128)} %copy-done.9), custom_call_target="tpu_custom_call" | custom-call | flops 4000000000 | bytes 10000000 | tf_op jit(solution)/shard_map/start_vectors/pallas_call | solution.py:267
  127.9 5.8 %start_vectors.2.from_first = f32[8,64,1024]{2,1,0:T(8,128)} custom-call(s32[48]{0:T(128)} %copy-done.8, bf16[16,1024,256]{2,1,0:T(8,128)(2,1)} %bitcast.23, bf16[64,256]{1,0:T(8,128)(2,1)} %copy-done.4, f32[64,64]{1,0:T(8,128)} %copy-done.9, f32[1,256]{1,0:T(1,128)} %bitcast.29), custom_call_target="tpu_custom_call" | custom-call | flops 4000000000 | bytes 10000000 | tf_op jit(solution)/shard_map/start_vectors/pallas_call | solution.py:267
  137.3 9.4 %apply_tiles.2 = (bf16[16,64,1024]{2,1,0:T(8,128)(2,1)}, bf16[8,64,1024]{2,1,0:T(8,128)(2,1)}) custom-call(s32[48]{0:T(128)} %copy-done.8, bf16[8,1024,1024]{2,1,0:T(8,128)(2,1)} %get-tuple-element.52.tiles, f32[8,64,1024]{2,1,0:T(8,128)} %start_vectors.2.from_first, f32[8,64,1024]{2,1,0:T(8,128)} %start_vectors.3.from_second, f32[128,1,1152]{2,1,0:T(1,128)} %copy-done, ...), custom_call_target="tpu_custom_call" | custom-call | tf_op jit(solution)/shard_map/apply_tiles/pallas_call | solution.py:38
  146.8 4.4 %all-to-all-start.6 = ((bf16[16,64,1024]{2,1,0:T(8,128)(2,1)}), bf16[16,64,1024]{2,1,0:T(8,128)(2,1)}, u32[]{:S(2)}, u32[]{:S(2)}) async-start(bf16[16,64,1024]{2,1,0:T(8,128)(2,1)} %get-tuple-element.55), calls=%async_computation.6 | async-start | bytes 4194304 | tf_op jit(solution)/shard_map/all_to_all | solution.py:454
  155.1 25.8 %all-to-all-done.6.first_parts = bf16[16,64,1024]{2,1,0:T(8,128)(2,1)} async-done(((bf16[16,64,1024]{2,1,0:T(8,128)(2,1)}), bf16[16,64,1024]{2,1,0:T(8,128)(2,1)}, u32[]{:S(2)}, u32[]{:S(2)}) %all-to-all-start.6) | async-done | bytes 2097184 | tf_op jit(solution)/shard_map/all_to_all | solution.py:454
  181.0 3.9 %between.1 = (bf16[16,64,1024]{2,1,0:T(8,128)(2,1)}, bf16[64,1024]{1,0:T(8,128)(2,1)}) custom-call(f32[64,1024]{1,0:T(8,128)} %fusion.own_part, bf16[16,64,1024]{2,1,0:T(8,128)(2,1)} %all-to-all-done.6.first_parts, bf16[64,1024]{1,0:T(8,128)(2,1)} %bitcast.27, f32[1,1024]{1,0:T(1,128)} %copy-done.5, f32[64,64]{1,0:T(8,128)} %copy-done.2), custom_call_target="tpu_custom_call" | custom-call | tf_op jit(solution)/shard_map/between/pallas_call | solution.py:233
  184.8 4.4 %all-to-all-start.7 = ((bf16[16,64,1024]{2,1,0:T(8,128)(2,1)}), bf16[16,64,1024]{2,1,0:T(8,128)(2,1)}, u32[]{:S(2)}, u32[]{:S(2)}) async-start(bf16[16,64,1024]{2,1,0:T(8,128)(2,1)} %get-tuple-element.58), calls=%async_computation.8 | async-start | bytes 4194304 | tf_op jit(solution)/shard_map/all_to_all | solution.py:454
  190.0 27.0 %all-gather.7.cloned.1.call-done = bf16[512,1024]{1,0:T(8,128)(2,1)} async-done(((bf16[64,1024]{1,0:T(8,128)(2,1)}), bf16[512,1024]{1,0:T(8,128)(2,1)}) %all-gather.7.cloned.1.call-update) | async-done | bytes 1048592 | tf_op jit(solution)/shard_map/all_gather | solution.py:619
  217.0 9.2 %apply_tiles.3 = (bf16[16,64,1024]{2,1,0:T(8,128)(2,1)}, bf16[8,64,1024]{2,1,0:T(8,128)(2,1)}) custom-call(s32[48]{0:T(128)} %copy-done.8, bf16[8,1024,1024]{2,1,0:T(8,128)(2,1)} %get-tuple-element.52.tiles, bf16[16,64,1024]{2,1,0:T(8,128)(2,1)} %all-to-all-done.7.from_first, bf16[8,64,1024]{2,1,0:T(8,128)(2,1)} %bitcast.26), custom_call_target="tpu_custom_call" | custom-call | tf_op jit(solution)/shard_map/apply_tiles/pallas_call | solution.py:38
  226.3 6.9 %all-to-all-start.8 = ((bf16[16,64,1024]{2,1,0:T(8,128)(2,1)}), bf16[16,64,1024]{2,1,0:T(8,128)(2,1)}, u32[]{:S(2)}, u32[]{:S(2)}) async-start(bf16[16,64,1024]{2,1,0:T(8,128)(2,1)} %get-tuple-element.59), calls=%async_computation.9 | async-start | bytes 4194304 | tf_op jit(solution)/shard_map/all_to_all | solution.py:454
  233.7 30.4 %all-to-all-done.8.first_parts = bf16[16,64,1024]{2,1,0:T(8,128)(2,1)} async-done(((bf16[16,64,1024]{2,1,0:T(8,128)(2,1)}), bf16[16,64,1024]{2,1,0:T(8,128)(2,1)}, u32[]{:S(2)}, u32[]{:S(2)}) %all-to-all-start.8) | async-done | bytes 2097184 | tf_op jit(solution)/shard_map/all_to_all | solution.py:454
  267.3 8.9 %all_to_all.57.grams = f32[8,24,128]{2,1,0:T(8,128)S(1)} all-to-all(f32[8,24,128]{2,1,0:T(8,128)S(1)} %get-tuple-element.61), channel_id=1, replica_groups=mesh['row'=8,'col'=16] {'row'}, dimensions={0} | all-to-all | bytes 196608 | tf_op jit(solution)/shard_map/all_to_all | solution.py:454
  276.2 11.9 %all_to_all.58.grams = f32[16,24,128]{2,1,0:T(8,128)S(1)} all-to-all(f32[16,24,128]{2,1,0:T(8,128)S(1)} %relay.3), channel_id=1, replica_groups=mesh['row'=8,'col'=16] {'col'}, dimensions={0} | all-to-all | bytes 393216 | tf_op jit(solution)/shard_map/all_to_all | solution.py:454
  (86 shorter events, 42.4 us)
Async XLA Ops:
  6.5 79.3 %all-gather.5.cloned.1.call-start = ((), (), s32[]{:S(2)}) async-start(), calls=%async_computation.15 | async-start | bytes 8912896 | tf_op jit(solution)/shard_map/all_gather | solution.py:543
  8.4 19.5 %collective-permute-start = (bf16[1024,256]{1,0:T(8,128)(2,1)S(1)}, bf16[1024,256]{1,0:T(8,128)(2,1)S(1)}, u32[]{:S(2)}, u32[]{:S(2)}) collective-permute-start(bf16[1024,256]{1,0:T(8,128)(2,1)S(1)} %multiply_convert_fusion.own), channel_id=1, source_target_pairs={{0,32},{16,48},{32,64},{48,80},{64,96},{80,112},{96,0},{112,16},{1... | collective-permute-start | bytes 1572872 | tf_op jit(solution)/shard_map/ppermute | solution.py:549
  10.0 17.9 %collective-permute-start.1 = (bf16[1024,256]{1,0:T(8,128)(2,1)S(1)}, bf16[1024,256]{1,0:T(8,128)(2,1)S(1)}, u32[]{:S(2)}, u32[]{:S(2)}) collective-permute-start(bf16[1024,256]{1,0:T(8,128)(2,1)S(1)} %multiply_convert_fusion.own), channel_id=1, source_target_pairs={{0,96},{16,112},{32,0},{48,16},{64,32},{80,48},{96,64},{112,80},{1... | collective-permute-start | bytes 1572872 | tf_op jit(solution)/shard_map/ppermute | solution.py:549
  14.7 26.4 %copy-start.10 = (bf16[1024,256]{1,0:T(8,128)(2,1)S(1)}, bf16[1024,256]{1,0:T(8,128)(2,1)}, u32[]{:S(2)}) copy-start(bf16[1024,256]{1,0:T(8,128)(2,1)} %param.5) | copy-start | bytes 1572868
  14.7 26.4 %copy-start.14 = (f32[256]{0:T(256)S(1)}, f32[256]{0:T(256)}, u32[]{:S(2)}) copy-start(f32[256]{0:T(256)} %param.6) | copy-start | bytes 3076
  27.9 11.0 %copy-start.11 = (bf16[1024,256]{1,0:T(8,128)(2,1)}, bf16[1024,256]{1,0:T(8,128)(2,1)S(1)}, u32[]{:S(2)}) copy-start(bf16[1024,256]{1,0:T(8,128)(2,1)S(1)} %collective-permute-done.1) | copy-start | bytes 1572868
  29.0 21.0 %all-to-all-start.1 = ((bf16[16,80,256]{2,1,0:T(8,128)(2,1)}), bf16[16,80,256]{2,1,0:T(8,128)(2,1)S(1)}, u32[]{:S(2)}, u32[]{:S(2)}) async-start(bf16[16,80,256]{2,1,0:T(8,128)(2,1)} %broadcast_in_dim.72), calls=%async_computation.1 | async-start | bytes 1310720 | tf_op jit(solution)/shard_map/all_to_all | solution.py:450
  37.0 14.5 %collective-permute-start.2 = (bf16[512,256]{1,0:T(8,128)(2,1)S(1)}, bf16[512,256]{1,0:T(8,128)(2,1)}, u32[]{:S(2)}, u32[]{:S(2)}) collective-permute-start(bf16[512,256]{1,0:T(8,128)(2,1)S(1)} %slice.12), channel_id=1, source_target_pairs={{0,32},{16,48},{32,64},{48,80},{64,96},{80,112},{96,0},{112,16},{1... | collective-permute-start | bytes 786440 | tf_op jit(solution)/shard_map/ppermute | solution.py:549
  39.0 12.6 %collective-permute-start.3 = (bf16[512,256]{1,0:T(8,128)(2,1)}, bf16[512,256]{1,0:T(8,128)(2,1)}, u32[]{:S(2)}, u32[]{:S(2)}) collective-permute-start(bf16[512,256]{1,0:T(8,128)(2,1)} %slice.13), channel_id=1, source_target_pairs={{0,96},{16,112},{32,0},{48,16},{64,32},{80,48},{96,64},{112,80},{1... | collective-permute-start | bytes 786440 | tf_op jit(solution)/shard_map/ppermute | solution.py:549
  50.1 7.5 %copy-start.4 = (bf16[64,256]{1,0:T(8,128)(2,1)}, bf16[64,256]{1,0:T(8,128)(2,1)S(1)}, u32[]{:S(2)}) copy-start(bf16[64,256]{1,0:T(8,128)(2,1)S(1)} %slice.18.seeds) | copy-start | bytes 98308
  51.5 9.2 %all-to-all-start.2 = ((f32[8,24,128]{2,1,0:T(8,128)}), f32[8,24,128]{2,1,0:T(8,128)S(1)}, u32[]{:S(2)}, u32[]{:S(2)}) async-start(f32[8,24,128]{2,1,0:T(8,128)} %get-tuple-element.40), calls=%async_computation.2 | async-start | bytes 196608 | tf_op jit(solution)/shard_map/all_to_all | solution.py:454
  60.7 10.8 %collective-permute-start.4 = (bf16[4,1024,256]{2,1,0:T(8,128)(2,1)}, bf16[4,1024,256]{2,1,0:T(8,128)(2,1)}, u32[]{:S(2)}, u32[]{:S(2)}) collective-permute-start(bf16[4,1024,256]{2,1,0:T(8,128)(2,1)} %pad_maximum_fusion.1), channel_id=1, source_target_pairs={{0,16},{16,0},{32,48},{48,32},{64,80},{80,64},{96,112},{112,96},{1... | collective-permute-start | bytes 6291464 | tf_op jit(solution)/shard_map/ppermute | solution.py:585
  67.3 8.9 %copy-start.8 = (s32[48]{0:T(128)}, s32[48]{0:T(128)S(1)}, u32[]{:S(2)}) copy-start(s32[48]{0:T(128)S(1)} %assign_tasks.1.lists) | copy-start | bytes 580
  68.0 13.9 %all-to-all-start.3 = ((f32[16,24,128]{2,1,0:T(8,128)}), f32[16,24,128]{2,1,0:T(8,128)S(1)}, u32[]{:S(2)}, u32[]{:S(2)}) async-start(f32[16,24,128]{2,1,0:T(8,128)} %relay.2), calls=%async_computation.3 | async-start | bytes 393216 | tf_op jit(solution)/shard_map/all_to_all | solution.py:454
  85.7 10.4 %copy-start.9 = (f32[64,64]{1,0:T(8,128)}, f32[64,64]{1,0:T(8,128)S(1)}, u32[]{:S(2)}) copy-start(f32[64,64]{1,0:T(8,128)S(1)} %get-tuple-element.53.factor) | copy-start | bytes 49156
  117.6 33.7 %copy-start.5 = (f32[1,1024]{1,0:T(1,128)}, f32[1,1024]{1,0:T(1,128)S(1)}, u32[]{:S(2)}) copy-start(f32[1,1024]{1,0:T(1,128)S(1)} %get-tuple-element.51.root) | copy-start | bytes 12292
  117.6 18.9 %all-to-all-start.5 = ((f32[128,1,1152]{2,1,0:T(1,128)}), f32[128,1,1152]{2,1,0:T(1,128)S(1)}, u32[]{:S(2)}, u32[]{:S(2)}) async-start(f32[128,1,1152]{2,1,0:T(1,128)} %get-tuple-element.54), calls=%async_computation.5 | async-start | bytes 1179648 | tf_op jit(solution)/shard_map/all_to_all | solution.py:454
  122.2 58.7 %reduce-scatter.3.cloned.1.call-start = ((), (), s32[]{:S(2)}) async-start(), calls=%async_computation.13 | async-start | bytes 1179648 | tf_op jit(solution)/shard_map/reduce_scatter | solution.py:613
  146.8 34.2 %all-to-all-start.6 = ((bf16[16,64,1024]{2,1,0:T(8,128)(2,1)}), bf16[16,64,1024]{2,1,0:T(8,128)(2,1)}, u32[]{:S(2)}, u32[]{:S(2)}) async-start(bf16[16,64,1024]{2,1,0:T(8,128)(2,1)} %get-tuple-element.55), calls=%async_computation.6 | async-start | bytes 4194304 | tf_op jit(solution)/shard_map/all_to_all | solution.py:454
  184.8 32.2 %all-to-all-start.7 = ((bf16[16,64,1024]{2,1,0:T(8,128)(2,1)}), bf16[16,64,1024]{2,1,0:T(8,128)(2,1)}, u32[]{:S(2)}, u32[]{:S(2)}) async-start(bf16[16,64,1024]{2,1,0:T(8,128)(2,1)} %get-tuple-element.58), calls=%async_computation.8 | async-start | bytes 4194304 | tf_op jit(solution)/shard_map/all_to_all | solution.py:454
  189.3 27.8 %all-gather.7.cloned.1.call-start = ((), (), s32[]{:S(2)}) async-start(), calls=%async_computation.16 | async-start | bytes 1179648 | tf_op jit(solution)/shard_map/all_gather | solution.py:619
  190.0 74.1 %reduce-scatter.5.cloned.1.call-start = ((), (), s32[]{:S(2)}) async-start(), calls=%async_computation.14 | async-start | bytes 1179648 | tf_op jit(solution)/shard_map/reduce_scatter | solution.py:613
  226.3 37.8 %all-to-all-start.8 = ((bf16[16,64,1024]{2,1,0:T(8,128)(2,1)}), bf16[16,64,1024]{2,1,0:T(8,128)(2,1)}, u32[]{:S(2)}, u32[]{:S(2)}) async-start(bf16[16,64,1024]{2,1,0:T(8,128)(2,1)} %get-tuple-element.59), calls=%async_computation.9 | async-start | bytes 4194304 | tf_op jit(solution)/shard_map/all_to_all | solution.py:454
  233.2 30.9 %copy-start.6 = (f32[1,1024]{1,0:T(1,128)S(1)}, f32[1,1024]{1,0:T(1,128)}, u32[]{:S(2)}) copy-start(f32[1,1024]{1,0:T(1,128)} %copy-done.5) | copy-start | bytes 12292
  (7 other events, 17.1 us)
Sparse Core Ops, SparseCore 0:
  9.5 76.2 all-gather.4
  146.9 29.0 reduce-scatter.2
  191.8 25.1 all-gather.6
  226.4 33.0 reduce-scatter.4

commit v9 on v7

--- a/solution.py
+++ b/solution.py
@@ -13,7 +13,7 @@
 VMEM = 60 * 1024 * 1024
 SMALL = 24 * 1024 * 1024
 HIGH = lax.Precision.HIGHEST
-RIDGE = 1e-6
+RIDGE = 1e-5
 
 
 def weigh(block, scale):
@@ -346,75 +346,85 @@
     )(own)
 
 
-def apply_kernel(slots, lists, tile, left, right, *rest):
-    step = pl.program_id(0)
-    left_roots, right_roots, to_first, to_second = rest if len(rest) == 4 else (None, None) + rest
-
-    def scaled(vectors, roots):
-        if roots is None:
-            return vectors[0]
-        return (vectors[0] * roots[0, :, : vectors.shape[2]]).astype(jnp.bfloat16)
-
-    def add(out, slot, vectors, contract):
-        product = lax.dot_general(
-            vectors, tile[0], (((1,), (contract,)), ((), ())), preferred_element_type=jnp.float32
-        )
-        out[slot] = (out[slot].astype(jnp.float32) + product).astype(jnp.bfloat16)
-
-    @pl.when(step == 0)
-    def clear():
-        to_first[...] = jnp.zeros_like(to_first)
-        to_second[...] = jnp.zeros_like(to_second)
-
-    @pl.when(step < lists[5 * slots])
-    def work():
-        add(to_second, lists[slots + step], scaled(left, left_roots), 0)
-        add(to_first, lists[step], scaled(right, right_roots), 1)
+def apply_kernel(slots, by_slot, lists, tiles, from_first, from_second, *rest):
+    count = 5 if by_slot else 3
+    lines = rest[0] if by_slot else None
+    to_first, to_second = rest[-count - 3 : -count - 1]
+    held, semaphores = rest[-count - 1 : -1], rest[-1]
+    rows = tiles.shape[1]
+    live = lists[5 * slots]
+
+    def copies(step, side):
+        first, second = lists[step], lists[slots + step]
+        sources = [tiles.at[step]]
+        if by_slot:
+            sources += [from_first.at[step], from_second.at[step]]
+            sources += [lines.at[lists[3 * slots + 2 * step + end]] for end in range(2)]
+        else:
+            sources += [from_first.at[first], from_second.at[second]]
+        return [
+            pltpu.make_async_copy(source, held[index].at[side], semaphores.at[index, side])
+            for index, source in enumerate(sources)
+        ]
+
+    @pl.when(live > 0)
+    def begin():
+        for copy in copies(0, 0):
+            copy.start()
+
+    to_first[...] = jnp.zeros_like(to_first)
+    to_second[...] = jnp.zeros_like(to_second)
+
+    def one(step, state):
+        side = lax.rem(step, 2)
+
+        @pl.when(step + 1 < live)
+        def ahead():
+            for copy in copies(step + 1, 1 - side):
+                copy.start()
+
+        for copy in copies(step, side):
+            copy.wait()
+
+        def vectors(end):
+            block = held[1 + end][side]
+            if not by_slot:
+                return block
+            return (block * held[3 + end][side][:, :rows]).astype(jnp.bfloat16)
+
+        def add(out, slot, block, contract):
+            product = lax.dot_general(
+                block,
+                held[0][side],
+                (((1,), (contract,)), ((), ())),
+                preferred_element_type=jnp.float32,
+            )
+            out[slot] = (out[slot].astype(jnp.float32) + product).astype(jnp.bfloat16)
+
+        add(to_second, lists[slots + step], vectors(0), 0)
+        add(to_first, lists[step], vectors(1), 1)
+        return state
+
+    lax.fori_loop(0, live, one, 0)
 
 
 def apply_tiles(lists, tiles, from_first, from_second, roots, col_devices, row_devices):
     slots, rows, unused = tiles.shape
     vecs = from_first.shape[1]
-
-    def by_task(s, t):
-        return (live_step(s, t, slots), 0, 0)
-
-    def by_first(s, t):
-        return (t[live_step(s, t, slots)], 0, 0)
-
-    def by_second(s, t):
-        return (t[slots + live_step(s, t, slots)], 0, 0)
-
-    def by_owner(side):
-        return lambda s, t: (t[3 * slots + 2 * live_step(s, t, slots) + side], 0, 0)
-
-    block = (1, vecs, rows)
     by_slot = roots is not None
-    in_specs = [
-        pl.BlockSpec((1, rows, rows), by_task),
-        pl.BlockSpec(block, by_task if by_slot else by_first),
-        pl.BlockSpec(block, by_task if by_slot else by_second),
-    ]
-    operands = [lists, tiles, from_first, from_second]
-    if by_slot:
-        for side in range(2):
-            in_specs.append(pl.BlockSpec((1,) + roots.shape[1:], by_owner(side)))
-            operands.append(roots)
+    operands = [tiles, from_first, from_second] + ([roots] if by_slot else [])
+    held = operands + ([roots] if by_slot else [])
     return pl.pallas_call(
-        functools.partial(apply_kernel, slots),
-        grid_spec=pltpu.PrefetchScalarGridSpec(
-            num_scalar_prefetch=1,
-            grid=(slots,),
-            in_specs=in_specs,
-            out_specs=[
-                pl.BlockSpec((col_devices, vecs, rows), lambda s, t: (0, 0, 0)),
-                pl.BlockSpec((row_devices, vecs, rows), lambda s, t: (0, 0, 0)),
-            ],
-        ),
+        functools.partial(apply_kernel, slots, by_slot),
+        in_specs=[pl.BlockSpec(memory_space=pltpu.SMEM)]
+        + [pl.BlockSpec(memory_space=pl.ANY)] * len(operands),
+        out_specs=[pl.BlockSpec(memory_space=pltpu.VMEM)] * 2,
         out_shape=[bf16(col_devices, vecs, rows), bf16(row_devices, vecs, rows)],
+        scratch_shapes=[pltpu.VMEM((2,) + one.shape[1:], one.dtype) for one in held]
+        + [pltpu.SemaphoreType.DMA((len(held), 2))],
         compiler_params=pltpu.CompilerParams(vmem_limit_bytes=VMEM),
         name="apply_tiles",
-    )(*operands)
+    )(lists, *operands)
 
 
 def spread_to(array, axis):

time: 300 us -> 301 us (level)
  Pallas kernels: 48.6 us -> 64.4 us
  blocking collectives: 63.5 us -> 57.4 us
  waiting for transfers between devices: 112 us -> 106 us
  starting transfers between devices: 44.3 us -> 39.8 us
    pallas_call x2, Pallas kernels: 11.8 us -> 18.4 us  [apply_tiles(): pl.pallas_call(functools.partial(apply_kernel, slots, by_slot), in_specs=...]
    all_to_all x3, blocking collectives: 50.3 us -> 44.2 us  [exchange(): return lax.all_to_all(copies, axis, 0, 0, tiled=True)]
    all_to_all x6, waiting for transfers between devices: 76.2 us -> 70.6 us  [exchange(): return lax.all_to_all(copies, axis, 0, 0, tiled=True)]
    pallas_call x1, Pallas kernels: 5.48 us -> 10.2 us  [form_tiles(): pl.pallas_call(functools.partial(form_kernel, min(256, rows), slots), gri...]
    all_to_all x6, starting transfers between devices: 29.5 us -> 25 us  [exchange(): return lax.all_to_all(copies, axis, 0, 0, tiled=True)]
    pallas_call x2, Pallas kernels: 6.86 us -> 11.4 us  [start_vectors(): pl.pallas_call(functools.partial(vectors_kernel, slots), grid_spec=pltpu....]
  transfers between devices with their start and end apart: 16 -> 16, of which waited for: 9 -> 9; matrix products, arithmetic and copies ran while one was open for 5% -> 5% of each run, Pallas kernels for 7% -> 8%
where the time goes in v9:
time: 301 us; the launch traced here: 299 us
  waiting for transfers between devices  106 us (35%)
  Pallas kernels  64.4 us (21%)
  blocking collectives  57.4 us (19%)
  starting transfers between devices  39.8 us (13%)
  between operations  14.1 us (5%)
  other arithmetic  10.3 us (3%)
  local copies, waits for them, and re-layouts  5.49 us (2%)
    all_to_all x6, waiting for transfers between devices, exchange(): return lax.all_to_all(copies, axis, 0, 0, tiled=True)  70.6 us
    all_to_all x3, blocking collectives, exchange(): return lax.all_to_all(copies, axis, 0, 0, tiled=True)  44.2 us
    all_gather x1, waiting for transfers between devices, shards(): from_second = lax.all_gather(spread, 'row', axis=0)  25.3 us
    all_to_all x6, starting transfers between devices, exchange(): return lax.all_to_all(copies, axis, 0, 0, tiled=True)  25 us
    pallas_call x2, Pallas kernels, apply_tiles(): pl.pallas_call(functools.partial(apply_kernel, slots, by_slot), in_specs=...  18.4 us
    all_to_all x1, blocking collectives, spread_to(): return lax.all_to_all(copies, axis, 0, 0, tiled=True)  13.2 us
    pallas_call x2, Pallas kernels, start_vectors(): pl.pallas_call(functools.partial(vectors_kernel, slots), grid_spec=pltpu....  11.4 us
    pallas_call x1, Pallas kernels, form_tiles(): pl.pallas_call(functools.partial(form_kernel, min(256, rows), slots), gri...  10.2 us
  transfers between devices with their start and end apart: 16, of which 9 were waited for; matrix products, arithmetic and copies ran while one was open for 5% of the time, Pallas kernels for 8%

profile of v9, /device:TPU:0, one launch (start us, length us, event | category | flops | bytes accessed | tf_op | source)
XLA Modules:
  0.0 299.4 jit_solution(7484394741478271434)
XLA Ops:
  14.7 13.2 %all_to_all.55 = bf16[8,80,256]{2,1,0:T(8,128)(2,1)S(1)} all-to-all(bf16[8,80,256]{2,1,0:T(8,128)(2,1)S(1)} %broadcast_in_dim.71), channel_id=1, replica_groups=mesh['row'=8,'col'=16] {'row'}, dimensions={0} | all-to-all | bytes 655360 | tf_op jit(solution)/shard_map/all_to_all | solution.py:433
  29.0 8.0 %all-to-all-start.1 = ((bf16[16,80,256]{2,1,0:T(8,128)(2,1)}), bf16[16,80,256]{2,1,0:T(8,128)(2,1)S(1)}, u32[]{:S(2)}, u32[]{:S(2)}) async-start(bf16[16,80,256]{2,1,0:T(8,128)(2,1)} %broadcast_in_dim.72), calls=%async_computation.1 | async-start | bytes 1310720 | tf_op jit(solution)/shard_map/all_to_all | solution.py:433
  41.2 8.8 %all-to-all-done.1 = bf16[16,80,256]{2,1,0:T(8,128)(2,1)S(1)} async-done(((bf16[16,80,256]{2,1,0:T(8,128)(2,1)}), bf16[16,80,256]{2,1,0:T(8,128)(2,1)S(1)}, u32[]{:S(2)}, u32[]{:S(2)}) %all-to-all-start.1) | async-done | bytes 655392 | tf_op jit(solution)/shard_map/all_to_all | solution.py:433
  51.5 3.4 %all-to-all-start.2 = ((f32[8,24,128]{2,1,0:T(8,128)}), f32[8,24,128]{2,1,0:T(8,128)S(1)}, u32[]{:S(2)}, u32[]{:S(2)}) async-start(f32[8,24,128]{2,1,0:T(8,128)} %get-tuple-element.40), calls=%async_computation.2 | async-start | bytes 196608 | tf_op jit(solution)/shard_map/all_to_all | solution.py:437
  61.9 5.3 %assign_tasks.1.lists = s32[48]{0:T(128)S(1)} custom-call(s32[1]{0:T(128)} %bitcast.6.here, f32[16,128]{1,0:T(8,128)S(1)} %slice_convert_fusion.table), custom_call_target="tpu_custom_call" | custom-call | tf_op jit(solution)/shard_map/assign_tasks/pallas_call | solution.py:507
  68.0 3.5 %all-to-all-start.3 = ((f32[16,24,128]{2,1,0:T(8,128)}), f32[16,24,128]{2,1,0:T(8,128)S(1)}, u32[]{:S(2)}, u32[]{:S(2)}) async-start(f32[16,24,128]{2,1,0:T(8,128)} %relay.2), calls=%async_computation.3 | async-start | bytes 393216 | tf_op jit(solution)/shard_map/all_to_all | solution.py:437
  71.5 4.7 %pad_maximum_fusion.right.block = bf16[8,1024,256]{2,1,0:T(8,128)(2,1)} fusion(bf16[4,1024,256]{2,1,0:T(8,128)(2,1)} %collective-permute-done.4, bf16[4,1024,256]{2,1,0:T(8,128)(2,1)} %pad_maximum_fusion.1), kind=kLoop, calls=%fused_computation.1 | loop fusion | flops 2097152 | bytes 8388608 | tf_op jit(solution)/shard_map/concatenate | solution.py:573
  76.2 5.7 %all-to-all-done.3.grams = f32[16,24,128]{2,1,0:T(8,128)S(1)} async-done(((f32[16,24,128]{2,1,0:T(8,128)}), f32[16,24,128]{2,1,0:T(8,128)S(1)}, u32[]{:S(2)}, u32[]{:S(2)}) %all-to-all-start.3) | async-done | bytes 196640 | tf_op jit(solution)/shard_map/all_to_all | solution.py:437
  85.8 10.2 %form_tiles.1 = (bf16[8,1024,1024]{2,1,0:T(8,128)(2,1)}, f32[128,1,1152]{2,1,0:T(1,128)}) custom-call(s32[48]{0:T(128)} %copy-done.8, bf16[16,1024,256]{2,1,0:T(8,128)(2,1)} %bitcast.22, bf16[8,1024,256]{2,1,0:T(8,128)(2,1)} %pad_maximum_fusion.right.block, f32[1,256]{1,0:T(1,128)} %bitcast.28, f32[24,128]{1,0:T(8,128)} %copy-done.7), custom_call_target="tpu_custom_call" | custom-call | tf_op jit(solution)/shard_map/form_tiles/pallas_call | solution.py:298
  96.1 21.2 %all_to_all.56.parts = f32[128,1,1152]{2,1,0:T(1,128)S(1)} all-to-all(f32[128,1,1152]{2,1,0:T(1,128)} %get-tuple-element.50), channel_id=1, replica_groups=mesh['row'=8,'col'=16] {'row','col'}, dimensions={0} | all-to-all | bytes 1179648 | tf_op jit(solution)/shard_map/all_to_all | solution.py:437
  118.6 4.6 %all-to-all-start.5 = ((f32[128,1,1152]{2,1,0:T(1,128)}), f32[128,1,1152]{2,1,0:T(1,128)S(1)}, u32[]{:S(2)}, u32[]{:S(2)}) async-start(f32[128,1,1152]{2,1,0:T(1,128)} %get-tuple-element.54), calls=%async_computation.5 | async-start | bytes 1179648 | tf_op jit(solution)/shard_map/all_to_all | solution.py:437
  123.3 5.6 %start_vectors.3.from_second = f32[8,64,1024]{2,1,0:T(8,128)} custom-call(s32[48]{0:T(128)} %copy-done.8, bf16[8,1024,256]{2,1,0:T(8,128)(2,1)} %pad_maximum_fusion.right.block, bf16[64,256]{1,0:T(8,128)(2,1)} %copy-done.4, f32[64,64]{1,0:T(8,128)} %copy-done.9), custom_call_target="tpu_custom_call" | custom-call | flops 4000000000 | bytes 10000000 | tf_op jit(solution)/shard_map/start_vectors/pallas_call | solution.py:237
  128.9 5.8 %start_vectors.2.from_first = f32[8,64,1024]{2,1,0:T(8,128)} custom-call(s32[48]{0:T(128)} %copy-done.8, bf16[16,1024,256]{2,1,0:T(8,128)(2,1)} %bitcast.23, bf16[64,256]{1,0:T(8,128)(2,1)} %copy-done.4, f32[64,64]{1,0:T(8,128)} %copy-done.9, f32[1,256]{1,0:T(1,128)} %bitcast.29), custom_call_target="tpu_custom_call" | custom-call | flops 4000000000 | bytes 10000000 | tf_op jit(solution)/shard_map/start_vectors/pallas_call | solution.py:237
  138.3 9.3 %apply_tiles.2 = (bf16[16,64,1024]{2,1,0:T(8,128)(2,1)}, bf16[8,64,1024]{2,1,0:T(8,128)(2,1)}) custom-call(s32[48]{0:T(128)} %copy-done.8, bf16[8,1024,1024]{2,1,0:T(8,128)(2,1)} %get-tuple-element.52.tiles, f32[8,64,1024]{2,1,0:T(8,128)} %start_vectors.2.from_first, f32[8,64,1024]{2,1,0:T(8,128)} %start_vectors.3.from_second, f32[128,1,1152]{2,1,0:T(1,128)} %copy-done), custom_call_target="tpu_custom_call" | custom-call | tf_op jit(solution)/shard_map/apply_tiles/pallas_call | solution.py:417
  147.7 4.4 %all-to-all-start.6 = ((bf16[16,64,1024]{2,1,0:T(8,128)(2,1)}), bf16[16,64,1024]{2,1,0:T(8,128)(2,1)}, u32[]{:S(2)}, u32[]{:S(2)}) async-start(bf16[16,64,1024]{2,1,0:T(8,128)(2,1)} %get-tuple-element.55), calls=%async_computation.6 | async-start | bytes 4194304 | tf_op jit(solution)/shard_map/all_to_all | solution.py:437
  156.0 26.7 %all-to-all-done.6.first_parts = bf16[16,64,1024]{2,1,0:T(8,128)(2,1)} async-done(((bf16[16,64,1024]{2,1,0:T(8,128)(2,1)}), bf16[16,64,1024]{2,1,0:T(8,128)(2,1)}, u32[]{:S(2)}, u32[]{:S(2)}) %all-to-all-start.6) | async-done | bytes 2097184 | tf_op jit(solution)/shard_map/all_to_all | solution.py:437
  182.7 3.8 %between.1 = (bf16[16,64,1024]{2,1,0:T(8,128)(2,1)}, bf16[64,1024]{1,0:T(8,128)(2,1)}) custom-call(f32[64,1024]{1,0:T(8,128)} %fusion.own_part, bf16[16,64,1024]{2,1,0:T(8,128)(2,1)} %all-to-all-done.6.first_parts, bf16[64,1024]{1,0:T(8,128)(2,1)} %bitcast.27, f32[1,1024]{1,0:T(1,128)} %copy-done.5, f32[64,64]{1,0:T(8,128)} %copy-done.2), custom_call_target="tpu_custom_call" | custom-call | tf_op jit(solution)/shard_map/between/pallas_call | solution.py:203
  186.6 4.4 %all-to-all-start.7 = ((bf16[16,64,1024]{2,1,0:T(8,128)(2,1)}), bf16[16,64,1024]{2,1,0:T(8,128)(2,1)}, u32[]{:S(2)}, u32[]{:S(2)}) async-start(bf16[16,64,1024]{2,1,0:T(8,128)(2,1)} %get-tuple-element.58), calls=%async_computation.8 | async-start | bytes 4194304 | tf_op jit(solution)/shard_map/all_to_all | solution.py:437
  191.8 25.3 %all-gather.7.cloned.1.call-done = bf16[512,1024]{1,0:T(8,128)(2,1)} async-done(((bf16[64,1024]{1,0:T(8,128)(2,1)}), bf16[512,1024]{1,0:T(8,128)(2,1)}) %all-gather.7.cloned.1.call-update) | async-done | bytes 1048592 | tf_op jit(solution)/shard_map/all_gather | solution.py:602
  219.0 9.1 %apply_tiles.3 = (bf16[16,64,1024]{2,1,0:T(8,128)(2,1)}, bf16[8,64,1024]{2,1,0:T(8,128)(2,1)}) custom-call(s32[48]{0:T(128)} %copy-done.8, bf16[8,1024,1024]{2,1,0:T(8,128)(2,1)} %get-tuple-element.52.tiles, bf16[16,64,1024]{2,1,0:T(8,128)(2,1)} %all-to-all-done.7.from_first, bf16[8,64,1024]{2,1,0:T(8,128)(2,1)} %bitcast.26), custom_call_target="tpu_custom_call" | custom-call | tf_op jit(solution)/shard_map/apply_tiles/pallas_call | solution.py:417
  228.2 4.6 %all-to-all-start.8 = ((bf16[16,64,1024]{2,1,0:T(8,128)(2,1)}), bf16[16,64,1024]{2,1,0:T(8,128)(2,1)}, u32[]{:S(2)}, u32[]{:S(2)}) async-start(bf16[16,64,1024]{2,1,0:T(8,128)(2,1)} %get-tuple-element.59), calls=%async_computation.9 | async-start | bytes 4194304 | tf_op jit(solution)/shard_map/all_to_all | solution.py:437
  233.3 30.3 %all-to-all-done.8.first_parts = bf16[16,64,1024]{2,1,0:T(8,128)(2,1)} async-done(((bf16[16,64,1024]{2,1,0:T(8,128)(2,1)}), bf16[16,64,1024]{2,1,0:T(8,128)(2,1)}, u32[]{:S(2)}, u32[]{:S(2)}) %all-to-all-start.8) | async-done | bytes 2097184 | tf_op jit(solution)/shard_map/all_to_all | solution.py:437
  266.8 10.0 %all_to_all.57.grams = f32[8,24,128]{2,1,0:T(8,128)S(1)} all-to-all(f32[8,24,128]{2,1,0:T(8,128)S(1)} %get-tuple-element.61), channel_id=1, replica_groups=mesh['row'=8,'col'=16] {'row'}, dimensions={0} | all-to-all | bytes 196608 | tf_op jit(solution)/shard_map/all_to_all | solution.py:437
  276.9 12.9 %all_to_all.58.grams = f32[16,24,128]{2,1,0:T(8,128)S(1)} all-to-all(f32[16,24,128]{2,1,0:T(8,128)S(1)} %relay.3), channel_id=1, replica_groups=mesh['row'=8,'col'=16] {'col'}, dimensions={0} | all-to-all | bytes 393216 | tf_op jit(solution)/shard_map/all_to_all | solution.py:437
  (86 shorter events, 44.3 us)
Async XLA Ops:
  6.5 79.3 %all-gather.5.cloned.1.call-start = ((), (), s32[]{:S(2)}) async-start(), calls=%async_computation.15 | async-start | bytes 8912896 | tf_op jit(solution)/shard_map/all_gather | solution.py:526
  8.4 19.5 %collective-permute-start = (bf16[1024,256]{1,0:T(8,128)(2,1)S(1)}, bf16[1024,256]{1,0:T(8,128)(2,1)S(1)}, u32[]{:S(2)}, u32[]{:S(2)}) collective-permute-start(bf16[1024,256]{1,0:T(8,128)(2,1)S(1)} %multiply_convert_fusion.own), channel_id=1, source_target_pairs={{0,32},{16,48},{32,64},{48,80},{64,96},{80,112},{96,0},{112,16},{1... | collective-permute-start | bytes 1572872 | tf_op jit(solution)/shard_map/ppermute | solution.py:532
  10.0 17.9 %collective-permute-start.1 = (bf16[1024,256]{1,0:T(8,128)(2,1)S(1)}, bf16[1024,256]{1,0:T(8,128)(2,1)S(1)}, u32[]{:S(2)}, u32[]{:S(2)}) collective-permute-start(bf16[1024,256]{1,0:T(8,128)(2,1)S(1)} %multiply_convert_fusion.own), channel_id=1, source_target_pairs={{0,96},{16,112},{32,0},{48,16},{64,32},{80,48},{96,64},{112,80},{1... | collective-permute-start | bytes 1572872 | tf_op jit(solution)/shard_map/ppermute | solution.py:532
  14.7 26.4 %copy-start.10 = (bf16[1024,256]{1,0:T(8,128)(2,1)S(1)}, bf16[1024,256]{1,0:T(8,128)(2,1)}, u32[]{:S(2)}) copy-start(bf16[1024,256]{1,0:T(8,128)(2,1)} %param.5) | copy-start | bytes 1572868
  14.7 26.4 %copy-start.14 = (f32[256]{0:T(256)S(1)}, f32[256]{0:T(256)}, u32[]{:S(2)}) copy-start(f32[256]{0:T(256)} %param.6) | copy-start | bytes 3076
  27.9 11.0 %copy-start.11 = (bf16[1024,256]{1,0:T(8,128)(2,1)}, bf16[1024,256]{1,0:T(8,128)(2,1)S(1)}, u32[]{:S(2)}) copy-start(bf16[1024,256]{1,0:T(8,128)(2,1)S(1)} %collective-permute-done.1) | copy-start | bytes 1572868
  29.0 21.0 %all-to-all-start.1 = ((bf16[16,80,256]{2,1,0:T(8,128)(2,1)}), bf16[16,80,256]{2,1,0:T(8,128)(2,1)S(1)}, u32[]{:S(2)}, u32[]{:S(2)}) async-start(bf16[16,80,256]{2,1,0:T(8,128)(2,1)} %broadcast_in_dim.72), calls=%async_computation.1 | async-start | bytes 1310720 | tf_op jit(solution)/shard_map/all_to_all | solution.py:433
  37.0 14.5 %collective-permute-start.2 = (bf16[512,256]{1,0:T(8,128)(2,1)S(1)}, bf16[512,256]{1,0:T(8,128)(2,1)}, u32[]{:S(2)}, u32[]{:S(2)}) collective-permute-start(bf16[512,256]{1,0:T(8,128)(2,1)S(1)} %slice.12), channel_id=1, source_target_pairs={{0,32},{16,48},{32,64},{48,80},{64,96},{80,112},{96,0},{112,16},{1... | collective-permute-start | bytes 786440 | tf_op jit(solution)/shard_map/ppermute | solution.py:532
  39.0 12.6 %collective-permute-start.3 = (bf16[512,256]{1,0:T(8,128)(2,1)}, bf16[512,256]{1,0:T(8,128)(2,1)}, u32[]{:S(2)}, u32[]{:S(2)}) collective-permute-start(bf16[512,256]{1,0:T(8,128)(2,1)} %slice.13), channel_id=1, source_target_pairs={{0,96},{16,112},{32,0},{48,16},{64,32},{80,48},{96,64},{112,80},{1... | collective-permute-start | bytes 786440 | tf_op jit(solution)/shard_map/ppermute | solution.py:532
  50.1 7.5 %copy-start.4 = (bf16[64,256]{1,0:T(8,128)(2,1)}, bf16[64,256]{1,0:T(8,128)(2,1)S(1)}, u32[]{:S(2)}) copy-start(bf16[64,256]{1,0:T(8,128)(2,1)S(1)} %slice.18.seeds) | copy-start | bytes 98308
  51.5 9.2 %all-to-all-start.2 = ((f32[8,24,128]{2,1,0:T(8,128)}), f32[8,24,128]{2,1,0:T(8,128)S(1)}, u32[]{:S(2)}, u32[]{:S(2)}) async-start(f32[8,24,128]{2,1,0:T(8,128)} %get-tuple-element.40), calls=%async_computation.2 | async-start | bytes 196608 | tf_op jit(solution)/shard_map/all_to_all | solution.py:437
  60.7 10.8 %collective-permute-start.4 = (bf16[4,1024,256]{2,1,0:T(8,128)(2,1)}, bf16[4,1024,256]{2,1,0:T(8,128)(2,1)}, u32[]{:S(2)}, u32[]{:S(2)}) collective-permute-start(bf16[4,1024,256]{2,1,0:T(8,128)(2,1)} %pad_maximum_fusion.1), channel_id=1, source_target_pairs={{0,16},{16,0},{32,48},{48,32},{64,80},{80,64},{96,112},{112,96},{1... | collective-permute-start | bytes 6291464 | tf_op jit(solution)/shard_map/ppermute | solution.py:568
  67.3 8.9 %copy-start.8 = (s32[48]{0:T(128)}, s32[48]{0:T(128)S(1)}, u32[]{:S(2)}) copy-start(s32[48]{0:T(128)S(1)} %assign_tasks.1.lists) | copy-start | bytes 580
  68.0 13.9 %all-to-all-start.3 = ((f32[16,24,128]{2,1,0:T(8,128)}), f32[16,24,128]{2,1,0:T(8,128)S(1)}, u32[]{:S(2)}, u32[]{:S(2)}) async-start(f32[16,24,128]{2,1,0:T(8,128)} %relay.2), calls=%async_computation.3 | async-start | bytes 393216 | tf_op jit(solution)/shard_map/all_to_all | solution.py:437
  85.7 10.4 %copy-start.9 = (f32[64,64]{1,0:T(8,128)}, f32[64,64]{1,0:T(8,128)S(1)}, u32[]{:S(2)}) copy-start(f32[64,64]{1,0:T(8,128)S(1)} %get-tuple-element.53.factor) | copy-start | bytes 49156
  118.6 33.5 %copy-start.5 = (f32[1,1024]{1,0:T(1,128)}, f32[1,1024]{1,0:T(1,128)S(1)}, u32[]{:S(2)}) copy-start(f32[1,1024]{1,0:T(1,128)S(1)} %get-tuple-element.51.root) | copy-start | bytes 12292
  118.6 18.9 %all-to-all-start.5 = ((f32[128,1,1152]{2,1,0:T(1,128)}), f32[128,1,1152]{2,1,0:T(1,128)S(1)}, u32[]{:S(2)}, u32[]{:S(2)}) async-start(f32[128,1,1152]{2,1,0:T(1,128)} %get-tuple-element.54), calls=%async_computation.5 | async-start | bytes 1179648 | tf_op jit(solution)/shard_map/all_to_all | solution.py:437
  123.2 59.5 %reduce-scatter.3.cloned.1.call-start = ((), (), s32[]{:S(2)}) async-start(), calls=%async_computation.13 | async-start | bytes 1179648 | tf_op jit(solution)/shard_map/reduce_scatter | solution.py:596
  147.7 35.1 %all-to-all-start.6 = ((bf16[16,64,1024]{2,1,0:T(8,128)(2,1)}), bf16[16,64,1024]{2,1,0:T(8,128)(2,1)}, u32[]{:S(2)}, u32[]{:S(2)}) async-start(bf16[16,64,1024]{2,1,0:T(8,128)(2,1)} %get-tuple-element.55), calls=%async_computation.6 | async-start | bytes 4194304 | tf_op jit(solution)/shard_map/all_to_all | solution.py:437
  186.6 32.5 %all-to-all-start.7 = ((bf16[16,64,1024]{2,1,0:T(8,128)(2,1)}), bf16[16,64,1024]{2,1,0:T(8,128)(2,1)}, u32[]{:S(2)}, u32[]{:S(2)}) async-start(bf16[16,64,1024]{2,1,0:T(8,128)(2,1)} %get-tuple-element.58), calls=%async_computation.8 | async-start | bytes 4194304 | tf_op jit(solution)/shard_map/all_to_all | solution.py:437
  191.0 26.1 %all-gather.7.cloned.1.call-start = ((), (), s32[]{:S(2)}) async-start(), calls=%async_computation.16 | async-start | bytes 1179648 | tf_op jit(solution)/shard_map/all_gather | solution.py:602
  191.8 71.8 %reduce-scatter.5.cloned.1.call-start = ((), (), s32[]{:S(2)}) async-start(), calls=%async_computation.14 | async-start | bytes 1179648 | tf_op jit(solution)/shard_map/reduce_scatter | solution.py:596
  228.2 35.4 %all-to-all-start.8 = ((bf16[16,64,1024]{2,1,0:T(8,128)(2,1)}), bf16[16,64,1024]{2,1,0:T(8,128)(2,1)}, u32[]{:S(2)}, u32[]{:S(2)}) async-start(bf16[16,64,1024]{2,1,0:T(8,128)(2,1)} %get-tuple-element.59), calls=%async_computation.9 | async-start | bytes 4194304 | tf_op jit(solution)/shard_map/all_to_all | solution.py:437
  232.8 30.8 %copy-start.6 = (f32[1,1024]{1,0:T(1,128)S(1)}, f32[1,1024]{1,0:T(1,128)}, u32[]{:S(2)}) copy-start(f32[1,1024]{1,0:T(1,128)} %copy-done.5) | copy-start | bytes 12292
  (7 other events, 14.8 us)
Sparse Core Ops, SparseCore 0:
  9.5 76.2 all-gather.4
  147.8 30.7 reduce-scatter.2
  193.6 23.4 all-gather.6
  228.3 31.8 reduce-scatter.4

commit v10 on v9

--- a/solution.py
+++ b/solution.py
@@ -353,18 +353,21 @@
     held, semaphores = rest[-count - 1 : -1], rest[-1]
     rows = tiles.shape[1]
     live = lists[5 * slots]
+    half = rows // 2
 
     def copies(step, side):
         first, second = lists[step], lists[slots + step]
-        sources = [tiles.at[step]]
+        sources = [tiles.at[step, pl.ds(start, half)] for start in (0, half)]
+        targets = [held[0].at[side, pl.ds(start, half)] for start in (0, half)]
+        targets += [one.at[side] for one in held[1:]]
         if by_slot:
             sources += [from_first.at[step], from_second.at[step]]
             sources += [lines.at[lists[3 * slots + 2 * step + end]] for end in range(2)]
         else:
             sources += [from_first.at[first], from_second.at[second]]
         return [
-            pltpu.make_async_copy(source, held[index].at[side], semaphores.at[index, side])
-            for index, source in enumerate(sources)
+            pltpu.make_async_copy(source, target, semaphores.at[index, side])
+            for index, (source, target) in enumerate(zip(sources, targets))
         ]
 
     @pl.when(live > 0)
@@ -383,7 +386,8 @@
             for copy in copies(step + 1, 1 - side):
                 copy.start()
 
-        for copy in copies(step, side):
+        upper, lower, *others = copies(step, side)
+        for copy in (upper, *others):
             copy.wait()
 
         def vectors(end):
@@ -392,17 +396,20 @@
                 return block
             return (block * held[3 + end][side][:, :rows]).astype(jnp.bfloat16)
 
-        def add(out, slot, block, contract):
-            product = lax.dot_general(
-                block,
-                held[0][side],
-                (((1,), (contract,)), ((), ())),
-                preferred_element_type=jnp.float32,
+        def product(block, tile, contract):
+            return lax.dot_general(
+                block, tile, (((1,), (contract,)), ((), ())), preferred_element_type=jnp.float32
             )
-            out[slot] = (out[slot].astype(jnp.float32) + product).astype(jnp.bfloat16)
-
-        add(to_second, lists[slots + step], vectors(0), 0)
-        add(to_first, lists[step], vectors(1), 1)
+
+        def add(out, slot, value):
+            out[slot] = (out[slot].astype(jnp.float32) + value).astype(jnp.bfloat16)
+
+        left = vectors(0)
+        value = product(left[:, :half], held[0][side, :half, :], 0)
+        lower.wait()
+        value = value + product(left[:, half:], held[0][side, half:, :], 0)
+        add(to_second, lists[slots + step], value)
+        add(to_first, lists[step], product(vectors(1), held[0][side], 1))
         return state
 
     lax.fori_loop(0, live, one, 0)
@@ -421,7 +428,7 @@
         out_specs=[pl.BlockSpec(memory_space=pltpu.VMEM)] * 2,
         out_shape=[bf16(col_devices, vecs, rows), bf16(row_devices, vecs, rows)],
         scratch_shapes=[pltpu.VMEM((2,) + one.shape[1:], one.dtype) for one in held]
-        + [pltpu.SemaphoreType.DMA((len(held), 2))],
+        + [pltpu.SemaphoreType.DMA((len(held) + 1, 2))],
         compiler_params=pltpu.CompilerParams(vmem_limit_bytes=VMEM),
         name="apply_tiles",
     )(lists, *operands)

time: 301 us -> 298 us (0.990)
  Pallas kernels: 64.4 us -> 52.2 us
  waiting for transfers between devices: 106 us -> 110 us
  starting transfers between devices: 39.8 us -> 42.9 us
    pallas_call x2, Pallas kernels: 18.4 us -> 12.9 us  [apply_tiles(): pl.pallas_call(functools.partial(apply_kernel, slots, by_slot), in_specs=...]
    all_to_all x6, waiting for transfers between devices: 70.6 us -> 74.8 us  [exchange(): return lax.all_to_all(copies, axis, 0, 0, tiled=True)]
    pallas_call x1, Pallas kernels: 10.2 us -> 6.88 us  [form_tiles(): pl.pallas_call(functools.partial(form_kernel, min(256, rows), slots), gri...]
    pallas_call x2, Pallas kernels: 11.4 us -> 8.03 us  [start_vectors(): pl.pallas_call(functools.partial(vectors_kernel, slots), grid_spec=pltpu....]
    all_to_all x6, starting transfers between devices: 25 us -> 28.1 us  [exchange(): return lax.all_to_all(copies, axis, 0, 0, tiled=True)]
  transfers between devices with their start and end apart: 16 -> 16, of which waited for: 9 -> 9; matrix products, arithmetic and copies ran while one was open for 5% -> 5% of each run, Pallas kernels for 8% -> 7%
where the time goes in v10:
time: 298 us; the launch traced here: 296 us
  waiting for transfers between devices  110 us (37%)
  blocking collectives  59.4 us (20%)
  Pallas kernels  52.2 us (18%)
  starting transfers between devices  42.9 us (14%)
  between operations  14.1 us (5%)
  other arithmetic  10.3 us (3%)
  local copies, waits for them, and re-layouts  5.49 us (2%)
    all_to_all x6, waiting for transfers between devices, exchange(): return lax.all_to_all(copies, axis, 0, 0, tiled=True)  74.8 us
    all_to_all x3, blocking collectives, exchange(): return lax.all_to_all(copies, axis, 0, 0, tiled=True)  46.2 us
    all_to_all x6, starting transfers between devices, exchange(): return lax.all_to_all(copies, axis, 0, 0, tiled=True)  28.1 us
    all_gather x1, waiting for transfers between devices, shards(): from_second = lax.all_gather(spread, 'row', axis=0)  24.6 us
    all_to_all x1, blocking collectives, spread_to(): return lax.all_to_all(copies, axis, 0, 0, tiled=True)  13.2 us
    pallas_call x2, Pallas kernels, apply_tiles(): pl.pallas_call(functools.partial(apply_kernel, slots, by_slot), in_specs=...  12.9 us
    all_to_all x1, waiting for transfers between devices, spread_to(): return lax.all_to_all(copies, axis, 0, 0, tiled=True)  8.76 us
    all_to_all x1, starting transfers between devices, spread_to(): return lax.all_to_all(copies, axis, 0, 0, tiled=True)  8.05 us
  transfers between devices with their start and end apart: 16, of which 9 were waited for; matrix products, arithmetic and copies ran while one was open for 5% of the time, Pallas kernels for 7%

profile of v10, /device:TPU:0, one launch (start us, length us, event | category | flops | bytes accessed | tf_op | source)
XLA Modules:
  0.0 295.9 jit_solution(8257230434138598232)
XLA Ops:
  14.7 13.2 %all_to_all.55 = bf16[8,80,256]{2,1,0:T(8,128)(2,1)S(1)} all-to-all(bf16[8,80,256]{2,1,0:T(8,128)(2,1)S(1)} %broadcast_in_dim.71), channel_id=1, replica_groups=mesh['row'=8,'col'=16] {'row'}, dimensions={0} | all-to-all | bytes 655360 | tf_op jit(solution)/shard_map/all_to_all | solution.py:440
  29.0 8.0 %all-to-all-start.1 = ((bf16[16,80,256]{2,1,0:T(8,128)(2,1)}), bf16[16,80,256]{2,1,0:T(8,128)(2,1)S(1)}, u32[]{:S(2)}, u32[]{:S(2)}) async-start(bf16[16,80,256]{2,1,0:T(8,128)(2,1)} %broadcast_in_dim.72), calls=%async_computation.1 | async-start | bytes 1310720 | tf_op jit(solution)/shard_map/all_to_all | solution.py:440
  41.2 8.8 %all-to-all-done.1 = bf16[16,80,256]{2,1,0:T(8,128)(2,1)S(1)} async-done(((bf16[16,80,256]{2,1,0:T(8,128)(2,1)}), bf16[16,80,256]{2,1,0:T(8,128)(2,1)S(1)}, u32[]{:S(2)}, u32[]{:S(2)}) %all-to-all-start.1) | async-done | bytes 655392 | tf_op jit(solution)/shard_map/all_to_all | solution.py:440
  61.9 5.3 %assign_tasks.1.lists = s32[48]{0:T(128)S(1)} custom-call(s32[1]{0:T(128)} %bitcast.6.here, f32[16,128]{1,0:T(8,128)S(1)} %slice_convert_fusion.table), custom_call_target="tpu_custom_call" | custom-call | tf_op jit(solution)/shard_map/assign_tasks/pallas_call | solution.py:514
  71.5 4.7 %pad_maximum_fusion.right.block = bf16[8,1024,256]{2,1,0:T(8,128)(2,1)} fusion(bf16[4,1024,256]{2,1,0:T(8,128)(2,1)} %collective-permute-done.4, bf16[4,1024,256]{2,1,0:T(8,128)(2,1)} %pad_maximum_fusion.1), kind=kLoop, calls=%fused_computation.1 | loop fusion | flops 2097152 | bytes 8388608 | tf_op jit(solution)/shard_map/concatenate | solution.py:580
  76.2 5.7 %all-to-all-done.3.grams = f32[16,24,128]{2,1,0:T(8,128)S(1)} async-done(((f32[16,24,128]{2,1,0:T(8,128)}), f32[16,24,128]{2,1,0:T(8,128)S(1)}, u32[]{:S(2)}, u32[]{:S(2)}) %all-to-all-start.3) | async-done | bytes 196640 | tf_op jit(solution)/shard_map/all_to_all | solution.py:444
  85.8 6.9 %form_tiles.1 = (bf16[8,1024,1024]{2,1,0:T(8,128)(2,1)}, f32[128,1,1152]{2,1,0:T(1,128)}) custom-call(s32[48]{0:T(128)} %copy-done.8, bf16[16,1024,256]{2,1,0:T(8,128)(2,1)} %bitcast.22, bf16[8,1024,256]{2,1,0:T(8,128)(2,1)} %pad_maximum_fusion.right.block, f32[1,256]{1,0:T(1,128)} %bitcast.28, f32[24,128]{1,0:T(8,128)} %copy-done.7), custom_call_target="tpu_custom_call" | custom-call | tf_op jit(solution)/shard_map/form_tiles/pallas_call | solution.py:298
  92.7 24.5 %all_to_all.56.parts = f32[128,1,1152]{2,1,0:T(1,128)S(1)} all-to-all(f32[128,1,1152]{2,1,0:T(1,128)} %get-tuple-element.50), channel_id=1, replica_groups=mesh['row'=8,'col'=16] {'row','col'}, dimensions={0} | all-to-all | bytes 1179648 | tf_op jit(solution)/shard_map/all_to_all | solution.py:444
  118.5 4.6 %all-to-all-start.5 = ((f32[128,1,1152]{2,1,0:T(1,128)}), f32[128,1,1152]{2,1,0:T(1,128)S(1)}, u32[]{:S(2)}, u32[]{:S(2)}) async-start(f32[128,1,1152]{2,1,0:T(1,128)} %get-tuple-element.54), calls=%async_computation.5 | async-start | bytes 1179648 | tf_op jit(solution)/shard_map/all_to_all | solution.py:444
  123.2 4.0 %start_vectors.3.from_second = f32[8,64,1024]{2,1,0:T(8,128)} custom-call(s32[48]{0:T(128)} %copy-done.8, bf16[8,1024,256]{2,1,0:T(8,128)(2,1)} %pad_maximum_fusion.right.block, bf16[64,256]{1,0:T(8,128)(2,1)} %copy-done.4, f32[64,64]{1,0:T(8,128)} %copy-done.9), custom_call_target="tpu_custom_call" | custom-call | flops 4000000000 | bytes 10000000 | tf_op jit(solution)/shard_map/start_vectors/pallas_call | solution.py:237
  127.1 4.1 %start_vectors.2.from_first = f32[8,64,1024]{2,1,0:T(8,128)} custom-call(s32[48]{0:T(128)} %copy-done.8, bf16[16,1024,256]{2,1,0:T(8,128)(2,1)} %bitcast.23, bf16[64,256]{1,0:T(8,128)(2,1)} %copy-done.4, f32[64,64]{1,0:T(8,128)} %copy-done.9, f32[1,256]{1,0:T(1,128)} %bitcast.29), custom_call_target="tpu_custom_call" | custom-call | flops 4000000000 | bytes 10000000 | tf_op jit(solution)/shard_map/start_vectors/pallas_call | solution.py:237
  131.2 6.2 %all-to-all-done.5.rest_0_.gram_rows = f32[128,1,1152]{2,1,0:T(1,128)S(1)} async-done(((f32[128,1,1152]{2,1,0:T(1,128)}), f32[128,1,1152]{2,1,0:T(1,128)S(1)}, u32[]{:S(2)}, u32[]{:S(2)}) %all-to-all-start.5) | async-done | bytes 589856 | tf_op jit(solution)/shard_map/all_to_all | solution.py:444
  138.2 6.5 %apply_tiles.2 = (bf16[16,64,1024]{2,1,0:T(8,128)(2,1)}, bf16[8,64,1024]{2,1,0:T(8,128)(2,1)}) custom-call(s32[48]{0:T(128)} %copy-done.8, bf16[8,1024,1024]{2,1,0:T(8,128)(2,1)} %get-tuple-element.52.tiles, f32[8,64,1024]{2,1,0:T(8,128)} %start_vectors.2.from_first, f32[8,64,1024]{2,1,0:T(8,128)} %start_vectors.3.from_second, f32[128,1,1152]{2,1,0:T(1,128)} %copy-done), custom_call_target="tpu_custom_call" | custom-call | tf_op jit(solution)/shard_map/apply_tiles/pallas_call | solution.py:424
  144.8 4.6 %all-to-all-start.6 = ((bf16[16,64,1024]{2,1,0:T(8,128)(2,1)}), bf16[16,64,1024]{2,1,0:T(8,128)(2,1)}, u32[]{:S(2)}, u32[]{:S(2)}) async-start(bf16[16,64,1024]{2,1,0:T(8,128)(2,1)} %get-tuple-element.55), calls=%async_computation.6 | async-start | bytes 4194304 | tf_op jit(solution)/shard_map/all_to_all | solution.py:444
  153.3 26.9 %all-to-all-done.6.first_parts = bf16[16,64,1024]{2,1,0:T(8,128)(2,1)} async-done(((bf16[16,64,1024]{2,1,0:T(8,128)(2,1)}), bf16[16,64,1024]{2,1,0:T(8,128)(2,1)}, u32[]{:S(2)}, u32[]{:S(2)}) %all-to-all-start.6) | async-done | bytes 2097184 | tf_op jit(solution)/shard_map/all_to_all | solution.py:444
  180.2 3.9 %between.1 = (bf16[16,64,1024]{2,1,0:T(8,128)(2,1)}, bf16[64,1024]{1,0:T(8,128)(2,1)}) custom-call(f32[64,1024]{1,0:T(8,128)} %fusion.own_part, bf16[16,64,1024]{2,1,0:T(8,128)(2,1)} %all-to-all-done.6.first_parts, bf16[64,1024]{1,0:T(8,128)(2,1)} %bitcast.27, f32[1,1024]{1,0:T(1,128)} %copy-done.5, f32[64,64]{1,0:T(8,128)} %copy-done.2), custom_call_target="tpu_custom_call" | custom-call | tf_op jit(solution)/shard_map/between/pallas_call | solution.py:203
  184.0 6.6 %all-to-all-start.7 = ((bf16[16,64,1024]{2,1,0:T(8,128)(2,1)}), bf16[16,64,1024]{2,1,0:T(8,128)(2,1)}, u32[]{:S(2)}, u32[]{:S(2)}) async-start(bf16[16,64,1024]{2,1,0:T(8,128)(2,1)} %get-tuple-element.58), calls=%async_computation.8 | async-start | bytes 4194304 | tf_op jit(solution)/shard_map/all_to_all | solution.py:444
  191.4 24.6 %all-gather.7.cloned.1.call-done = bf16[512,1024]{1,0:T(8,128)(2,1)} async-done(((bf16[64,1024]{1,0:T(8,128)(2,1)}), bf16[512,1024]{1,0:T(8,128)(2,1)}) %all-gather.7.cloned.1.call-update) | async-done | bytes 1048592 | tf_op jit(solution)/shard_map/all_gather | solution.py:609
  216.0 4.9 %all-to-all-done.7.from_first = bf16[16,64,1024]{2,1,0:T(8,128)(2,1)} async-done(((bf16[16,64,1024]{2,1,0:T(8,128)(2,1)}), bf16[16,64,1024]{2,1,0:T(8,128)(2,1)}, u32[]{:S(2)}, u32[]{:S(2)}) %all-to-all-start.7) | async-done | bytes 2097184 | tf_op jit(solution)/shard_map/all_to_all | solution.py:444
  220.8 6.4 %apply_tiles.3 = (bf16[16,64,1024]{2,1,0:T(8,128)(2,1)}, bf16[8,64,1024]{2,1,0:T(8,128)(2,1)}) custom-call(s32[48]{0:T(128)} %copy-done.8, bf16[8,1024,1024]{2,1,0:T(8,128)(2,1)} %get-tuple-element.52.tiles, bf16[16,64,1024]{2,1,0:T(8,128)(2,1)} %all-to-all-done.7.from_first, bf16[8,64,1024]{2,1,0:T(8,128)(2,1)} %bitcast.26), custom_call_target="tpu_custom_call" | custom-call | tf_op jit(solution)/shard_map/apply_tiles/pallas_call | solution.py:424
  227.2 5.5 %all-to-all-start.8 = ((bf16[16,64,1024]{2,1,0:T(8,128)(2,1)}), bf16[16,64,1024]{2,1,0:T(8,128)(2,1)}, u32[]{:S(2)}, u32[]{:S(2)}) async-start(bf16[16,64,1024]{2,1,0:T(8,128)(2,1)} %get-tuple-element.59), calls=%async_computation.9 | async-start | bytes 4194304 | tf_op jit(solution)/shard_map/all_to_all | solution.py:444
  233.2 28.1 %all-to-all-done.8.first_parts = bf16[16,64,1024]{2,1,0:T(8,128)(2,1)} async-done(((bf16[16,64,1024]{2,1,0:T(8,128)(2,1)}), bf16[16,64,1024]{2,1,0:T(8,128)(2,1)}, u32[]{:S(2)}, u32[]{:S(2)}) %all-to-all-start.8) | async-done | bytes 2097184 | tf_op jit(solution)/shard_map/all_to_all | solution.py:444
  264.6 9.2 %all_to_all.57.grams = f32[8,24,128]{2,1,0:T(8,128)S(1)} all-to-all(f32[8,24,128]{2,1,0:T(8,128)S(1)} %get-tuple-element.61), channel_id=1, replica_groups=mesh['row'=8,'col'=16] {'row'}, dimensions={0} | all-to-all | bytes 196608 | tf_op jit(solution)/shard_map/all_to_all | solution.py:444
  273.8 12.5 %all_to_all.58.grams = f32[16,24,128]{2,1,0:T(8,128)S(1)} all-to-all(f32[16,24,128]{2,1,0:T(8,128)S(1)} %relay.3), channel_id=1, replica_groups=mesh['row'=8,'col'=16] {'col'}, dimensions={0} | all-to-all | bytes 393216 | tf_op jit(solution)/shard_map/all_to_all | solution.py:444
  (86 shorter events, 46.4 us)
Async XLA Ops:
  6.5 79.3 %all-gather.5.cloned.1.call-start = ((), (), s32[]{:S(2)}) async-start(), calls=%async_computation.15 | async-start | bytes 8912896 | tf_op jit(solution)/shard_map/all_gather | solution.py:533
  8.4 19.5 %collective-permute-start = (bf16[1024,256]{1,0:T(8,128)(2,1)S(1)}, bf16[1024,256]{1,0:T(8,128)(2,1)S(1)}, u32[]{:S(2)}, u32[]{:S(2)}) collective-permute-start(bf16[1024,256]{1,0:T(8,128)(2,1)S(1)} %multiply_convert_fusion.own), channel_id=1, source_target_pairs={{0,32},{16,48},{32,64},{48,80},{64,96},{80,112},{96,0},{112,16},{1... | collective-permute-start | bytes 1572872 | tf_op jit(solution)/shard_map/ppermute | solution.py:539
  10.0 17.9 %collective-permute-start.1 = (bf16[1024,256]{1,0:T(8,128)(2,1)S(1)}, bf16[1024,256]{1,0:T(8,128)(2,1)S(1)}, u32[]{:S(2)}, u32[]{:S(2)}) collective-permute-start(bf16[1024,256]{1,0:T(8,128)(2,1)S(1)} %multiply_convert_fusion.own), channel_id=1, source_target_pairs={{0,96},{16,112},{32,0},{48,16},{64,32},{80,48},{96,64},{112,80},{1... | collective-permute-start | bytes 1572872 | tf_op jit(solution)/shard_map/ppermute | solution.py:539
  14.7 26.4 %copy-start.10 = (bf16[1024,256]{1,0:T(8,128)(2,1)S(1)}, bf16[1024,256]{1,0:T(8,128)(2,1)}, u32[]{:S(2)}) copy-start(bf16[1024,256]{1,0:T(8,128)(2,1)} %param.5) | copy-start | bytes 1572868
  14.7 26.4 %copy-start.14 = (f32[256]{0:T(256)S(1)}, f32[256]{0:T(256)}, u32[]{:S(2)}) copy-start(f32[256]{0:T(256)} %param.6) | copy-start | bytes 3076
  27.9 11.0 %copy-start.11 = (bf16[1024,256]{1,0:T(8,128)(2,1)}, bf16[1024,256]{1,0:T(8,128)(2,1)S(1)}, u32[]{:S(2)}) copy-start(bf16[1024,256]{1,0:T(8,128)(2,1)S(1)} %collective-permute-done.1) | copy-start | bytes 1572868
  29.0 21.0 %all-to-all-start.1 = ((bf16[16,80,256]{2,1,0:T(8,128)(2,1)}), bf16[16,80,256]{2,1,0:T(8,128)(2,1)S(1)}, u32[]{:S(2)}, u32[]{:S(2)}) async-start(bf16[16,80,256]{2,1,0:T(8,128)(2,1)} %broadcast_in_dim.72), calls=%async_computation.1 | async-start | bytes 1310720 | tf_op jit(solution)/shard_map/all_to_all | solution.py:440
  37.0 14.5 %collective-permute-start.2 = (bf16[512,256]{1,0:T(8,128)(2,1)S(1)}, bf16[512,256]{1,0:T(8,128)(2,1)}, u32[]{:S(2)}, u32[]{:S(2)}) collective-permute-start(bf16[512,256]{1,0:T(8,128)(2,1)S(1)} %slice.12), channel_id=1, source_target_pairs={{0,32},{16,48},{32,64},{48,80},{64,96},{80,112},{96,0},{112,16},{1... | collective-permute-start | bytes 786440 | tf_op jit(solution)/shard_map/ppermute | solution.py:539
  39.0 12.6 %collective-permute-start.3 = (bf16[512,256]{1,0:T(8,128)(2,1)}, bf16[512,256]{1,0:T(8,128)(2,1)}, u32[]{:S(2)}, u32[]{:S(2)}) collective-permute-start(bf16[512,256]{1,0:T(8,128)(2,1)} %slice.13), channel_id=1, source_target_pairs={{0,96},{16,112},{32,0},{48,16},{64,32},{80,48},{96,64},{112,80},{1... | collective-permute-start | bytes 786440 | tf_op jit(solution)/shard_map/ppermute | solution.py:539
  50.1 7.5 %copy-start.4 = (bf16[64,256]{1,0:T(8,128)(2,1)}, bf16[64,256]{1,0:T(8,128)(2,1)S(1)}, u32[]{:S(2)}) copy-start(bf16[64,256]{1,0:T(8,128)(2,1)S(1)} %slice.18.seeds) | copy-start | bytes 98308
  51.5 9.2 %all-to-all-start.2 = ((f32[8,24,128]{2,1,0:T(8,128)}), f32[8,24,128]{2,1,0:T(8,128)S(1)}, u32[]{:S(2)}, u32[]{:S(2)}) async-start(f32[8,24,128]{2,1,0:T(8,128)} %get-tuple-element.40), calls=%async_computation.2 | async-start | bytes 196608 | tf_op jit(solution)/shard_map/all_to_all | solution.py:444
  60.7 10.8 %collective-permute-start.4 = (bf16[4,1024,256]{2,1,0:T(8,128)(2,1)}, bf16[4,1024,256]{2,1,0:T(8,128)(2,1)}, u32[]{:S(2)}, u32[]{:S(2)}) collective-permute-start(bf16[4,1024,256]{2,1,0:T(8,128)(2,1)} %pad_maximum_fusion.1), channel_id=1, source_target_pairs={{0,16},{16,0},{32,48},{48,32},{64,80},{80,64},{96,112},{112,96},{1... | collective-permute-start | bytes 6291464 | tf_op jit(solution)/shard_map/ppermute | solution.py:575
  67.3 8.9 %copy-start.8 = (s32[48]{0:T(128)}, s32[48]{0:T(128)S(1)}, u32[]{:S(2)}) copy-start(s32[48]{0:T(128)S(1)} %assign_tasks.1.lists) | copy-start | bytes 580
  68.0 13.9 %all-to-all-start.3 = ((f32[16,24,128]{2,1,0:T(8,128)}), f32[16,24,128]{2,1,0:T(8,128)S(1)}, u32[]{:S(2)}, u32[]{:S(2)}) async-start(f32[16,24,128]{2,1,0:T(8,128)} %relay.2), calls=%async_computation.3 | async-start | bytes 393216 | tf_op jit(solution)/shard_map/all_to_all | solution.py:444
  85.7 7.1 %copy-start.9 = (f32[64,64]{1,0:T(8,128)}, f32[64,64]{1,0:T(8,128)S(1)}, u32[]{:S(2)}) copy-start(f32[64,64]{1,0:T(8,128)S(1)} %get-tuple-element.53.factor) | copy-start | bytes 49156
  118.5 30.9 %copy-start.5 = (f32[1,1024]{1,0:T(1,128)}, f32[1,1024]{1,0:T(1,128)S(1)}, u32[]{:S(2)}) copy-start(f32[1,1024]{1,0:T(1,128)S(1)} %get-tuple-element.51.root) | copy-start | bytes 12292
  118.5 18.9 %all-to-all-start.5 = ((f32[128,1,1152]{2,1,0:T(1,128)}), f32[128,1,1152]{2,1,0:T(1,128)S(1)}, u32[]{:S(2)}, u32[]{:S(2)}) async-start(f32[128,1,1152]{2,1,0:T(1,128)} %get-tuple-element.54), calls=%async_computation.5 | async-start | bytes 1179648 | tf_op jit(solution)/shard_map/all_to_all | solution.py:444
  123.1 57.1 %reduce-scatter.3.cloned.1.call-start = ((), (), s32[]{:S(2)}) async-start(), calls=%async_computation.13 | async-start | bytes 1179648 | tf_op jit(solution)/shard_map/reduce_scatter | solution.py:603
  144.8 35.4 %all-to-all-start.6 = ((bf16[16,64,1024]{2,1,0:T(8,128)(2,1)}), bf16[16,64,1024]{2,1,0:T(8,128)(2,1)}, u32[]{:S(2)}, u32[]{:S(2)}) async-start(bf16[16,64,1024]{2,1,0:T(8,128)(2,1)} %get-tuple-element.55), calls=%async_computation.6 | async-start | bytes 4194304 | tf_op jit(solution)/shard_map/all_to_all | solution.py:444
  184.0 36.8 %all-to-all-start.7 = ((bf16[16,64,1024]{2,1,0:T(8,128)(2,1)}), bf16[16,64,1024]{2,1,0:T(8,128)(2,1)}, u32[]{:S(2)}, u32[]{:S(2)}) async-start(bf16[16,64,1024]{2,1,0:T(8,128)(2,1)} %get-tuple-element.58), calls=%async_computation.8 | async-start | bytes 4194304 | tf_op jit(solution)/shard_map/all_to_all | solution.py:444
  190.6 25.4 %all-gather.7.cloned.1.call-start = ((), (), s32[]{:S(2)}) async-start(), calls=%async_computation.16 | async-start | bytes 1179648 | tf_op jit(solution)/shard_map/all_gather | solution.py:609
  191.3 70.0 %reduce-scatter.5.cloned.1.call-start = ((), (), s32[]{:S(2)}) async-start(), calls=%async_computation.14 | async-start | bytes 1179648 | tf_op jit(solution)/shard_map/reduce_scatter | solution.py:603
  227.2 34.1 %all-to-all-start.8 = ((bf16[16,64,1024]{2,1,0:T(8,128)(2,1)}), bf16[16,64,1024]{2,1,0:T(8,128)(2,1)}, u32[]{:S(2)}, u32[]{:S(2)}) async-start(bf16[16,64,1024]{2,1,0:T(8,128)(2,1)} %get-tuple-element.59), calls=%async_computation.9 | async-start | bytes 4194304 | tf_op jit(solution)/shard_map/all_to_all | solution.py:444
  232.7 28.6 %copy-start.6 = (f32[1,1024]{1,0:T(1,128)S(1)}, f32[1,1024]{1,0:T(1,128)}, u32[]{:S(2)}) copy-start(f32[1,1024]{1,0:T(1,128)} %copy-done.5) | copy-start | bytes 12292
  (7 other events, 15.6 us)
Sparse Core Ops, SparseCore 0:
  9.5 76.2 all-gather.4
  144.9 33.3 reduce-scatter.2
  193.1 22.7 all-gather.6
  227.3 29.8 reduce-scatter.4
